TPU v7x, 32 devices: a whole 2x2x4 slice. The times are simulated.
32 devices in a mesh: lat: 4 (over y, x), lon: 8 (over z, core).
Axes of the slice: x: 2, y: 2, z: 4, core: 2. Of those that a mesh axis runs over, the one named last changes fastest.
Arguments:
- state_field: bfloat16 [8, 720, 512], P('lat', 'lon'), may hold values from -32 to 32
- cotangent: bfloat16 [8, 720, 512], P('lat', 'lon'), may hold values from -6 to 6
- key_bias: bfloat16 [8, 720, 16], P('lat', 'lon'), may hold values from -3 to 250
- input_gain: float32 [512], replicated, may hold values from 0.1 to 1.9
- expand_weight: bfloat16 [512, 2048], replicated, may hold values from -0.25 to 0.25
- depth_weight: bfloat16 [3, 3, 2048], replicated, may hold values from -2 to 2
- shrink_weight: bfloat16 [2048, 512], replicated, may hold values from -0.125 to 0.125
- attention_gain: float32 [512], replicated, may hold values from 0.1 to 1.9
- attention_in: bfloat16 [512, 1536], replicated, may hold values from -0.25 to 0.25
- attention_out: bfloat16 [512, 512], replicated, may hold values from -0.25 to 0.25
Outputs:
- output_field: bfloat16 [8, 720, 512], P('lat', 'lon')
- input_grad: bfloat16 [8, 720, 512], P('lat', 'lon')
- expand_grad: float32 [512, 2048], P('lat', 'lon')
- shrink_grad: float32 [2048, 512], P('lat', 'lon')
- attention_in_grad: float32 [512, 1536], P('lat', 'lon')
- attention_out_grad: float32 [512, 512], P('lat', 'lon')
- depth_grad: float32 [3, 3, 2048], replicated
- input_gain_grad: float32 [512], replicated
- attention_gain_grad: float32 [512], replicated
All inputs are finite; a program needn't handle non-finite values.
Results may differ from a plain program's by a relative error of at most 0.035.
Values may be sent and summed in bfloat16 or wider, within the bound.
No kernel may reach another device: no remote copies, remote signals or barrier semaphores. Data moves between devices by JAX's collectives and lax.ppermute only.
A program may use at most 128 MiB of HBM per device.

v0:
```python
import math

import jax
import jax.numpy as jnp
from jax import lax
from jax.sharding import PartitionSpec as P

EPSILON = 1e-06


def with_halo(block, sides, width, periodic):
    for axis, dim in sides:
        count = lax.axis_size(axis)
        forward = [(i, i + 1) for i in range(count - 1)]
        if periodic:
            forward.append((count - 1, 0))
        backward = [(target, source) for source, target in forward]
        low = lax.ppermute(
            lax.slice_in_dim(block, block.shape[dim] - width, None, axis=dim), axis, forward
        )
        high = lax.ppermute(lax.slice_in_dim(block, 0, width, axis=dim), axis, backward)
        block = jnp.concatenate([low, block, high], axis=dim)
    return block


def inverse_rms(values):
    return lax.rsqrt(jnp.mean(values * values, axis=-1, keepdims=True) + EPSILON)


def silu_slope(values):
    sigmoid = jax.nn.sigmoid(values)
    return sigmoid * (1.0 + values * (1.0 - sigmoid))


def depthwise_sum(padded, weights, row_count, lon_count):
    total = jnp.zeros((row_count, lon_count, padded.shape[2]), jnp.float32)
    for lat_step in range(3):
        for lon_step in range(3):
            total = total + weights[lat_step, lon_step].astype(jnp.float32) * padded[
                lat_step : lat_step + row_count, lon_step : lon_step + lon_count
            ].astype(jnp.float32)
    return total


def transposed_sum(padded, weights, row_count, lon_count):
    total = jnp.zeros((row_count, lon_count, padded.shape[2]), jnp.float32)
    for lat_step in range(3):
        for lon_step in range(3):
            total = total + weights[lat_step, lon_step].astype(jnp.float32) * padded[
                2 - lat_step : 2 - lat_step + row_count, 2 - lon_step : 2 - lon_step + lon_count
            ].astype(jnp.float32)
    return total


def cross_cells(left, right):
    return lax.dot_general(
        left.reshape(-1, left.shape[-1]),
        right.reshape(-1, right.shape[-1]),
        (((0,), (0,)), ((), ())),
        preferred_element_type=jnp.float32,
    )


def times_transpose(values, weights):
    return lax.dot_general(
        values, weights, (((values.ndim - 1,), (1,)), ((), ())), preferred_element_type=jnp.float32
    )


def norm_back(back_normed, state, inverse, gain):
    scaled = back_normed * gain
    return inverse * scaled - inverse * inverse * inverse * state * jnp.mean(
        scaled * state, axis=-1, keepdims=True
    )


def to_items(values, head_count):
    row_count, lon_count, channels = values.shape
    head_width = channels // head_count
    return (
        values.reshape(row_count, lon_count, head_count, head_width)
        .transpose(0, 2, 1, 3)
        .reshape(row_count * head_count, lon_count, head_width)
    )


def from_items(values, row_count):
    item_count, lon_count, head_width = values.shape
    head_count = item_count // row_count
    return (
        values.reshape(row_count, head_count, lon_count, head_width)
        .transpose(0, 2, 1, 3)
        .reshape(row_count, lon_count, head_count * head_width)
    )


def per_device(
    state_field,
    cotangent,
    key_bias,
    input_gain,
    expand_weight,
    depth_weight,
    shrink_weight,
    attention_gain,
    attention_in,
    attention_out,
):
    row_count, lon_count, channels = state_field.shape
    head_count = key_bias.shape[2]
    head_width = channels // head_count
    query_parts = 4
    norm_factor = 1.0 / math.sqrt(
        row_count * lon_count * lax.axis_size("lat") * lax.axis_size("lon")
    )
    score_scale = 1.0 / math.sqrt(head_width)
    state_float = state_field.astype(jnp.float32)
    inverse_first = inverse_rms(state_float)
    normed = (state_float * inverse_first * input_gain).astype(jnp.bfloat16)
    expanded = jnp.dot(normed, expand_weight, preferred_element_type=jnp.float32)
    activated = jax.nn.silu(expanded).astype(jnp.bfloat16)
    padded = with_halo(activated, (("lon", 1),), 1, True)
    padded = with_halo(padded, (("lat", 0),), 1, False)
    convolved = depthwise_sum(padded, depth_weight, row_count, lon_count)
    mixed = jax.nn.silu(convolved).astype(jnp.bfloat16)
    inner_state = (
        state_float + jnp.dot(mixed, shrink_weight, preferred_element_type=jnp.float32)
    ).astype(jnp.bfloat16)
    inner_float = inner_state.astype(jnp.float32)
    inverse_second = inverse_rms(inner_float)
    normed_second = (inner_float * inverse_second * attention_gain).astype(jnp.bfloat16)
    projected = jnp.dot(normed_second, attention_in, preferred_element_type=jnp.float32).astype(
        jnp.bfloat16
    )
    queries = to_items(projected[..., :channels], head_count)
    keys_local = to_items(projected[..., channels : 2 * channels], head_count)
    values_local = to_items(projected[..., 2 * channels :], head_count)
    bias_items = key_bias.transpose(0, 2, 1).reshape(row_count * head_count, lon_count)
    query_rows, key_rows, value_rows, bias_rows = (
        lax.all_to_all(queries, "lon", split_axis=0, concat_axis=1, tiled=True),
        lax.all_to_all(keys_local, "lon", split_axis=0, concat_axis=1, tiled=True),
        lax.all_to_all(values_local, "lon", split_axis=0, concat_axis=1, tiled=True),
        lax.all_to_all(bias_items, "lon", split_axis=0, concat_axis=1, tiled=True),
    )

    def score_block(query_block, key_row, bias_row):
        return (
            jnp.einsum("qd,kd->qk", query_block, key_row, preferred_element_type=jnp.float32)
            * score_scale
            + bias_row.astype(jnp.float32)[None, :]
        )

    def attend(operands):
        query_row, key_row, value_row, bias_row = operands
        full_length = query_row.shape[0]
        query_blocks = query_row.reshape(query_parts, full_length // query_parts, head_width)

        def one_block(query_block):
            scores = score_block(query_block, key_row, bias_row)
            highest = jnp.max(scores, axis=1, keepdims=True)
            exponent = jnp.exp(scores - highest)
            total = jnp.sum(exponent, axis=1, keepdims=True)
            attention_weights = (exponent / total).astype(jnp.bfloat16)
            block_rows = jnp.dot(
                attention_weights, value_row, preferred_element_type=jnp.float32
            ).astype(jnp.bfloat16)
            return (block_rows, highest + jnp.log(total))

        block_rows, block_levels = lax.map(one_block, query_blocks)
        return (block_rows.reshape(full_length, head_width), block_levels.reshape(full_length, 1))

    head_rows, levels = lax.map(attend, (query_rows, key_rows, value_rows, bias_rows))
    head_local = lax.all_to_all(head_rows, "lon", split_axis=1, concat_axis=0, tiled=True)
    heads_field = from_items(head_local, row_count)
    output_field = (
        inner_float + jnp.dot(heads_field, attention_out, preferred_element_type=jnp.float32)
    ).astype(jnp.bfloat16)
    out_grad_local = cross_cells(heads_field, cotangent) * norm_factor
    back_heads = times_transpose(cotangent, attention_out).astype(jnp.bfloat16)
    back_rows = lax.all_to_all(
        to_items(back_heads, head_count), "lon", split_axis=0, concat_axis=1, tiled=True
    )

    def attend_back(operands):
        query_row, key_row, value_row, bias_row, level_row, back_row = operands
        full_length = query_row.shape[0]
        block_length = full_length // query_parts
        query_blocks = query_row.reshape(query_parts, block_length, head_width)
        level_blocks = level_row.reshape(query_parts, block_length, 1)
        back_blocks = back_row.reshape(query_parts, block_length, head_width)

        def one_block(carry, block):
            key_total, value_total = carry
            query_block, level_block, back_block = block
            scores = score_block(query_block, key_row, bias_row)
            probs_float = jnp.exp(scores - level_block)
            probs_low = probs_float.astype(jnp.bfloat16)
            value_total = value_total + lax.dot_general(
                probs_low, back_block, (((0,), (0,)), ((), ())), preferred_element_type=jnp.float32
            )
            back_probs = jnp.einsum(
                "qd,kd->qk", back_block, value_row, preferred_element_type=jnp.float32
            )
            centred = jnp.sum(probs_float * back_probs, axis=1, keepdims=True)
            back_scores = (probs_float * (back_probs - centred)).astype(jnp.bfloat16)
            query_block_grads = (
                jnp.dot(back_scores, key_row, preferred_element_type=jnp.float32) * score_scale
            ).astype(jnp.bfloat16)
            key_total = key_total + lax.dot_general(
                back_scores,
                query_block,
                (((0,), (0,)), ((), ())),
                preferred_element_type=jnp.float32,
            )
            return ((key_total, value_total), query_block_grads)

        start_totals = (
            jnp.zeros((full_length, head_width), jnp.float32),
            jnp.zeros((full_length, head_width), jnp.float32),
        )
        final_totals, query_grad_blocks = lax.scan(
            one_block, start_totals, (query_blocks, level_blocks, back_blocks)
        )
        key_grads = (final_totals[0] * score_scale).astype(jnp.bfloat16)
        value_grads = final_totals[1].astype(jnp.bfloat16)
        return (query_grad_blocks.reshape(full_length, head_width), key_grads, value_grads)

    query_grads, key_grads, value_grads = lax.map(
        attend_back, (query_rows, key_rows, value_rows, bias_rows, levels, back_rows)
    )
    query_grads, key_grads, value_grads = (
        lax.all_to_all(query_grads, "lon", split_axis=1, concat_axis=0, tiled=True),
        lax.all_to_all(key_grads, "lon", split_axis=1, concat_axis=0, tiled=True),
        lax.all_to_all(value_grads, "lon", split_axis=1, concat_axis=0, tiled=True),
    )
    back_projected = jnp.concatenate(
        [
            from_items(query_grads, row_count),
            from_items(key_grads, row_count),
            from_items(value_grads, row_count),
        ],
        axis=-1,
    )
    in_grad_local = cross_cells(normed_second, back_projected) * norm_factor
    back_second = times_transpose(back_projected, attention_in)
    gain_two = jnp.sum(back_second * inner_float * inverse_second, axis=(0, 1)) * norm_factor
    back_inner = (
        cotangent.astype(jnp.float32)
        + norm_back(back_second, inner_float, inverse_second, attention_gain)
    ).astype(jnp.bfloat16)
    attention_part = (in_grad_local, out_grad_local)
    shrink_local = cross_cells(mixed, back_inner) * norm_factor
    back_convolved = (times_transpose(back_inner, shrink_weight) * silu_slope(convolved)).astype(
        jnp.bfloat16
    )
    back_pad = with_halo(back_convolved, (("lon", 1),), 1, True)
    back_pad = with_halo(back_pad, (("lat", 0),), 1, False)
    back_activated = transposed_sum(back_pad, depth_weight, row_count, lon_count)
    back_conv_float = back_convolved.astype(jnp.float32)
    depth_local = (
        jnp.stack(
            [
                jnp.stack(
                    [
                        jnp.sum(
                            padded[
                                lat_step : lat_step + row_count, lon_step : lon_step + lon_count
                            ].astype(jnp.float32)
                            * back_conv_float,
                            axis=(0, 1),
                        )
                        for lon_step in range(3)
                    ]
                )
                for lat_step in range(3)
            ]
        )
        * norm_factor
    )
    back_expanded = (back_activated * silu_slope(expanded)).astype(jnp.bfloat16)
    expand_local = cross_cells(normed, back_expanded) * norm_factor
    back_normed = times_transpose(back_expanded, expand_weight)
    gain_one = jnp.sum(back_normed * state_float * inverse_first, axis=(0, 1)) * norm_factor
    input_grad = (
        back_inner.astype(jnp.float32)
        + norm_back(back_normed, state_float, inverse_first, input_gain)
    ).astype(jnp.bfloat16)
    depth_grad, input_gain_grad, attention_gain_grad = lax.psum(
        (depth_local, gain_one, gain_two), ("lat", "lon")
    )
    results = (
        lax.psum_scatter(
            expand_local.astype(jnp.bfloat16), "lon", scatter_dimension=1, tiled=True
        ).astype(jnp.float32),
        lax.psum_scatter(
            shrink_local.astype(jnp.bfloat16), "lon", scatter_dimension=1, tiled=True
        ).astype(jnp.float32),
        lax.psum_scatter(
            attention_part[0].astype(jnp.bfloat16), "lon", scatter_dimension=1, tiled=True
        ).astype(jnp.float32),
        lax.psum_scatter(
            attention_part[1].astype(jnp.bfloat16), "lon", scatter_dimension=1, tiled=True
        ).astype(jnp.float32),
    )
    results = (
        lax.psum_scatter(
            results[0].astype(jnp.bfloat16), "lat", scatter_dimension=0, tiled=True
        ).astype(jnp.float32),
        lax.psum_scatter(
            results[1].astype(jnp.bfloat16), "lat", scatter_dimension=0, tiled=True
        ).astype(jnp.float32),
        lax.psum_scatter(
            results[2].astype(jnp.bfloat16), "lat", scatter_dimension=0, tiled=True
        ).astype(jnp.float32),
        lax.psum_scatter(
            results[3].astype(jnp.bfloat16), "lat", scatter_dimension=0, tiled=True
        ).astype(jnp.float32),
    )
    return (
        output_field,
        input_grad,
        results[0],
        results[1],
        results[2],
        results[3],
        depth_grad,
        input_gain_grad,
        attention_gain_grad,
    )


def solution(mesh):
    placed = (
        P("lat", "lon", None),
        P("lat", "lon", None),
        P("lat", "lon", None),
        P(),
        P(),
        P(),
        P(),
        P(),
        P(),
        P(),
    )
    return jax.shard_map(
        per_device,
        mesh=mesh,
        in_specs=placed,
        out_specs=(
            P("lat", "lon", None),
            P("lat", "lon", None),
            P("lat", "lon"),
            P("lat", "lon"),
            P("lat", "lon"),
            P("lat", "lon"),
            P(),
            P(),
            P(),
        ),
        check_vma=False,
    )
```

profile of v0, /device:TPU:0, one launch (start us, length us, event | category | flops | bytes accessed | tf_op | source)
XLA Modules:
  0.0 612.8 jit_solution(13954542608638060893)
XLA Ops:
  30.6 7.4 %collective-permute-done.2 = bf16[1,92,2048]{2,1,0:T(8,128)(2,1)S(1)} collective-permute-done((bf16[1,92,2048]{2,1,0:T(8,128)(2,1)S(1)}, bf16[1,92,2048]{2,1,0:T(8,128)(2,1)S(1)}, u32[]{:S(2)}, u32[]{:S(2)}) %collective-permute-start.2) | collective-permute-done | bytes 376864 | tf_op jit(solution)/shard_map/ppermute | solution.py:18
  38.0 10.4 %collective-permute-done.3 = bf16[1,92,2048]{2,1,0:T(8,128)(2,1)S(1)} collective-permute-done((bf16[1,92,2048]{2,1,0:T(8,128)(2,1)S(1)}, bf16[1,92,2048]{2,1,0:T(8,128)(2,1)S(1)}, u32[]{:S(2)}, u32[]{:S(2)}) %collective-permute-start.3) | collective-permute-done | bytes 376864 | tf_op jit(solution)/shard_map/ppermute | solution.py:21
  53.1 4.8 all-to-all-start.5
  61.4 6.2 %all-to-all-done.5 = bf16[32,90,32]{1,2,0:T(8,128)(2,1)S(1)} async-done(((bf16[32,90,32]{1,2,0:T(8,128)(2,1)}), bf16[32,90,32]{1,2,0:T(8,128)(2,1)S(1)}, u32[]{:S(2)}, u32[]{:S(2)}) %all-to-all-start.5) | async-done | bytes 184352 | tf_op jit(solution)/shard_map/all_to_all | solution.py:180
  71.9 8.8 %all-to-all-done.1 = bf16[32,90,32]{1,2,0:T(8,128)(2,1)S(1)} async-done(((bf16[32,90,32]{1,2,0:T(8,128)(2,1)}), bf16[32,90,32]{1,2,0:T(8,128)(2,1)S(1)}, u32[]{:S(2)}, u32[]{:S(2)}) %all-to-all-start.1) | async-done | bytes 184352 | tf_op jit(solution)/shard_map/all_to_all | solution.py:141
  85.0 8.8 %all-to-all-done.3 = bf16[32,90,32]{1,2,0:T(8,128)(2,1)S(1)} async-done(((bf16[32,90,32]{1,2,0:T(8,128)(2,1)}), bf16[32,90,32]{1,2,0:T(8,128)(2,1)S(1)}, u32[]{:S(2)}, u32[]{:S(2)}) %all-to-all-start.3) | async-done | bytes 184352 | tf_op jit(solution)/shard_map/all_to_all | solution.py:142
  109.6 30.3 %while.54 = (s32[]{:T(128)}, bf16[4,720,32]{1,2,0:T(8,128)(2,1)S(1)}, f32[4,720,1]{1,2,0:T(1,128)}, bf16[4,720,32]{1,2,0:T(8,128)(2,1)}, bf16[4,720,32]{2,1,0:T(...) while((s32[]{:T(128)}, ...), condition=%wide.region_7.8_spmd, body=%wide.region_2.7_spmd.sunk | while | flops 17631900 | bytes 2594474 | solution.py:172
  148.5 174.5 %while.56 = (s32[]{:T(128)}, bf16[4,720,32]{1,2,0:T(8,128)(2,1)}, bf16[4,720,32]{1,2,0:T(8,128)(2,1)}, bf16[4,720,32]{1,2,0:T(8,128)(2,1)}, bf16[4,720,32]{1,2,0...) while((s32[]{:T(128)}, bf16[4,720,32]{1,2,0:T(8,128)(2,1)}, ...), condition=%wide.region_12.13_spmd, body=%wide.region_8.12_spmd.sunk | while | flops 42811740 | bytes 6672413 | solution.py:228
  152.1 35.3 %while.58 = (s32[]{:T(128)}, f32[720,32]{0,1:T(8,128)}, f32[720,32]{0,1:T(8,128)}, bf16[4,180,32]{1,2,0:T(8,128)(2,1)}, bf16[4,180,32]{1,0,2:T(4,128)(2,1)S(1)},...) while((s32[]{:T(128)}, f32[720,32]{0,1:T(8,128)}, ...), condition=%wide.region_11.11_spmd.clone, body=%wide.region_9.10_spmd.clone.sunk | while | flops 42742620 | bytes 5528800 | solution.py:221
  195.7 35.3 %while.58 = (s32[]{:T(128)}, f32[720,32]{0,1:T(8,128)}, f32[720,32]{0,1:T(8,128)}, bf16[4,180,32]{1,2,0:T(8,128)(2,1)}, bf16[4,180,32]{1,0,2:T(4,128)(2,1)S(1)},...) while((s32[]{:T(128)}, f32[720,32]{0,1:T(8,128)}, ...), condition=%wide.region_11.11_spmd.clone, body=%wide.region_9.10_spmd.clone.sunk | while | flops 42742620 | bytes 5528800 | solution.py:221
  239.4 35.3 %while.58 = (s32[]{:T(128)}, f32[720,32]{0,1:T(8,128)}, f32[720,32]{0,1:T(8,128)}, bf16[4,180,32]{1,2,0:T(8,128)(2,1)}, bf16[4,180,32]{1,0,2:T(4,128)(2,1)S(1)},...) while((s32[]{:T(128)}, f32[720,32]{0,1:T(8,128)}, ...), condition=%wide.region_11.11_spmd.clone, body=%wide.region_9.10_spmd.clone.sunk | while | flops 42742620 | bytes 5528800 | solution.py:221
  283.0 35.3 %while.58 = (s32[]{:T(128)}, f32[720,32]{0,1:T(8,128)}, f32[720,32]{0,1:T(8,128)}, bf16[4,180,32]{1,2,0:T(8,128)(2,1)}, bf16[4,180,32]{1,0,2:T(4,128)(2,1)S(1)},...) while((s32[]{:T(128)}, f32[720,32]{0,1:T(8,128)}, ...), condition=%wide.region_11.11_spmd.clone, body=%wide.region_9.10_spmd.clone.sunk | while | flops 42742620 | bytes 5528800 | solution.py:221
  326.2 4.8 all-to-all-start.6
  344.9 6.5 %all-to-all-done.7 = bf16[8,2,5760]{2,1,0:T(2,128)(2,1)S(1)} async-done(((bf16[8,2,5760]{2,1,0:T(2,128)(2,1)}), bf16[8,2,5760]{2,1,0:T(2,128)(2,1)S(1)}, u32[]{:S(2)}, u32[]{:S(2)}) %all-to-all-start.7) | async-done | bytes 184352 | tf_op jit(solution)/shard_map/all_to_all | solution.py:233
  379.1 7.6 %fusion.46 = (f32[2048]{0:T(1024)}, f32[2048]{0:T(1024)}, f32[2048]{0:T(1024)}, f32[2048]{0:T(1024)}, f32[2048]{0:T(1024)}, /*index=5*/f32[2048]{0:T(1024)}, f32...) fusion(bf16[3,92,2048]{2,1,0:T(8,128)(2,1)S(1)} %copy-done.8, ...), kind=kOutput, calls=%fused_computation.101 | convolution fusion | flops 393320448 | bytes 9744384 | tf_op jit(solution)/shard_map/dot_general | solution.py:65
  393.4 4.7 collective-permute-start.7
  398.1 7.8 %collective-permute-done.6 = bf16[1,92,2048]{2,1,0:T(8,128)(2,1)S(1)} collective-permute-done((bf16[1,92,2048]{2,1,0:T(8,128)(2,1)S(1)}, bf16[1,92,2048]{2,1,0:T(8,128)(2,1)S(1)}, u32[]{:S(2)}, u32[]{:S(2)}) %collective-permute-start.6) | collective-permute-done | bytes 376864 | tf_op jit(solution)/shard_map/ppermute | solution.py:21
  416.0 24.4 %reduce-scatter.17.cloned.1.call-done = bf16[2048,64]{0,1:T(8,128)(2,1)} async-done(((bf16[2048,512]{0,1:T(8,128)(2,1)}), bf16[2048,64]{0,1:T(8,128)(2,1)}) %reduce-scatter.17.cloned.1.call-update) | async-done | bytes 262160 | tf_op jit(solution)/shard_map/reduce_scatter | solution.py:295
  440.8 36.3 %reduce-scatter.13.cloned.1.call-done = bf16[512,256]{1,0:T(8,128)(2,1)} async-done(((bf16[512,2048]{1,0:T(8,128)(2,1)}), bf16[512,256]{1,0:T(8,128)(2,1)}) %reduce-scatter.13.cloned.1.call-update) | async-done | bytes 262160 | tf_op jit(solution)/shard_map/reduce_scatter | solution.py:292
  483.0 37.8 %all-reduce = (f32[512]{0:T(512)}, f32[512]{0:T(512)}) all-reduce(f32[512]{0:T(512)S(1)} %broadcast_multiply_fusion.1, f32[512]{0:T(512)S(1)} %broadcast_multiply_fusion), channel_id=1, replica_groups=mesh['lat'=4,'lon'=8] {'lat','lon'}, use_global_device_ids=true, to_apply=%region_34.35 | all-reduce | flops 1024 | bytes 8192 | tf_op jit(solution)/shard_map/psum | solution.py:288
  522.3 7.5 %reduce-scatter.25.cloned.1.call-done = bf16[128,192]{1,0:T(8,128)(2,1)} async-done(((bf16[512,192]{1,0:T(8,128)(2,1)}), bf16[128,192]{1,0:T(8,128)(2,1)}) %reduce-scatter.25.cloned.1.call-update) | async-done | bytes 49168
  531.4 25.5 %reduce-scatter.19.cloned.1.call-done = bf16[512,64]{0,1:T(8,128)(2,1)} async-done(((bf16[2048,64]{0,1:T(8,128)(2,1)}), bf16[512,64]{0,1:T(8,128)(2,1)}) %reduce-scatter.19.cloned.1.call-update) | async-done | bytes 65552 | tf_op jit(solution)/shard_map/reduce_scatter | solution.py:309
  558.4 25.4 %reduce-scatter.15.cloned.1.call-done = bf16[128,256]{1,0:T(8,128)(2,1)} async-done(((bf16[512,256]{1,0:T(8,128)(2,1)}), bf16[128,256]{1,0:T(8,128)(2,1)}) %reduce-scatter.15.cloned.1.call-update) | async-done | bytes 65552 | tf_op jit(solution)/shard_map/reduce_scatter | solution.py:306
  585.3 18.5 %all-reduce.3.cloned.1.call-done = f32[3,3,2048]{2,1,0:T(4,128)} async-done(((f32[3,3,2048]{2,1,0:T(4,128)}), f32[3,3,2048]{2,1,0:T(4,128)}) %all-reduce.3.cloned.1.call-update) | async-done | bytes 73744 | tf_op jit(solution)/shard_map/psum | solution.py:288
  (881 shorter events, 358.7 us)
Async XLA Ops:
  12.6 12.3 %collective-permute-start = (bf16[2,1,2048]{2,1,0:T(2,128)(2,1)S(1)}, bf16[2,1,2048]{2,1,0:T(2,128)(2,1)S(1)}, u32[]{:S(2)}, u32[]{:S(2)}) collective-permute-start(bf16[2,1,2048]{2,1,0:T(2,128)(2,1)S(1)} %get-tuple-element.533), channel_id=1, source_target_pairs={{0,1},{1,2},{2,3},{3,4},{4,5},{5,6},{6,7},{7,0},{8,9},{9,10},{10,1... | collective-permute-start | bytes 24584 | tf_op jit(solution)/shard_map/ppermute | solution.py:18
  13.2 11.8 %collective-permute-start.1 = (bf16[2,1,2048]{2,1,0:T(2,128)(2,1)S(1)}, bf16[2,1,2048]{2,1,0:T(2,128)(2,1)S(1)}, u32[]{:S(2)}, u32[]{:S(2)}) collective-permute-start(bf16[2,1,2048]{2,1,0:T(2,128)(2,1)S(1)} %get-tuple-element.534), channel_id=1, source_target_pairs={{1,0},{2,1},{3,2},{4,3},{5,4},{6,5},{7,6},{0,7},{9,8},{10,9},{11,1... | collective-permute-start | bytes 24584 | tf_op jit(solution)/shard_map/ppermute | solution.py:21
  17.3 35.9 %all-to-all-start.2 = ((bf16[8,4,90]{2,1,0:T(4,128)(2,1)}), bf16[8,4,90]{2,1,0:T(4,128)(2,1)}, u32[]{:S(2)}, u32[]{:S(2)}) async-start(bf16[8,4,90]{2,1,0:T(4,128)(2,1)} %bitcast.32), calls=%async_computation.2 | async-start | bytes 16384 | tf_op jit(solution)/shard_map/all_to_all | solution.py:143
  25.2 12.7 %collective-permute-start.2 = (bf16[1,92,2048]{2,1,0:T(8,128)(2,1)S(1)}, bf16[1,92,2048]{2,1,0:T(8,128)(2,1)S(1)}, u32[]{:S(2)}, u32[]{:S(2)}) collective-permute-start(bf16[1,92,2048]{2,1,0:T(8,128)(2,1)S(1)} %get-tuple-element.531), channel_id=1, source_target_pairs={{0,8},{8,16},{16,24},{1,9},{9,17},{17,25},{2,10},{10,18},{18,26},{... | collective-permute-start | bytes 1130504 | tf_op jit(solution)/shard_map/ppermute | solution.py:18
  29.1 19.2 %collective-permute-start.3 = (bf16[1,92,2048]{2,1,0:T(8,128)(2,1)S(1)}, bf16[1,92,2048]{2,1,0:T(8,128)(2,1)S(1)}, u32[]{:S(2)}, u32[]{:S(2)}) collective-permute-start(bf16[1,92,2048]{2,1,0:T(8,128)(2,1)S(1)} %get-tuple-element.532), channel_id=1, source_target_pairs={{8,0},{16,8},{24,16},{9,1},{17,9},{25,17},{10,2},{18,10},{26,18},{... | collective-permute-start | bytes 1130504 | tf_op jit(solution)/shard_map/ppermute | solution.py:21
  53.1 14.5 %all-to-all-start.5 = ((bf16[32,90,32]{1,2,0:T(8,128)(2,1)}), bf16[32,90,32]{1,2,0:T(8,128)(2,1)S(1)}, u32[]{:S(2)}, u32[]{:S(2)}) async-start(bf16[32,90,32]{1,2,0:T(8,128)(2,1)} %bitcast.48), calls=%async_computation.5 | async-start | bytes 524288 | tf_op jit(solution)/shard_map/all_to_all | solution.py:180
  67.6 13.1 %all-to-all-start.1 = ((bf16[32,90,32]{1,2,0:T(8,128)(2,1)}), bf16[32,90,32]{1,2,0:T(8,128)(2,1)S(1)}, u32[]{:S(2)}, u32[]{:S(2)}) async-start(bf16[32,90,32]{1,2,0:T(8,128)(2,1)} %bitcast.28), calls=%async_computation.1 | async-start | bytes 524288 | tf_op jit(solution)/shard_map/all_to_all | solution.py:141
  80.7 13.1 %all-to-all-start.3 = ((bf16[32,90,32]{1,2,0:T(8,128)(2,1)}), bf16[32,90,32]{1,2,0:T(8,128)(2,1)S(1)}, u32[]{:S(2)}, u32[]{:S(2)}) async-start(bf16[32,90,32]{1,2,0:T(8,128)(2,1)} %bitcast.36), calls=%async_computation.3 | async-start | bytes 524288 | tf_op jit(solution)/shard_map/all_to_all | solution.py:142
  93.8 13.8 %all-to-all-start = ((bf16[32,90,32]{1,2,0:T(8,128)(2,1)}), bf16[32,90,32]{1,2,0:T(8,128)(2,1)}, u32[]{:S(2)}, u32[]{:S(2)}) async-start(bf16[32,90,32]{1,2,0:T(8,128)(2,1)} %bitcast.23), calls=%async_computation | async-start | bytes 524288 | tf_op jit(solution)/shard_map/all_to_all | solution.py:140
  142.2 183.9 %all-to-all-start.4 = ((bf16[8,2,5760]{2,1,0:T(2,128)(2,1)}), bf16[8,2,5760]{2,1,0:T(2,128)(2,1)}, u32[]{:S(2)}, u32[]{:S(2)}) async-start(bf16[8,2,5760]{2,1,0:T(2,128)(2,1)} %reshape.215), calls=%async_computation.4 | async-start | bytes 368640 | tf_op jit(solution)/shard_map/all_to_all | solution.py:173
  326.2 13.0 %all-to-all-start.6 = ((bf16[8,2,5760]{2,1,0:T(2,128)(2,1)}), bf16[8,2,5760]{2,1,0:T(2,128)(2,1)}, u32[]{:S(2)}, u32[]{:S(2)}) async-start(bf16[8,2,5760]{2,1,0:T(2,128)(2,1)} %reshape.221), calls=%async_computation.6 | async-start | bytes 368640 | tf_op jit(solution)/shard_map/all_to_all | solution.py:232
  331.0 81.3 %reduce-scatter.23.cloned.1.call-start = ((), (), s32[]{:S(2)}) async-start(), calls=%async_computation.22 | async-start | bytes 589824 | tf_op jit(solution)/shard_map/reduce_scatter | solution.py:301
  339.2 12.2 %all-to-all-start.7 = ((bf16[8,2,5760]{2,1,0:T(2,128)(2,1)}), bf16[8,2,5760]{2,1,0:T(2,128)(2,1)S(1)}, u32[]{:S(2)}, u32[]{:S(2)}) async-start(bf16[8,2,5760]{2,1,0:T(2,128)(2,1)} %reshape.219), calls=%async_computation.7 | async-start | bytes 368640 | tf_op jit(solution)/shard_map/all_to_all | solution.py:233
  351.4 12.1 %all-to-all-start.8 = ((bf16[8,2,5760]{2,1,0:T(2,128)(2,1)}), bf16[8,2,5760]{2,1,0:T(2,128)(2,1)}, u32[]{:S(2)}, u32[]{:S(2)}) async-start(bf16[8,2,5760]{2,1,0:T(2,128)(2,1)} %reshape.217), calls=%async_computation.8 | async-start | bytes 368640 | tf_op jit(solution)/shard_map/all_to_all | solution.py:234
  355.4 58.7 %reduce-scatter.21.cloned.1.call-start = ((), (), s32[]{:S(2)}) async-start(), calls=%async_computation.21 | async-start | bytes 1769472 | tf_op jit(solution)/shard_map/reduce_scatter | solution.py:298
  370.8 69.5 %reduce-scatter.17.cloned.1.call-start = ((), (), s32[]{:S(2)}) async-start(), calls=%async_computation.19 | async-start | bytes 2359296 | tf_op jit(solution)/shard_map/reduce_scatter | solution.py:295
  377.8 99.3 %reduce-scatter.13.cloned.1.call-start = ((), (), s32[]{:S(2)}) async-start(), calls=%async_computation.17 | async-start | bytes 2359296 | tf_op jit(solution)/shard_map/reduce_scatter | solution.py:292
  392.0 13.9 %collective-permute-start.6 = (bf16[1,92,2048]{2,1,0:T(8,128)(2,1)S(1)}, bf16[1,92,2048]{2,1,0:T(8,128)(2,1)S(1)}, u32[]{:S(2)}, u32[]{:S(2)}) collective-permute-start(bf16[1,92,2048]{2,1,0:T(8,128)(2,1)S(1)} %get-tuple-element.527), channel_id=1, source_target_pairs={{8,0},{16,8},{24,16},{9,1},{17,9},{25,17},{10,2},{18,10},{26,18},{... | collective-permute-start | bytes 1130504 | tf_op jit(solution)/shard_map/ppermute | solution.py:21
  393.4 12.8 %collective-permute-start.7 = (bf16[1,92,2048]{2,1,0:T(8,128)(2,1)S(1)}, bf16[1,92,2048]{2,1,0:T(8,128)(2,1)S(1)}, u32[]{:S(2)}, u32[]{:S(2)}) collective-permute-start(bf16[1,92,2048]{2,1,0:T(8,128)(2,1)S(1)} %get-tuple-element.528), channel_id=1, source_target_pairs={{0,8},{8,16},{16,24},{1,9},{9,17},{17,25},{2,10},{10,18},{18,26},{... | collective-permute-start | bytes 1130504 | tf_op jit(solution)/shard_map/ppermute | solution.py:18
  412.2 108.6 %reduce-scatter.27.cloned.1.call-start = ((), (), s32[]{:S(2)}) async-start(), calls=%async_computation.25 | async-start | bytes 163840
  414.1 115.7 %reduce-scatter.25.cloned.1.call-start = ((), (), s32[]{:S(2)}) async-start(), calls=%async_computation.24 | async-start | bytes 327680
  415.9 141.0 %reduce-scatter.19.cloned.1.call-start = ((), (), s32[]{:S(2)}) async-start(), calls=%async_computation.20 | async-start | bytes 327680 | tf_op jit(solution)/shard_map/reduce_scatter | solution.py:309
  440.4 143.5 %reduce-scatter.15.cloned.1.call-start = ((), (), s32[]{:S(2)}) async-start(), calls=%async_computation.18 | async-start | bytes 327680 | tf_op jit(solution)/shard_map/reduce_scatter | solution.py:306
  477.1 126.7 %all-reduce.3.cloned.1.call-start = ((), (), s32[]{:S(2)}) async-start(), calls=%async_computation.23 | async-start | bytes 196608 | tf_op jit(solution)/shard_map/psum | solution.py:288
  (167 other events, 1323.5 us)
Sparse Core Ops, SparseCore 0:
  334.8 31.7 reduce-scatter.22
  370.9 32.7 reduce-scatter.20
  406.1 34.1 reduce-scatter.16
  442.6 34.4 reduce-scatter.12
  480.5 22.4 reduce-scatter.26
  505.5 24.2 reduce-scatter.24
  532.8 24.1 reduce-scatter.18
  559.7 24.0 reduce-scatter.14
Sparse Core Ops, SparseCore 1:
  484.7 119.0 all-reduce.2
where the time goes:
time: 618 us; the launch traced here: 613 us
  waiting for transfers between devices  204 us (33%)
  matrix products  165 us (27%)
  local copies, waits for them, and re-layouts  98.3 us (16%)
  starting transfers between devices  55.9 us (9%)
  blocking collectives  37.8 us (6%)
  other arithmetic  32.7 us (5%)
  between operations  16.8 us (3%)
    psum x1, blocking collectives, per_device(): lax.psum((depth_local, gain_one, gain_two), ('lat', 'lon'))  37.8 us
    reduce_scatter x1, waiting for transfers between devices, per_device(): lax.psum_scatter(expand_local.astype(jnp.bfloat16), 'lon', scatter_dimens...  36.3 us
    dot_general x16, matrix products, one_block(): lax.dot_general(back_scores, query_block, (((0,), (0,)), ((), ())), prefe...  28.6 us
    dot_general x16, matrix products, one_block(): jnp.dot(back_scores, key_row, preferred_element_type=jnp.float32)  28.4 us
    dot_general x16, matrix products, one_block(): lax.dot_general(probs_low, back_block, (((0,), (0,)), ((), ())), preferre...  28 us
    dot_general x32, matrix products, score_block(): jnp.einsum('qd,kd->qk', query_block, key_row, preferred_element_type=jnp....  27 us
    reduce_scatter x1, waiting for transfers between devices, per_device(): lax.psum_scatter(results[1].astype(jnp.bfloat16), 'lat', scatter_dimensio...  25.5 us
    reduce_scatter x1, waiting for transfers between devices, per_device(): lax.psum_scatter(results[0].astype(jnp.bfloat16), 'lat', scatter_dimensio...  25.4 us
  transfers between devices with their start and end apart: 26, of which 18 were waited for; matrix products, arithmetic and copies ran while one was open for 40% of the time, Pallas kernels for 0%

commit v1 on v0

v1 whole, which is shorter than its diff:
```python
import functools
import math

import jax
import jax.numpy as jnp
from jax import lax
from jax.experimental import pallas as pl
from jax.experimental.pallas import tpu as pltpu
from jax.sharding import Mesh
from jax.sharding import PartitionSpec as P

EPSILON = 1e-06
LON = ("z", "core")
BF16 = jnp.bfloat16
F32 = jnp.float32
MASKED = -1e30
SIDE = 3
LOG2E = math.log2(math.e)


def inverse_rms(values):
    return lax.rsqrt(jnp.mean(values * values, axis=-1, keepdims=True) + EPSILON)


def silu_slope(values):
    sigmoid = jax.nn.sigmoid(values)
    return sigmoid * (1.0 + values * (1.0 - sigmoid))


def norm_back(back_normed, state, inverse, gain):
    scaled = back_normed * gain
    return inverse * scaled - inverse * inverse * inverse * state * jnp.mean(
        scaled * state, axis=-1, keepdims=True
    )


def shifts(count, step, periodic):
    return [(i, (i + step) % count) for i in range(count) if periodic or 0 <= i + step < count]


def from_sides(block, width, dim, axis, periodic):
    count = lax.axis_size(axis)
    size = block.shape[dim]
    low = lax.ppermute(
        lax.slice_in_dim(block, size - width, size, axis=dim), axis, shifts(count, 1, periodic)
    )
    high = lax.ppermute(
        lax.slice_in_dim(block, 0, width, axis=dim), axis, shifts(count, -1, periodic)
    )
    return low, high


def core_swap(values):
    return lax.ppermute(values, "core", [(0, 1), (1, 0)])


def exchange(values, axis):
    return lax.all_to_all(values, axis, 0, 0, tiled=True)


def own_columns(values, blocks):
    cells = values.shape[0]
    view = values.reshape(cells, blocks, 2, -1)
    first = view[:, :, 0].reshape(cells, -1)
    second = view[:, :, 1].reshape(cells, -1)
    is_first = lax.axis_index("core") == 0
    return jnp.where(is_first, first, second), jnp.where(is_first, second, first)


def both_cores_columns(values, blocks):
    mine, other = own_columns(values, blocks)
    return jnp.concatenate([mine, core_swap(other)], axis=0)


def both_cores(values):
    return jnp.concatenate([values, core_swap(values)], axis=0)


def matmul(left, right):
    return jnp.dot(left, right, preferred_element_type=F32)


def cross_cells(left, right):
    return lax.dot_general(left, right, (((0,), (0,)), ((), ())), preferred_element_type=F32)


def times_transpose(values, weights):
    return lax.dot_general(
        values, weights, (((values.ndim - 1,), (1,)), ((), ())), preferred_element_type=F32
    )


def attention_kernel(
    head_width, query_block, qkv_ref, back_ref, bias_ref, out_ref, heads_t, query_grad_t, key_t,
    value_t, key_grad, value_grad,
):
    head = pl.program_id(0)
    cells, width = back_ref.shape
    scale = 1.0 / math.sqrt(head_width)
    keys = qkv_ref[:, width : 2 * width]
    values = qkv_ref[:, 2 * width : 3 * width]

    @pl.when(head == 0)
    def _():
        key_t[...] = keys.T
        value_t[...] = values.T
        key_grad[...] = jnp.zeros_like(key_grad)
        value_grad[...] = jnp.zeros_like(value_grad)

    lanes = lax.broadcasted_iota(jnp.int32, (1, width), 1) // head_width == head
    zero = jnp.zeros((), BF16)
    head_keys = jnp.where(lanes, keys, zero)
    head_values = jnp.where(lanes, values, zero)
    heads = lax.broadcasted_iota(jnp.int32, bias_ref.shape, 1)
    bias = LOG2E * jnp.sum(
        jnp.where(heads == head, bias_ref[...].astype(F32), 0.0), axis=1, keepdims=True
    )
    rows = pl.ds(pl.multiple_of(head * head_width, head_width), head_width)
    head_key_t = key_t[rows, :]
    head_value_t = value_t[rows, :]
    last_dims = (((1,), (1,)), ((), ()))

    def block(start):
        cols = pl.ds(start, query_block)
        queries = qkv_ref[cols, 0:width]
        backs = back_ref[cols, :]
        scores = lax.dot_general(head_keys, queries, last_dims, preferred_element_type=F32)
        scores = scores * (scale * LOG2E) + bias
        exponent = jnp.exp2(scores - jnp.max(scores, axis=0, keepdims=True))
        probs = exponent * (1.0 / jnp.sum(exponent, axis=0, keepdims=True))
        probs_low = probs.astype(BF16)
        heads_t[rows, cols] = matmul(head_value_t, probs_low)
        back_probs = lax.dot_general(head_values, backs, last_dims, preferred_element_type=F32)
        centred = jnp.sum(probs * back_probs, axis=0, keepdims=True)
        back_scores = (probs * (back_probs - centred)).astype(BF16)
        query_grad_t[rows, cols] = matmul(head_key_t, back_scores)
        value_grad[...] += matmul(probs_low, jnp.where(lanes, backs, zero))
        key_grad[...] += matmul(back_scores, jnp.where(lanes, queries, zero))

    block_count = cells // query_block
    if block_count <= 4:
        for index in range(block_count):
            block(index * query_block)
    else:

        def step(index, carry):
            block(pl.multiple_of(index * query_block, query_block))
            return carry

        lax.fori_loop(0, block_count, step, 0)

    @pl.when(head == pl.num_programs(0) - 1)
    def _():
        out_ref[:, 0:width] = heads_t[...].T.astype(BF16)
        out_ref[:, width : 2 * width] = (query_grad_t[...] * scale).T.astype(BF16)
        out_ref[:, 2 * width : 3 * width] = (key_grad[...] * scale).astype(BF16)
        out_ref[:, 3 * width : 4 * width] = value_grad[...].astype(BF16)


def attention(qkv, backs, bias, head_width):
    cells, width = backs.shape
    items = bias.shape[1]
    query_block = 256 if cells % 256 == 0 else 128
    whole = lambda shape: pl.BlockSpec(shape, lambda head: (0, 0))
    return pl.pallas_call(
        functools.partial(attention_kernel, head_width, query_block),
        grid=(items,),
        out_shape=jax.ShapeDtypeStruct((cells, 4 * width), BF16),
        in_specs=[whole(qkv.shape), whole(backs.shape), whole(bias.shape)],
        out_specs=whole((cells, 4 * width)),
        scratch_shapes=[
            pltpu.VMEM((width, cells), F32),
            pltpu.VMEM((width, cells), F32),
            pltpu.VMEM((width, cells), BF16),
            pltpu.VMEM((width, cells), BF16),
            pltpu.VMEM((cells, width), F32),
            pltpu.VMEM((cells, width), F32),
        ],
        compiler_params=pltpu.CompilerParams(
            vmem_limit_bytes=48 * 1024 * 1024, dimension_semantics=("arbitrary",)
        ),
        cost_estimate=pl.CostEstimate(
            flops=items * cells * cells * 32 * 14,
            bytes_accessed=cells * width * 16,
            transcendentals=items * cells * cells,
        ),
        name="attention",
    )(qkv, backs, bias)


def per_device(
    state_field,
    cotangent,
    key_bias,
    input_gain,
    expand_weight,
    depth_weight,
    shrink_weight,
    attention_gain,
    attention_in,
    attention_out,
):
    row_count, lon_count, channels = state_field.shape
    head_count = key_bias.shape[2]
    head_width = channels // head_count
    wide = expand_weight.shape[1]
    lat_size, z_size = lax.axis_size("lat"), lax.axis_size("z")
    lon_size = 2 * z_size
    norm_factor = 1.0 / math.sqrt(row_count * lon_count * lat_size * lon_size)
    items = row_count * head_count // lon_size
    groups = head_count // items
    width = items * head_width
    frame = lon_count + 2 * SIDE
    own = row_count * frame
    frame_pad = ((0, 0), (SIDE, SIDE), (0, 0))

    cot = jnp.pad(cotangent, frame_pad)
    back_heads = times_transpose(cot, attention_out).astype(BF16)
    bias = jnp.pad(key_bias, frame_pad, constant_values=MASKED)
    early = jnp.concatenate(
        [
            back_heads.reshape(row_count, frame, groups, width),
            bias.reshape(row_count, frame, groups, items),
        ],
        axis=-1,
    ).transpose(0, 2, 1, 3)
    early = exchange(early.reshape(lon_size, frame, width + items), LON)
    early = early.reshape(lon_size * frame, width + items)
    back_rows, bias_rows = early[:, :width], early[:, width:]

    low, high = from_sides(state_field, SIDE, 1, LON, True)
    state = jnp.concatenate([low, state_field, high], axis=1)
    below, above = from_sides(state, 2, 0, "lat", False)
    state = jnp.concatenate([below, state, above], axis=0).astype(F32)
    columns = lax.broadcasted_iota(jnp.int32, (1, frame, 1), 1)
    inside = (columns >= SIDE) & (columns < SIDE + lon_count)

    inverse_first = inverse_rms(state)
    normed = (state * inverse_first * input_gain).astype(BF16)
    expanded = matmul(normed, expand_weight)
    activated = jax.nn.silu(expanded).astype(BF16)
    kernel = depth_weight.astype(F32)

    def shifted(values, step):
        return jnp.roll(values, step, axis=1)

    around = [shifted(activated, 1), activated, shifted(activated, -1)]

    def convolve(first, count):
        total = jnp.zeros((count, frame, wide), F32)
        for a in range(3):
            for b in range(3):
                total = total + kernel[a, b] * around[b][first + a : first + a + count].astype(F32)
        return total

    convolved = convolve(0, row_count + 2)
    own_convolved = convolved[1 : 1 + row_count]
    mixed = jax.nn.silu(own_convolved).astype(BF16)
    own_state = state[2 : 2 + row_count]
    inner_state = (own_state + matmul(mixed, shrink_weight)).astype(BF16)
    inner = inner_state.astype(F32)
    inverse_second = inverse_rms(inner)
    normed_second = (inner * inverse_second * attention_gain).astype(BF16)
    grouped_in = (
        attention_in.reshape(channels, 3, groups, width)
        .transpose(0, 2, 1, 3)
        .reshape(channels, 3 * channels)
    )
    projected = matmul(normed_second, grouped_in).astype(BF16)
    qkv = (
        projected.reshape(row_count, frame, groups, 3 * width)
        .transpose(0, 2, 1, 3)
        .reshape(lon_size, frame, 3 * width)
    )
    qkv = exchange(qkv, LON).reshape(lon_size * frame, 3 * width)

    attended = attention(qkv, back_rows, bias_rows, head_width)
    attended = exchange(attended.reshape(lon_size, frame, 4 * width), LON)
    attended = (
        attended.reshape(row_count, groups, frame, 4, width)
        .transpose(3, 0, 2, 1, 4)
        .reshape(4, row_count, frame, channels)
    )
    heads_field = attended[0]
    back_projected = jnp.concatenate([attended[1], attended[2], attended[3]], axis=-1)
    output_field = (inner + matmul(heads_field, attention_out)).astype(BF16)
    output_field = output_field[:, SIDE : SIDE + lon_count]

    back_second = times_transpose(back_projected, attention_in)
    gain_two = jnp.sum(back_second * inner * inverse_second, axis=(0, 1)) * norm_factor
    back_inner = (
        cot.astype(F32) + norm_back(back_second, inner, inverse_second, attention_gain)
    ).astype(BF16)

    def cells(values):
        return values.reshape(own, values.shape[-1])

    def by_lat(left, right):
        return lax.dot_general(
            left,
            right.reshape(right.shape[0], lat_size, -1),
            (((0,), (0,)), ((), ())),
            preferred_element_type=F32,
        ).transpose(1, 0, 2)

    def scatter(parts):
        parts = jnp.sum(exchange(parts.astype(BF16), "lat").reshape(parts.shape).astype(F32), axis=0)
        parts = parts.reshape((z_size, -1) + parts.shape[1:])
        return jnp.sum(exchange(parts.astype(BF16), "z").astype(F32), axis=0)

    in_part = by_lat(
        both_cores_columns(cells(back_projected), z_size), both_cores(cells(normed_second))
    )
    out_part = by_lat(both_cores_columns(cells(cot), z_size), both_cores(cells(heads_field)))
    block = channels // lat_size
    part = jnp.concatenate(
        [
            in_part.reshape(lat_size, z_size, -1, block),
            out_part.reshape(lat_size, z_size, -1, block),
        ],
        axis=2,
    ).reshape(lat_size, -1, block)
    attention_grads = scatter(part * norm_factor)
    split = 3 * channels // lon_size
    attention_in_grad = attention_grads[:split].T
    attention_out_grad = attention_grads[split:].T

    shrink_part = by_lat(both_cores_columns(cells(back_inner), z_size), both_cores(cells(mixed)))
    shrink_grad = scatter(shrink_part * norm_factor).T

    low, high = from_sides(back_inner[:, SIDE : SIDE + lon_count], 1, 1, LON, True)
    back_sides = jnp.concatenate(
        [
            jnp.zeros((row_count, SIDE - 1, channels), BF16),
            low,
            back_inner[:, SIDE : SIDE + lon_count],
            high,
            jnp.zeros((row_count, SIDE - 1, channels), BF16),
        ],
        axis=1,
    )
    below, above = from_sides(back_sides, 1, 0, "lat", False)
    back_all = jnp.concatenate([below, back_sides, above], axis=0)
    back_convolved = (times_transpose(back_all, shrink_weight) * silu_slope(convolved)).astype(BF16)
    back_around = [shifted(back_convolved, -1), back_convolved, shifted(back_convolved, 1)]
    back_activated = jnp.zeros((row_count, frame, wide), F32)
    for a in range(3):
        for b in range(3):
            back_activated = back_activated + kernel[a, b] * back_around[b][
                2 - a : 2 - a + row_count
            ].astype(F32)
    own_back = jnp.where(inside, back_convolved[1 : 1 + row_count].astype(F32), 0.0)
    depth_part = jnp.stack(
        [
            jnp.sum(around[b][1 + a : 1 + a + row_count].astype(F32) * own_back, axis=(0, 1))
            for a in range(3)
            for b in range(3)
        ]
    )
    own_expanded = expanded[2 : 2 + row_count]
    back_expanded = jnp.where(inside, back_activated * silu_slope(own_expanded), 0.0).astype(BF16)
    own_normed = normed[2 : 2 + row_count]
    back_normed = times_transpose(back_expanded, expand_weight)
    own_inverse = inverse_first[2 : 2 + row_count]
    gain_one = jnp.sum(back_normed * own_state * own_inverse, axis=(0, 1)) * norm_factor
    input_grad = (
        back_inner.astype(F32) + norm_back(back_normed, own_state, own_inverse, input_gain)
    ).astype(BF16)

    expand_part = (
        cross_cells(
            both_cores(cells(own_normed)), both_cores_columns(cells(back_expanded), z_size)
        )
        * norm_factor
    )
    half = wide // 2
    expand_part = expand_part.reshape(lat_size, block, half)
    small = jnp.concatenate([(depth_part * norm_factor).reshape(-1), gain_one, gain_two])
    small = (small + core_swap(small)).reshape(-1, half)
    both = jnp.concatenate(
        [expand_part, jnp.broadcast_to(small, (lat_size,) + small.shape)], axis=1
    ).astype(BF16)
    both = jnp.sum(exchange(both, "lat").astype(F32), axis=0)
    expand_part = both[:block].reshape(block, z_size, -1).transpose(1, 0, 2)
    small = both[block:].reshape(-1, half // z_size)
    both = jnp.concatenate(
        [expand_part, jnp.broadcast_to(small, (z_size,) + small.shape)], axis=1
    ).astype(BF16)
    both = jnp.sum(exchange(both, "z").astype(F32), axis=0)
    expand_grad = both[:block]
    small = both[block:].reshape(-1)
    depth_grad = small[: 9 * wide].reshape(3, 3, wide)
    input_gain_grad = small[9 * wide : 9 * wide + channels]
    attention_gain_grad = small[9 * wide + channels :]
    return (
        output_field,
        input_grad[:, SIDE : SIDE + lon_count],
        expand_grad,
        shrink_grad,
        attention_in_grad,
        attention_out_grad,
        depth_grad,
        input_gain_grad,
        attention_gain_grad,
    )


def solution(mesh):
    lat_size, lon_size = mesh.devices.shape
    split = Mesh(mesh.devices.reshape(lat_size, lon_size // 2, 2), ("lat", "z", "core"))
    grid = P("lat", LON, None)
    weight = P("lat", LON)

    def step(*arrays):
        outputs = jax.shard_map(
            per_device,
            mesh=split,
            in_specs=(grid, grid, grid) + (P(),) * 7,
            out_specs=(grid, grid, weight, weight, weight, weight, P(), P(), P()),
            check_vma=False,
        )(*arrays)
        return outputs

    return step
```

time: 618 us -> 265 us (0.43)
  waiting for transfers between devices: 204 us -> 51 us
  matrix products: 165 us -> 26.4 us
  blocking collectives: 37.8 us -> 0 us
  local copies, waits for them, and re-layouts: 98.3 us -> 68.5 us
  Pallas kernels: 0 us -> 18.6 us
  between operations: 16.8 us -> 1.73 us
    dot_general x120 -> x8, matrix products: 150 us -> 14.4 us  [the longest x4 6.45 us: matmul(): return jnp.dot(left, right, preferred_element_type=F32)]
    reduce_scatter x6 -> x0, waiting for transfers between devices: 112 us -> none  [the longest x1 36.3 us: per_device(): lax.psum_scatter(expand_local.astype(jnp.bfloat16), 'lon', scatter_dimens...]
    psum x1 -> x0, blocking collectives: 37.8 us -> none  [per_device(): lax.psum((depth_local, gain_one, gain_two), ('lat', 'lon'))]
    ppermute x8 -> x17, waiting for transfers between devices: 27.3 us -> 0.19 us  [the longest x4 0.15 us: from_sides(): lax.ppermute(lax.slice_in_dim(block, size - width, size, axis=dim), axis,...]
    pallas_call x0 -> x1, Pallas kernels: none -> 18.6 us  [attention(): pl.pallas_call(functools.partial(attention_kernel, head_width, query_bloc...]
    psum x1 -> x0, waiting for transfers between devices: 18.5 us -> none  [per_device(): lax.psum((depth_local, gain_one, gain_two), ('lat', 'lon'))]
    dynamic_slice x116 -> x0, local copies, waits for them, and re-layouts: 18 us -> none  [the longest x80 8.26 us: attend(): block_rows, block_levels = lax.map(one_block, query_blocks)]
    while x206 -> x0, local copies, waits for them, and re-layouts: 17.6 us -> none
  transfers between devices with their start and end apart: 26 -> 26, of which waited for: 18 -> 8; matrix products, arithmetic and copies ran while one was open for 40% -> 47% of each run, Pallas kernels for 0% -> 0%
where the time goes in v1:
time: 265 us; the launch traced here: 263 us
  local copies, waits for them, and re-layouts  68.5 us (26%)
  starting transfers between devices  60.3 us (23%)
  waiting for transfers between devices  51 us (19%)
  other arithmetic  36.8 us (14%)
  matrix products  26.4 us (10%)
  Pallas kernels  18.6 us (7%)
    all_to_all x9, waiting for transfers between devices, exchange(): return lax.all_to_all(values, axis, 0, 0, tiled=True)  50.8 us
    all_to_all x9, starting transfers between devices, exchange(): return lax.all_to_all(values, axis, 0, 0, tiled=True)  40.3 us
    pallas_call x1, Pallas kernels, attention(): pl.pallas_call(functools.partial(attention_kernel, head_width, query_bloc...  18.6 us
    unnamed x120, local copies, waits for them, and re-layouts  14.5 us
    dot_general x4, matrix products, times_transpose(): lax.dot_general(values, weights, (((values.ndim - 1,), (1,)), ((), ())),...  11.9 us
    concatenate x7, local copies, waits for them, and re-layouts, both_cores(): return jnp.concatenate([values, core_swap(values)], axis=0)  9.85 us
    ppermute x4, starting transfers between devices, from_sides(): lax.ppermute(lax.slice_in_dim(block, size - width, size, axis=dim), axis,...  9.63 us
    ppermute x4, starting transfers between devices, from_sides(): lax.ppermute(lax.slice_in_dim(block, 0, width, axis=dim), axis, shifts(co...  8.04 us
  transfers between devices with their start and end apart: 26, of which 8 were waited for; matrix products, arithmetic and copies ran while one was open for 47% of the time, Pallas kernels for 0%

profile of v1, /device:TPU:0, one launch (start us, length us, event | category | flops | bytes accessed | tf_op | source)
XLA Modules:
  0.0 263.4 jit_solution(787723882095781414)
XLA Ops:
  2.3 4.1 %collective-permute-start.1 = (bf16[2,3,512]{2,1,0:T(4,128)(2,1)S(1)}, bf16[2,3,512]{2,1,0:T(4,128)(2,1)S(1)}, u32[]{:S(2)}, u32[]{:S(2)}) collective-permute-start(bf16[2,3,512]{2,1,0:T(4,128)(2,1)S(1)} %get-tuple-element.135), channel_id=1, source_target_pairs={{0,7},{1,0},{2,1},{3,2},{4,3},{5,4},{6,5},{7,6},{8,15},{9,8},{10,9... | collective-permute-start | bytes 18440 | tf_op jit(solution)/shard_map/ppermute | solution.py:47
  11.1 3.5 %all-to-all-start.1 = ((bf16[8,96,132]{1,2,0:T(8,128)(2,1)}), bf16[8,96,132]{1,2,0:T(8,128)(2,1)S(1)}, u32[]{:S(2)}, u32[]{:S(2)}) async-start(bf16[8,96,132]{1,2,0:T(8,128)(2,1)} %bitcast.170), calls=%async_computation.1 | async-start | bytes 557056 | tf_op jit(solution)/shard_map/all_to_all | solution.py:58
  16.0 4.6 %collective-permute-start.2 = (bf16[2,96,512]{2,1,0:T(8,128)(2,1)S(1)}, bf16[2,96,512]{2,1,0:T(8,128)(2,1)S(1)}, u32[]{:S(2)}, u32[]{:S(2)}) collective-permute-start(bf16[2,96,512]{2,1,0:T(8,128)(2,1)S(1)} %pad_maximum_fusion.7), channel_id=1, source_target_pairs={{0,8},{8,16},{16,24},{1,9},{9,17},{17,25},{2,10},{10,18},{18,26},{... | collective-permute-start | bytes 589832 | tf_op jit(solution)/shard_map/ppermute | solution.py:44
  25.6 3.9 %multiply_convert_fusion = (bf16[6,96,2048]{2,1,0:T(8,128)(2,1)S(1)}, f32[6,96,2048]{2,1,0:T(8,128)}) fusion(bf16[6,96,512]{2,1,0:T(8,128)(2,1)S(1)} %multiply_convert_fusion.5, bf16[512,2048]{1,0:T(8,128)(2,1)S(1)} %copy-done), kind=kOutput, calls=%fused_computation.10 | convolution fusion | flops 1213857792 | bytes 9764864 | tf_op jit(solution)/shard_map/dot_general | solution.py:80
  31.1 4.2 %multiply_add_fusion = f32[4,96,2048]{2,1,0:T(8,128)S(1)} fusion(bf16[6,1,2048]{2,1,0:T(2,128)(2,1)S(1)} %get-tuple-element.101, bf16[6,1,2048]{2,1,0:T(2,128)(2,1)S(1)} %get-tuple-element.100, bf16[6,96,2048]{2,1,0:T(8,128)(2,1)S(1)} %get-tuple-element.147, bf16[6,95,2048]{2,1,0:T(8,128)(2,1)S(1)} %get-tuple-element.99, ...), kind=kLoop, calls=%fused_computation.12 | loop fusion | flops 34603008 | bytes 12656640 | tf_op jit(solution)/shard_map/add | solution.py:253
  41.1 5.0 %all-to-all-start = ((bf16[8,96,384]{2,1,0:T(8,128)(2,1)}), bf16[8,96,384]{2,1,0:T(8,128)(2,1)S(1)}, u32[]{:S(2)}, u32[]{:S(2)}) async-start(bf16[8,96,384]{2,1,0:T(8,128)(2,1)} %bitcast.162), calls=%async_computation | async-start | bytes 1179648 | tf_op jit(solution)/shard_map/all_to_all | solution.py:58
  48.9 13.9 %all-to-all-done = bf16[8,96,384]{2,1,0:T(8,128)(2,1)S(1)} async-done(((bf16[8,96,384]{2,1,0:T(8,128)(2,1)}), bf16[8,96,384]{2,1,0:T(8,128)(2,1)S(1)}, u32[]{:S(2)}, u32[]{:S(2)}) %all-to-all-start) | async-done | bytes 589856 | tf_op jit(solution)/shard_map/all_to_all | solution.py:58
  62.8 18.6 %attention.1 = bf16[768,512]{1,0:T(8,128)(2,1)} custom-call(bf16[768,384]{1,0:T(8,128)(2,1)S(1)} %bitcast.154, bf16[768,128]{1,0:T(8,128)(2,1)S(1)} %slice.415.back_ref, bf16[768,4]{1,0:T(8,128)(2,1)S(1)} %slice.416.bias_ref), custom_call_target="tpu_custom_call" | custom-call | flops 1056964608 | bytes 1572864 | tf_op jit(solution)/shard_map/attention/pallas_call | solution.py:165
  81.5 4.3 %all-to-all-start.2 = ((bf16[8,96,512]{2,1,0:T(8,128)(2,1)}), bf16[8,96,512]{2,1,0:T(8,128)(2,1)}, u32[]{:S(2)}, u32[]{:S(2)}) async-start(bf16[8,96,512]{2,1,0:T(8,128)(2,1)} %bitcast.22), calls=%async_computation.2 | async-start | bytes 1572864 | tf_op jit(solution)/shard_map/all_to_all | solution.py:58
  130.1 3.5 %copy.210 = bf16[192,4,1,192]{0,3,1,2:T(8,128)(2,1)} copy(bf16[192,4,1,192]{3,2,1,0:T(2,128)(2,1)} %get-tuple-element.112) | data formatting | bytes 589824 | tf_op jit(solution)/shard_map/jit(_where)/select_n | solution.py:67
  136.7 4.6 %collective-permute-start.6 = (bf16[1,96,512]{2,1,0:T(8,128)(2,1)S(1)}, bf16[1,96,512]{2,1,0:T(8,128)(2,1)S(1)}, u32[]{:S(2)}, u32[]{:S(2)}) collective-permute-start(bf16[1,96,512]{2,1,0:T(8,128)(2,1)S(1)} %get-tuple-element.130), channel_id=1, source_target_pairs={{0,8},{8,16},{16,24},{1,9},{9,17},{17,25},{2,10},{10,18},{18,26},{... | collective-permute-start | bytes 294920 | tf_op jit(solution)/shard_map/ppermute | solution.py:44
  145.8 6.7 %all-to-all-start.5 = ((bf16[4,256,512]{2,1,0:T(8,128)(2,1)}), bf16[4,256,512]{2,1,0:T(8,128)(2,1)}, u32[]{:S(2)}, u32[]{:S(2)}) async-start(bf16[4,256,512]{2,1,0:T(8,128)(2,1)} %fusion.45), calls=%async_computation.5 | async-start | bytes 2097152 | tf_op jit(solution)/shard_map/all_to_all | solution.py:58
  152.5 4.1 %multiply_convert_fusion.1 = bf16[4,96,2048]{2,1,0:T(8,128)(2,1)S(1)} fusion(f32[4,96,2048]{2,1,0:T(8,128)} %copy-done.9, bf16[2048,512]{1,0:T(8,128)(2,1)} %param.16, bf16[1,96,512]{2,1,0:T(8,128)(2,1)S(1)} %collective-permute-done.7, bf16[2,96,512]{2,1,0:T(8,128)(2,1)S(1)} %concatenate.97, bf16[1,96,512]{2,1,0:T(8,128)(2,1)S(1)} %collective-permute-done.6), kind=kOutput, calls=%fused_computation.11 | convolution fusion | flops 812777472 | bytes 7208960 | tf_op jit(solution)/shard_map/dot_general | solution.py:88
  161.0 5.3 %fusion.25 = (f32[2048]{0:T(1024)S(1)}, f32[2048]{0:T(1024)S(1)}, f32[2048]{0:T(1024)S(1)}, f32[2048]{0:T(1024)S(1)}, f32[2048]{0:T(1024)S(1)}, /*index=5*/f32[2...) fusion(bf16[6,1,2048]{2,1,0:T(2,128)(2,1)S(1)} %copy-done.33, ...), kind=kLoop, calls=%fused_computation.49 | loop fusion | flops 18462720 | bytes 7938144 | tf_op jit(solution)/shard_map/reduce_sum | solution.py:355
  166.5 5.0 %fusion.33 = bf16[2,96,2048]{2,1,0:T(8,128)(2,1)S(1)} fusion(f32[6,96,2048]{2,1,0:T(8,128)} %get-tuple-element.148, bf16[4,95,2048]{2,1,0:T(8,128)(2,1)} %get-tuple-element.110, bf16[4,95,2048]{2,1,0:T(8,128)(2,1)} %get-tuple-element.109, bf16[4,1,2048]{2,1,0:T(2,128)(2,1)} %get-tuple-element.108, bf16[4,1,2048]{2,1,0:T(2,128)(2,1)} %get-tuple-element.107, ...), kind=kLoop, calls=%fused_computation.57 | loop fusion | flops 21233664 | bytes 7938144 | tf_op jit(solution)/shard_map/convert_element_type | solution.py:361
  181.6 4.6 %all-to-all-start.7 = ((bf16[4,1024,128]{2,1,0:T(8,128)(2,1)}), bf16[4,1024,128]{2,1,0:T(8,128)(2,1)}, u32[]{:S(2)}, u32[]{:S(2)}) async-start(bf16[4,1024,128]{2,1,0:T(8,128)(2,1)} %bitcast.159), calls=%async_computation.7 | async-start | bytes 2097152 | tf_op jit(solution)/shard_map/all_to_all | solution.py:58
  191.3 10.7 %all-to-all-done.7 = bf16[4,1024,128]{2,1,0:T(8,128)(2,1)} async-done(((bf16[4,1024,128]{2,1,0:T(8,128)(2,1)}), bf16[4,1024,128]{2,1,0:T(8,128)(2,1)}, u32[]{:S(2)}, u32[]{:S(2)}) %all-to-all-start.7) | async-done | bytes 1048608 | tf_op jit(solution)/shard_map/all_to_all | solution.py:58
  201.9 4.3 %all-to-all-start.6 = ((bf16[4,64,512]{2,1,0:T(8,128)(2,1)}), bf16[4,64,512]{2,1,0:T(8,128)(2,1)}, u32[]{:S(2)}, u32[]{:S(2)}) async-start(bf16[4,64,512]{2,1,0:T(8,128)(2,1)} %bitcast.45), calls=%async_computation.6 | async-start | bytes 524288 | tf_op jit(solution)/shard_map/all_to_all | solution.py:58
  211.7 3.7 %all-to-all-done.6 = bf16[4,64,512]{2,1,0:T(8,128)(2,1)} async-done(((bf16[4,64,512]{2,1,0:T(8,128)(2,1)}), bf16[4,64,512]{2,1,0:T(8,128)(2,1)}, u32[]{:S(2)}, u32[]{:S(2)}) %all-to-all-start.6) | async-done | bytes 262176 | tf_op jit(solution)/shard_map/all_to_all | solution.py:58
  215.4 4.3 %all-to-all-start.3 = ((bf16[4,147,1024]{2,1,0:T(8,128)(2,1)}), bf16[4,147,1024]{2,1,0:T(8,128)(2,1)}, u32[]{:S(2)}, u32[]{:S(2)}) async-start(bf16[4,147,1024]{2,1,0:T(8,128)(2,1)} %pad_maximum_fusion), calls=%async_computation.3 | async-start | bytes 2490368 | tf_op jit(solution)/shard_map/all_to_all | solution.py:58
  225.6 8.5 %all-to-all-done.3 = bf16[4,147,1024]{2,1,0:T(8,128)(2,1)} async-done(((bf16[4,147,1024]{2,1,0:T(8,128)(2,1)}), bf16[4,147,1024]{2,1,0:T(8,128)(2,1)}, u32[]{:S(2)}, u32[]{:S(2)}) %all-to-all-start.3) | async-done | bytes 1204256 | tf_op jit(solution)/shard_map/all_to_all | solution.py:58
  234.1 4.0 %all-to-all-start.8 = ((bf16[4,256,128]{2,1,0:T(8,128)(2,1)}), bf16[4,256,128]{2,1,0:T(8,128)(2,1)}, u32[]{:S(2)}, u32[]{:S(2)}) async-start(bf16[4,256,128]{2,1,0:T(8,128)(2,1)} %bitcast.60), calls=%async_computation.8 | async-start | bytes 524288 | tf_op jit(solution)/shard_map/all_to_all | solution.py:58
  242.3 4.2 %all-to-all-done.8 = bf16[4,256,128]{2,1,0:T(8,128)(2,1)} async-done(((bf16[4,256,128]{2,1,0:T(8,128)(2,1)}), bf16[4,256,128]{2,1,0:T(8,128)(2,1)}, u32[]{:S(2)}, u32[]{:S(2)}) %all-to-all-start.8) | async-done | bytes 262176 | tf_op jit(solution)/shard_map/all_to_all | solution.py:58
  253.9 6.9 %all-to-all-done.4 = bf16[4,204,256]{2,1,0:T(8,128)(2,1)S(1)} async-done(((bf16[4,204,256]{2,1,0:T(8,128)(2,1)}), bf16[4,204,256]{2,1,0:T(8,128)(2,1)S(1)}, u32[]{:S(2)}, u32[]{:S(2)}) %all-to-all-start.4) | async-done | bytes 417824 | tf_op jit(solution)/shard_map/all_to_all | solution.py:58
  (263 shorter events, 119.2 us)
Async XLA Ops:
  1.8 12.8 %collective-permute-start = (bf16[2,3,512]{2,1,0:T(4,128)(2,1)S(1)}, bf16[2,3,512]{2,1,0:T(4,128)(2,1)S(1)}, u32[]{:S(2)}, u32[]{:S(2)}) collective-permute-start(bf16[2,3,512]{2,1,0:T(4,128)(2,1)S(1)} %get-tuple-element.134), channel_id=1, source_target_pairs={{0,1},{1,2},{2,3},{3,4},{4,5},{5,6},{6,7},{7,0},{8,9},{9,10},{10,1... | collective-permute-start | bytes 18440 | tf_op jit(solution)/shard_map/ppermute | solution.py:44
  2.3 12.3 %collective-permute-start.1 = (bf16[2,3,512]{2,1,0:T(4,128)(2,1)S(1)}, bf16[2,3,512]{2,1,0:T(4,128)(2,1)S(1)}, u32[]{:S(2)}, u32[]{:S(2)}) collective-permute-start(bf16[2,3,512]{2,1,0:T(4,128)(2,1)S(1)} %get-tuple-element.135), channel_id=1, source_target_pairs={{0,7},{1,0},{2,1},{3,2},{4,3},{5,4},{6,5},{7,6},{8,15},{9,8},{10,9... | collective-permute-start | bytes 18440 | tf_op jit(solution)/shard_map/ppermute | solution.py:47
  11.1 30.0 %all-to-all-start.1 = ((bf16[8,96,132]{1,2,0:T(8,128)(2,1)}), bf16[8,96,132]{1,2,0:T(8,128)(2,1)S(1)}, u32[]{:S(2)}, u32[]{:S(2)}) async-start(bf16[8,96,132]{1,2,0:T(8,128)(2,1)} %bitcast.170), calls=%async_computation.1 | async-start | bytes 557056 | tf_op jit(solution)/shard_map/all_to_all | solution.py:58
  14.7 10.2 %collective-permute-start.3 = (bf16[2,96,512]{2,1,0:T(8,128)(2,1)S(1)}, bf16[2,96,512]{2,1,0:T(8,128)(2,1)S(1)}, u32[]{:S(2)}, u32[]{:S(2)}) collective-permute-start(bf16[2,96,512]{2,1,0:T(8,128)(2,1)S(1)} %pad_maximum_fusion.7), channel_id=1, source_target_pairs={{8,0},{16,8},{24,16},{9,1},{17,9},{25,17},{10,2},{18,10},{26,18},{... | collective-permute-start | bytes 589832 | tf_op jit(solution)/shard_map/ppermute | solution.py:47
  41.1 21.7 %all-to-all-start = ((bf16[8,96,384]{2,1,0:T(8,128)(2,1)}), bf16[8,96,384]{2,1,0:T(8,128)(2,1)S(1)}, u32[]{:S(2)}, u32[]{:S(2)}) async-start(bf16[8,96,384]{2,1,0:T(8,128)(2,1)} %bitcast.162), calls=%async_computation | async-start | bytes 1179648 | tf_op jit(solution)/shard_map/all_to_all | solution.py:58
  81.5 25.3 %all-to-all-start.2 = ((bf16[8,96,512]{2,1,0:T(8,128)(2,1)}), bf16[8,96,512]{2,1,0:T(8,128)(2,1)}, u32[]{:S(2)}, u32[]{:S(2)}) async-start(bf16[8,96,512]{2,1,0:T(8,128)(2,1)} %bitcast.22), calls=%async_computation.2 | async-start | bytes 1572864 | tf_op jit(solution)/shard_map/all_to_all | solution.py:58
  85.8 15.9 %collective-permute-start.12 = (bf16[192,2048]{1,0:T(8,128)(2,1)S(1)}, bf16[192,2048]{1,0:T(8,128)(2,1)}, u32[]{:S(2)}, u32[]{:S(2)}) collective-permute-start(bf16[192,2048]{1,0:T(8,128)(2,1)S(1)} %bitcast.155), channel_id=1, source_target_pairs={{0,1},{1,0},{2,3},{3,2},{4,5},{5,4},{6,7},{7,6},{8,9},{9,8},{10,11... | collective-permute-start | bytes 2359304 | tf_op jit(solution)/shard_map/ppermute | solution.py:54
  86.2 13.8 %collective-permute-start.14 = (bf16[192,512]{1,0:T(8,128)(2,1)}, bf16[192,512]{1,0:T(8,128)(2,1)}, u32[]{:S(2)}, u32[]{:S(2)}) collective-permute-start(bf16[192,512]{1,0:T(8,128)(2,1)} %bitcast.164), channel_id=1, source_target_pairs={{0,1},{1,0},{2,3},{3,2},{4,5},{5,4},{6,7},{7,6},{8,9},{9,8},{10,11... | collective-permute-start | bytes 589832 | tf_op jit(solution)/shard_map/ppermute | solution.py:54
  96.9 111.7 %collective-permute-start.8 = (bf16[192,512]{1,0:T(8,128)(2,1)}, bf16[192,512]{1,0:T(8,128)(2,1)}, u32[]{:S(2)}, u32[]{:S(2)}) collective-permute-start(bf16[192,512]{1,0:T(8,128)(2,1)} %bitcast.178), channel_id=1, source_target_pairs={{0,1},{1,0},{2,3},{3,2},{4,5},{5,4},{6,7},{7,6},{8,9},{9,8},{10,11... | collective-permute-start | bytes 589832 | tf_op jit(solution)/shard_map/ppermute | solution.py:54
  121.4 54.9 %collective-permute-start.16 = (bf16[192,512]{1,0:T(8,128)(2,1)}, bf16[192,512]{1,0:T(8,128)(2,1)}, u32[]{:S(2)}, u32[]{:S(2)}) collective-permute-start(bf16[192,512]{1,0:T(8,128)(2,1)} %bitcast.153), channel_id=1, source_target_pairs={{0,1},{1,0},{2,3},{3,2},{4,5},{5,4},{6,7},{7,6},{8,9},{9,8},{10,11... | collective-permute-start | bytes 589832 | tf_op jit(solution)/shard_map/ppermute | solution.py:54
  121.4 14.1 %collective-permute-start.5 = (bf16[2,1,512]{2,1,0:T(2,128)(2,1)S(1)}, bf16[2,1,512]{2,1,0:T(2,128)(2,1)S(1)}, u32[]{:S(2)}, u32[]{:S(2)}) collective-permute-start(bf16[2,1,512]{2,1,0:T(2,128)(2,1)S(1)} %get-tuple-element.132), channel_id=1, source_target_pairs={{0,7},{1,0},{2,1},{3,2},{4,3},{5,4},{6,5},{7,6},{8,15},{9,8},{10,9... | collective-permute-start | bytes 6152 | tf_op jit(solution)/shard_map/ppermute | solution.py:47
  122.7 12.8 %collective-permute-start.4 = (bf16[2,1,512]{2,1,0:T(2,128)(2,1)S(1)}, bf16[2,1,512]{2,1,0:T(2,128)(2,1)S(1)}, u32[]{:S(2)}, u32[]{:S(2)}) collective-permute-start(bf16[2,1,512]{2,1,0:T(2,128)(2,1)S(1)} %get-tuple-element.133), channel_id=1, source_target_pairs={{0,1},{1,2},{2,3},{3,4},{4,5},{5,6},{6,7},{7,0},{8,9},{9,10},{10,1... | collective-permute-start | bytes 6152 | tf_op jit(solution)/shard_map/ppermute | solution.py:44
  126.5 50.9 %collective-permute-start.15 = (bf16[192,256]{0,1:T(8,128)(2,1)}, bf16[192,256]{0,1:T(8,128)(2,1)}, u32[]{:S(2)}, u32[]{:S(2)}) collective-permute-start(bf16[192,256]{0,1:T(8,128)(2,1)} %bitcast.54), channel_id=1, source_target_pairs={{0,1},{1,0},{2,3},{3,2},{4,5},{5,4},{6,7},{7,6},{8,9},{9,8},{10,11... | collective-permute-start | bytes 294920 | tf_op jit(solution)/shard_map/ppermute | solution.py:54
  136.7 15.8 %collective-permute-start.6 = (bf16[1,96,512]{2,1,0:T(8,128)(2,1)S(1)}, bf16[1,96,512]{2,1,0:T(8,128)(2,1)S(1)}, u32[]{:S(2)}, u32[]{:S(2)}) collective-permute-start(bf16[1,96,512]{2,1,0:T(8,128)(2,1)S(1)} %get-tuple-element.130), channel_id=1, source_target_pairs={{0,8},{8,16},{16,24},{1,9},{9,17},{17,25},{2,10},{10,18},{18,26},{... | collective-permute-start | bytes 294920 | tf_op jit(solution)/shard_map/ppermute | solution.py:44
  141.3 11.2 %collective-permute-start.7 = (bf16[1,96,512]{2,1,0:T(8,128)(2,1)S(1)}, bf16[1,96,512]{2,1,0:T(8,128)(2,1)S(1)}, u32[]{:S(2)}, u32[]{:S(2)}) collective-permute-start(bf16[1,96,512]{2,1,0:T(8,128)(2,1)S(1)} %get-tuple-element.131), channel_id=1, source_target_pairs={{8,0},{16,8},{24,16},{9,1},{17,9},{25,17},{10,2},{18,10},{26,18},{... | collective-permute-start | bytes 294920 | tf_op jit(solution)/shard_map/ppermute | solution.py:47
  145.8 35.8 %all-to-all-start.5 = ((bf16[4,256,512]{2,1,0:T(8,128)(2,1)}), bf16[4,256,512]{2,1,0:T(8,128)(2,1)}, u32[]{:S(2)}, u32[]{:S(2)}) async-start(bf16[4,256,512]{2,1,0:T(8,128)(2,1)} %fusion.45), calls=%async_computation.5 | async-start | bytes 2097152 | tf_op jit(solution)/shard_map/all_to_all | solution.py:58
  152.5 26.1 %collective-permute-start.13 = (bf16[192,768]{0,1:T(8,128)(2,1)}, bf16[192,768]{0,1:T(8,128)(2,1)}, u32[]{:S(2)}, u32[]{:S(2)}) collective-permute-start(bf16[192,768]{0,1:T(8,128)(2,1)} %bitcast.48), channel_id=1, source_target_pairs={{0,1},{1,0},{2,3},{3,2},{4,5},{5,4},{6,7},{7,6},{8,9},{9,8},{10,11... | collective-permute-start | bytes 884744 | tf_op jit(solution)/shard_map/ppermute | solution.py:54
  181.6 20.3 %all-to-all-start.7 = ((bf16[4,1024,128]{2,1,0:T(8,128)(2,1)}), bf16[4,1024,128]{2,1,0:T(8,128)(2,1)}, u32[]{:S(2)}, u32[]{:S(2)}) async-start(bf16[4,1024,128]{2,1,0:T(8,128)(2,1)} %bitcast.159), calls=%async_computation.7 | async-start | bytes 2097152 | tf_op jit(solution)/shard_map/all_to_all | solution.py:58
  186.9 19.4 %collective-permute-start.10 = (f32[19456]{0:T(1024)}, f32[19456]{0:T(1024)}, u32[]{:S(2)}, u32[]{:S(2)}) collective-permute-start(f32[19456]{0:T(1024)} %pad_maximum_fusion.8), channel_id=1, source_target_pairs={{0,1},{1,0},{2,3},{3,2},{4,5},{5,4},{6,7},{7,6},{8,9},{9,8},{10,11... | collective-permute-start | bytes 233480 | tf_op jit(solution)/shard_map/ppermute | solution.py:54
  189.0 19.6 %collective-permute-start.9 = (bf16[192,1024]{1,0:T(8,128)(2,1)S(1)}, bf16[192,1024]{1,0:T(8,128)(2,1)}, u32[]{:S(2)}, u32[]{:S(2)}) collective-permute-start(bf16[192,1024]{1,0:T(8,128)(2,1)S(1)} %bitcast.177), channel_id=1, source_target_pairs={{0,1},{1,0},{2,3},{3,2},{4,5},{5,4},{6,7},{7,6},{8,9},{9,8},{10,11... | collective-permute-start | bytes 1179656 | tf_op jit(solution)/shard_map/ppermute | solution.py:54
  201.9 13.4 %all-to-all-start.6 = ((bf16[4,64,512]{2,1,0:T(8,128)(2,1)}), bf16[4,64,512]{2,1,0:T(8,128)(2,1)}, u32[]{:S(2)}, u32[]{:S(2)}) async-start(bf16[4,64,512]{2,1,0:T(8,128)(2,1)} %bitcast.45), calls=%async_computation.6 | async-start | bytes 524288 | tf_op jit(solution)/shard_map/all_to_all | solution.py:58
  215.4 18.7 %all-to-all-start.3 = ((bf16[4,147,1024]{2,1,0:T(8,128)(2,1)}), bf16[4,147,1024]{2,1,0:T(8,128)(2,1)}, u32[]{:S(2)}, u32[]{:S(2)}) async-start(bf16[4,147,1024]{2,1,0:T(8,128)(2,1)} %pad_maximum_fusion), calls=%async_computation.3 | async-start | bytes 2490368 | tf_op jit(solution)/shard_map/all_to_all | solution.py:58
  234.1 12.4 %all-to-all-start.8 = ((bf16[4,256,128]{2,1,0:T(8,128)(2,1)}), bf16[4,256,128]{2,1,0:T(8,128)(2,1)}, u32[]{:S(2)}, u32[]{:S(2)}) async-start(bf16[4,256,128]{2,1,0:T(8,128)(2,1)} %bitcast.60), calls=%async_computation.8 | async-start | bytes 524288 | tf_op jit(solution)/shard_map/all_to_all | solution.py:58
  246.5 14.3 %all-to-all-start.4 = ((bf16[4,204,256]{2,1,0:T(8,128)(2,1)}), bf16[4,204,256]{2,1,0:T(8,128)(2,1)S(1)}, u32[]{:S(2)}, u32[]{:S(2)}) async-start(bf16[4,204,256]{2,1,0:T(8,128)(2,1)} %copy.206), calls=%async_computation.4 | async-start | bytes 851968 | tf_op jit(solution)/shard_map/all_to_all | solution.py:58
  (55 other events, 326.6 us)

commit v2 on v1

v2 whole, which is shorter than its diff:
```python
import functools
import math

import jax
import jax.numpy as jnp
from jax import lax
from jax.experimental import pallas as pl
from jax.experimental.pallas import tpu as pltpu
from jax.sharding import Mesh
from jax.sharding import PartitionSpec as P

EPSILON = 1e-06
LON = ("z", "core")
BF16 = jnp.bfloat16
F32 = jnp.float32
MASKED = -1e30
SIDE = 3
LOG2E = math.log2(math.e)


def inverse_rms(values):
    return lax.rsqrt(jnp.mean(values * values, axis=-1, keepdims=True) + EPSILON)


def norm_back(back_normed, state, inverse, gain):
    scaled = back_normed * gain
    return inverse * scaled - inverse * inverse * inverse * state * jnp.mean(
        scaled * state, axis=-1, keepdims=True
    )


def shifts(count, step, periodic):
    return [(i, (i + step) % count) for i in range(count) if periodic or 0 <= i + step < count]


def from_sides(block, width, dim, axis, periodic):
    count = lax.axis_size(axis)
    size = block.shape[dim]
    low = lax.ppermute(
        lax.slice_in_dim(block, size - width, size, axis=dim), axis, shifts(count, 1, periodic)
    )
    high = lax.ppermute(
        lax.slice_in_dim(block, 0, width, axis=dim), axis, shifts(count, -1, periodic)
    )
    return low, high


def core_swap(values):
    return lax.ppermute(values, "core", [(0, 1), (1, 0)])


def exchange(values, axis):
    return lax.all_to_all(values, axis, 0, 0, tiled=True)


def matmul(left, right):
    return jnp.dot(left, right, preferred_element_type=F32)


def cross_cells(left, right):
    return lax.dot_general(left, right, (((0,), (0,)), ((), ())), preferred_element_type=F32)


def times_transpose(values, weights):
    return lax.dot_general(
        values, weights, (((values.ndim - 1,), (1,)), ((), ())), preferred_element_type=F32
    )


def sigmoid(values):
    return 0.5 + 0.5 * jnp.tanh(0.5 * values)


def silu(values):
    return values * sigmoid(values)


def silu_slope(values):
    gate = sigmoid(values)
    return gate * (1.0 + values * (1.0 - gate))


def call(kernel, name, out_shape, *operands, scratch=(), megabytes=24, flops=0):
    return pl.pallas_call(
        kernel,
        out_shape=out_shape,
        scratch_shapes=scratch,
        compiler_params=pltpu.CompilerParams(vmem_limit_bytes=megabytes * 1024 * 1024),
        cost_estimate=pl.CostEstimate(
            flops=flops,
            bytes_accessed=sum(x.size * x.dtype.itemsize for x in operands),
            transcendentals=0,
        ),
        name=name,
    )(*operands)


def early_kernel(groups, cot_ref, bias_ref, out_weight_ref, early_ref, framed_ref, bias_frame):
    row_count, lon_count, channels = cot_ref.shape
    frame = early_ref.shape[1]
    width = channels // groups
    items = bias_ref.shape[2] // groups
    framed_ref[...] = jnp.zeros_like(framed_ref)
    bias_frame[...] = jnp.full_like(bias_frame, MASKED)
    for row in range(row_count):
        framed_ref[row, SIDE : SIDE + lon_count, :] = cot_ref[row]
        bias_frame[row, SIDE : SIDE + lon_count, :] = bias_ref[row].astype(F32)
    for row in range(row_count):
        back_heads = times_transpose(framed_ref[row], out_weight_ref[...]).astype(BF16)
        for group in range(groups):
            target = row * groups + group
            early_ref[target, :, 0:width] = back_heads[:, group * width : (group + 1) * width]
            early_ref[target, :, width : width + items] = bias_frame[
                row, :, group * items : (group + 1) * items
            ].astype(BF16)


def early_parts(cotangent, key_bias, attention_out, groups):
    row_count, lon_count, channels = cotangent.shape
    frame = lon_count + 2 * SIDE
    head_count = key_bias.shape[2]
    return call(
        functools.partial(early_kernel, groups),
        "back_heads",
        (
            jax.ShapeDtypeStruct(
                (row_count * groups, frame, (channels + head_count) // groups), BF16
            ),
            jax.ShapeDtypeStruct((row_count, frame, channels), BF16),
        ),
        cotangent,
        key_bias,
        attention_out,
        scratch=[pltpu.VMEM((row_count, frame, head_count), F32)],
        flops=2 * row_count * frame * channels * channels,
    )


def normalise(values, gain):
    return (values * inverse_rms(values) * gain).astype(BF16)


def convolve(values, kernel, rows, frame):
    size = rows * frame
    total = None
    for b in range(3):
        part = kernel[b : b + 1] * values[0:size]
        for a in range(1, 3):
            part = part + kernel[3 * a + b : 3 * a + b + 1] * values[a * frame : a * frame + size]
        if b != 1:
            part = pltpu.roll(part, 1 if b == 0 else size - 1, 0)
        total = part if total is None else total + part
    return total


def forward_kernel(
    frame, groups, state_ref, gain_ref, expand_ref, kernel_ref, shrink_ref, second_gain_ref, in_ref,
    qkv_ref, inner_ref, normed, total,
):
    step = pl.program_id(0)
    cells, channels = inner_ref.shape
    rows = cells // frame
    width = channels // groups

    @pl.when(step == 0)
    def _():
        normed[...] = normalise(state_ref[...].astype(F32), gain_ref[...])
        total[...] = jnp.zeros_like(total)

    activated = silu(matmul(normed[...], expand_ref[...])).astype(BF16).astype(F32)
    mixed = silu(convolve(activated, kernel_ref[...], rows, frame)).astype(BF16)
    total[...] += matmul(mixed, shrink_ref[...])

    @pl.when(step == pl.num_programs(0) - 1)
    def _():
        inner = (state_ref[frame : frame + cells, :].astype(F32) + total[...]).astype(BF16)
        inner_ref[...] = inner
        normed_second = normalise(inner.astype(F32), second_gain_ref[...])
        projected = matmul(normed_second, in_ref[...]).astype(BF16)
        for row in range(rows):
            for group in range(groups):
                for kind in range(3):
                    start = kind * channels + group * width
                    qkv_ref[row * groups + group, :, kind * width : (kind + 1) * width] = projected[
                        row * frame : (row + 1) * frame, start : start + width
                    ]


def step_width(wide):
    return 256 if wide % 256 == 0 else wide


def forward(state, input_gain, expand_weight, kernel, shrink_weight, gain, attention_in, groups):
    all_rows, frame, channels = state.shape
    rows = all_rows - 2
    cells = rows * frame
    wide = expand_weight.shape[1]
    part = step_width(wide)
    fixed = lambda shape: pl.BlockSpec(shape, lambda step: (0,) * len(shape))
    return pl.pallas_call(
        functools.partial(forward_kernel, frame, groups),
        grid=(wide // part,),
        out_shape=(
            jax.ShapeDtypeStruct((rows * groups, frame, 3 * channels // groups), BF16),
            jax.ShapeDtypeStruct((cells, channels), BF16),
        ),
        in_specs=[
            fixed((all_rows * frame, channels)),
            fixed((1, channels)),
            pl.BlockSpec((channels, part), lambda step: (0, step)),
            pl.BlockSpec((9, part), lambda step: (0, step)),
            pl.BlockSpec((part, channels), lambda step: (step, 0)),
            fixed((1, channels)),
            fixed(attention_in.shape),
        ],
        out_specs=(
            fixed((rows * groups, frame, 3 * channels // groups)),
            fixed((cells, channels)),
        ),
        scratch_shapes=[
            pltpu.VMEM((all_rows * frame, channels), BF16),
            pltpu.VMEM((cells, channels), F32),
        ],
        compiler_params=pltpu.CompilerParams(
            vmem_limit_bytes=24 * 1024 * 1024, dimension_semantics=("arbitrary",)
        ),
        cost_estimate=pl.CostEstimate(
            flops=2 * cells * channels * (3 * wide + 3 * channels),
            bytes_accessed=4 * channels * wide + 6 * channels * channels,
            transcendentals=3 * cells * wide,
        ),
        name="forward",
    )(
        state.reshape(all_rows * frame, channels),
        input_gain,
        expand_weight,
        kernel,
        shrink_weight,
        gain,
        attention_in,
    )


def around_kernel(
    frame, state_ref, gain_ref, expand_ref, kernel_ref, activated_ref, slope_ref, mixed_ref,
    expand_slope_ref, normed,
):
    size = activated_ref.shape[0]
    cells = mixed_ref.shape[0]

    @pl.when(pl.program_id(0) == 0)
    def _():
        normed[...] = normalise(state_ref[...].astype(F32), gain_ref[...])

    expanded = matmul(normed[...], expand_ref[...])
    gate = sigmoid(expanded)
    activated = (expanded * gate).astype(BF16)
    activated_ref[...] = activated[frame : frame + size]
    own_gate, own = gate[2 * frame : 2 * frame + cells], expanded[2 * frame : 2 * frame + cells]
    expand_slope_ref[...] = own_gate * (1.0 + own * (1.0 - own_gate))
    convolved = convolve(activated.astype(F32), kernel_ref[...], size // frame, frame)
    gate = sigmoid(convolved)
    slope_ref[...] = gate * (1.0 + convolved * (1.0 - gate))
    mixed_ref[...] = (
        convolved[frame : frame + cells] * gate[frame : frame + cells]
    ).astype(BF16)


def around(state, input_gain, expand_weight, kernel):
    all_rows, frame, channels = state.shape
    size, cells = (all_rows - 2) * frame, (all_rows - 4) * frame
    wide = expand_weight.shape[1]
    part = step_width(wide)
    fixed = lambda shape: pl.BlockSpec(shape, lambda step: (0,) * len(shape))
    moving = lambda rows: pl.BlockSpec((rows, part), lambda step: (0, step))
    return pl.pallas_call(
        functools.partial(around_kernel, frame),
        grid=(wide // part,),
        out_shape=(
            jax.ShapeDtypeStruct((size, wide), BF16),
            jax.ShapeDtypeStruct((size, wide), F32),
            jax.ShapeDtypeStruct((cells, wide), BF16),
            jax.ShapeDtypeStruct((cells, wide), F32),
        ),
        in_specs=[
            fixed((all_rows * frame, channels)),
            fixed((1, channels)),
            moving(channels),
            moving(9),
        ],
        out_specs=(moving(size), moving(size), moving(cells), moving(cells)),
        scratch_shapes=[pltpu.VMEM((all_rows * frame, channels), BF16)],
        compiler_params=pltpu.CompilerParams(
            vmem_limit_bytes=24 * 1024 * 1024, dimension_semantics=("arbitrary",)
        ),
        cost_estimate=pl.CostEstimate(
            flops=2 * all_rows * frame * channels * wide,
            bytes_accessed=2 * channels * wide + 14 * size * wide,
            transcendentals=2 * size * wide,
        ),
        name="forward_around",
    )(state.reshape(all_rows * frame, channels), input_gain, expand_weight, kernel)


def inner_kernel(
    groups, norm_factor, attended_ref, inner_ref, cot_ref, out_weight_ref, in_weight_ref, gain_ref,
    output_ref, back_inner_ref, unpacked_ref, gain_grad_ref,
):
    targets, frame, width = attended_ref.shape
    width = width // 4
    row_count, lon_count, channels = output_ref.shape
    for target in range(targets):
        row, group = divmod(target, groups)
        for kind in range(4):
            start = kind * channels + group * width
            unpacked_ref[row * frame : (row + 1) * frame, start : start + width] = attended_ref[
                target, :, kind * width : (kind + 1) * width
            ]
    inner = inner_ref[...].astype(F32)
    output = (inner + matmul(unpacked_ref[:, :channels], out_weight_ref[...])).astype(BF16)
    for row in range(row_count):
        start = row * frame + SIDE
        output_ref[row] = output[start : start + lon_count]
    back_second = times_transpose(unpacked_ref[:, channels:], in_weight_ref[...])
    inverse = inverse_rms(inner)
    gain_grad_ref[...] = norm_factor * jnp.sum(back_second * inner * inverse, axis=0, keepdims=True)
    back_inner_ref[...] = (
        cot_ref[...].astype(F32) + norm_back(back_second, inner, inverse, gain_ref[...])
    ).astype(BF16)


def attention_grads_kernel(
    norm_factor, unpacked_ref, inner_ref, gain_ref, cot_ref, part_ref, in_t, out_t
):
    lat_size, lon_size, split, block = part_ref.shape
    channels = inner_ref.shape[1]
    in_split = 3 * channels // lon_size
    out_split = channels // lon_size
    normed_second = normalise(inner_ref[...].astype(F32), gain_ref[...])
    in_t[...] = unpacked_ref[:, channels:].T
    out_t[...] = cot_ref[...].T
    for lat in range(lat_size):
        cols = slice(lat * block, (lat + 1) * block)
        in_grad = (matmul(in_t[...], normed_second[:, cols]) * norm_factor).astype(BF16)
        out_grad = (matmul(out_t[...], unpacked_ref[:, cols]) * norm_factor).astype(BF16)
        for lon in range(lon_size):
            part_ref[lat, lon, 0:in_split, :] = in_grad[lon * in_split : (lon + 1) * in_split]
            part_ref[lat, lon, in_split:, :] = out_grad[lon * out_split : (lon + 1) * out_split]


def shrink_grads_kernel(norm_factor, back_inner_ref, mixed_ref, part_ref, back_t):
    lat_size, _, block = part_ref.shape
    back_t[...] = back_inner_ref[...].T
    for lat in range(lat_size):
        part_ref[lat] = (
            matmul(back_t[...], mixed_ref[:, lat * block : (lat + 1) * block]) * norm_factor
        ).astype(BF16)


def backward_kernel(
    frame, norm_factor, back_ref, state_ref, gain_ref, inside_ref, shrink_ref, slope_ref,
    activated_ref, expand_ref, expand_slope_ref, kernel_ref, part_ref, depth_ref, input_ref,
    gain_grad_ref, normed, back_normed,
):
    step = pl.program_id(0)
    cells, channels = state_ref.shape
    row_count, lon_count, _ = input_ref.shape
    lat_size, _, block, _ = part_ref.shape
    inside = inside_ref[...]

    @pl.when(step == 0)
    def _():
        normed[...] = normalise(state_ref[...].astype(F32), gain_ref[...]).T
        back_normed[...] = jnp.zeros_like(back_normed)

    kernel = kernel_ref[...]
    back_convolved = (
        (times_transpose(back_ref[...], shrink_ref[...]) * slope_ref[...]).astype(BF16).astype(F32)
    )
    flipped = jnp.concatenate([kernel[8 - i : 9 - i] for i in range(9)], axis=0)
    back_activated = convolve(back_convolved, flipped, row_count, frame)
    back_expanded = jnp.where(inside > 0, back_activated * expand_slope_ref[...], 0.0).astype(BF16)
    part_ref[...] = (
        (matmul(normed[...], back_expanded) * norm_factor)
        .astype(BF16)
        .reshape(lat_size, 1, block, back_expanded.shape[1])
    )
    back_normed[...] += times_transpose(back_expanded, expand_ref[...])
    own_back = jnp.where(inside > 0, back_convolved[frame : frame + cells], 0.0)
    activated = activated_ref[...].astype(F32)
    for b in range(3):
        moved = own_back
        if b != 1:
            moved = pltpu.roll(own_back, cells - 1 if b == 0 else 1, 0)
        for a in range(3):
            depth_ref[3 * a + b : 3 * a + b + 1, :] = norm_factor * jnp.sum(
                activated[a * frame : a * frame + cells] * moved, axis=0, keepdims=True
            )

    @pl.when(step == pl.num_programs(0) - 1)
    def _():
        state = state_ref[...].astype(F32)
        inverse = inverse_rms(state)
        grads = back_normed[...]
        gain_grad_ref[...] = norm_factor * jnp.sum(grads * state * inverse, axis=0, keepdims=True)
        result = (
            back_ref[frame : frame + cells, :].astype(F32)
            + norm_back(grads, state, inverse, gain_ref[...])
        ).astype(BF16)
        for row in range(row_count):
            start = row * frame + SIDE
            input_ref[row] = result[start : start + lon_count]


def backward(
    back, state, gain, inside, shrink_weight, slope, activated, expand_weight, expand_slope, kernel,
    norm_factor, lat_size, row_count, lon_count,
):
    cells, channels = state.shape
    frame = cells // row_count
    size = activated.shape[0]
    wide = expand_weight.shape[1]
    part = step_width(wide)
    fixed = lambda shape: pl.BlockSpec(shape, lambda step: (0,) * len(shape))
    moving = lambda rows: pl.BlockSpec((rows, part), lambda step: (0, step))
    block = channels // lat_size
    return pl.pallas_call(
        functools.partial(backward_kernel, frame, norm_factor),
        grid=(wide // part,),
        out_shape=(
            jax.ShapeDtypeStruct((lat_size, wide // part, block, part), BF16),
            jax.ShapeDtypeStruct((9, wide), F32),
            jax.ShapeDtypeStruct((row_count, lon_count, channels), BF16),
            jax.ShapeDtypeStruct((1, channels), F32),
        ),
        in_specs=[
            fixed((size, channels)),
            fixed((cells, channels)),
            fixed((1, channels)),
            fixed((cells, 1)),
            pl.BlockSpec((part, channels), lambda step: (step, 0)),
            moving(size),
            moving(size),
            moving(channels),
            moving(cells),
            moving(9),
        ],
        out_specs=(
            pl.BlockSpec((lat_size, 1, block, part), lambda step: (0, step, 0, 0)),
            moving(9),
            fixed((row_count, lon_count, channels)),
            fixed((1, channels)),
        ),
        scratch_shapes=[
            pltpu.VMEM((channels, cells), BF16),
            pltpu.VMEM((cells, channels), F32),
        ],
        compiler_params=pltpu.CompilerParams(
            vmem_limit_bytes=24 * 1024 * 1024, dimension_semantics=("arbitrary",)
        ),
        cost_estimate=pl.CostEstimate(
            flops=8 * cells * channels * wide,
            bytes_accessed=6 * channels * wide + 12 * size * wide,
            transcendentals=0,
        ),
        name="backward",
    )(
        back, state, gain, inside, shrink_weight, slope, activated, expand_weight, expand_slope,
        kernel,
    )


def attention_kernel(
    head_width, query_block, qkv_ref, early_ref, out_ref, heads_t, query_grad_t, key_t,
    value_t, key_grad, value_grad,
):
    head = pl.program_id(0)
    cells = qkv_ref.shape[0]
    width = qkv_ref.shape[1] // 3
    items = early_ref.shape[1] - width
    scale = 1.0 / math.sqrt(head_width)
    keys = qkv_ref[:, width : 2 * width]
    values = qkv_ref[:, 2 * width : 3 * width]

    @pl.when(head == 0)
    def _():
        key_t[...] = keys.T
        value_t[...] = values.T
        key_grad[...] = jnp.zeros_like(key_grad)
        value_grad[...] = jnp.zeros_like(value_grad)

    lanes = lax.broadcasted_iota(jnp.int32, (1, width), 1) // head_width == head
    zero = jnp.zeros((), BF16)
    head_keys = jnp.where(lanes, keys, zero)
    head_values = jnp.where(lanes, values, zero)
    heads = lax.broadcasted_iota(jnp.int32, (cells, items), 1)
    bias = LOG2E * jnp.sum(
        jnp.where(heads == head, early_ref[:, width:].astype(F32), 0.0), axis=1, keepdims=True
    )
    rows = pl.ds(pl.multiple_of(head * head_width, head_width), head_width)
    head_key_t = key_t[rows, :]
    head_value_t = value_t[rows, :]
    last_dims = (((1,), (1,)), ((), ()))

    def block(start):
        cols = pl.ds(start, query_block)
        queries = qkv_ref[cols, 0:width]
        backs = early_ref[cols, 0:width]
        scores = lax.dot_general(head_keys, queries, last_dims, preferred_element_type=F32)
        scores = scores * (scale * LOG2E) + bias
        exponent = jnp.exp2(scores - jnp.max(scores, axis=0, keepdims=True))
        probs = exponent * (1.0 / jnp.sum(exponent, axis=0, keepdims=True))
        probs_low = probs.astype(BF16)
        heads_t[rows, cols] = matmul(head_value_t, probs_low)
        back_probs = lax.dot_general(head_values, backs, last_dims, preferred_element_type=F32)
        centred = jnp.sum(probs * back_probs, axis=0, keepdims=True)
        back_scores = (probs * (back_probs - centred)).astype(BF16)
        query_grad_t[rows, cols] = matmul(head_key_t, back_scores)
        value_grad[...] += matmul(probs_low, jnp.where(lanes, backs, zero))
        key_grad[...] += matmul(back_scores, jnp.where(lanes, queries, zero))

    block_count = cells // query_block
    if block_count <= 4:
        for index in range(block_count):
            block(index * query_block)
    else:

        def step(index, carry):
            block(pl.multiple_of(index * query_block, query_block))
            return carry

        lax.fori_loop(0, block_count, step, 0)

    @pl.when(head == pl.num_programs(0) - 1)
    def _():
        out_ref[:, 0:width] = heads_t[...].T.astype(BF16)
        out_ref[:, width : 2 * width] = (query_grad_t[...] * scale).T.astype(BF16)
        out_ref[:, 2 * width : 3 * width] = (key_grad[...] * scale).astype(BF16)
        out_ref[:, 3 * width : 4 * width] = value_grad[...].astype(BF16)


def attention(qkv, early, head_width):
    cells = qkv.shape[0]
    width = qkv.shape[1] // 3
    items = early.shape[1] - width
    query_block = 256 if cells % 256 == 0 else 128
    whole = lambda shape: pl.BlockSpec(shape, lambda head: (0, 0))
    return pl.pallas_call(
        functools.partial(attention_kernel, head_width, query_block),
        grid=(items,),
        out_shape=jax.ShapeDtypeStruct((cells, 4 * width), BF16),
        in_specs=[whole(qkv.shape), whole(early.shape)],
        out_specs=whole((cells, 4 * width)),
        scratch_shapes=[
            pltpu.VMEM((width, cells), F32),
            pltpu.VMEM((width, cells), F32),
            pltpu.VMEM((width, cells), BF16),
            pltpu.VMEM((width, cells), BF16),
            pltpu.VMEM((cells, width), F32),
            pltpu.VMEM((cells, width), F32),
        ],
        compiler_params=pltpu.CompilerParams(
            vmem_limit_bytes=48 * 1024 * 1024, dimension_semantics=("arbitrary",)
        ),
        cost_estimate=pl.CostEstimate(
            flops=items * cells * cells * 32 * 14,
            bytes_accessed=cells * width * 16,
            transcendentals=items * cells * cells,
        ),
        name="attention",
    )(qkv, early)


def per_device(
    state_field,
    cotangent,
    key_bias,
    input_gain,
    expand_weight,
    depth_weight,
    shrink_weight,
    attention_gain,
    attention_in,
    attention_out,
):
    row_count, lon_count, channels = state_field.shape
    head_count = key_bias.shape[2]
    head_width = channels // head_count
    wide = expand_weight.shape[1]
    lat_size, z_size = lax.axis_size("lat"), lax.axis_size("z")
    lon_size = 2 * z_size
    core = lax.axis_index("core")
    norm_factor = 1.0 / math.sqrt(row_count * lon_count * lat_size * lon_size)
    items = row_count * head_count // lon_size
    groups = head_count // items
    width = items * head_width
    frame = lon_count + 2 * SIDE
    own = row_count * frame
    kernel = depth_weight.astype(F32).reshape(9, wide)
    input_gain = input_gain.reshape(1, channels)
    attention_gain = attention_gain.reshape(1, channels)

    low, high = from_sides(state_field, SIDE, 1, LON, True)
    state = jnp.concatenate([low, state_field, high], axis=1)
    below, above = from_sides(state, 1, 0, "lat", False)

    early, cot = early_parts(cotangent, key_bias, attention_out, groups)
    early = exchange(early, LON).reshape(lon_size * frame, width + items)

    near = jnp.concatenate([below, state, above], axis=0)
    qkv, inner = forward(
        near, input_gain, expand_weight, kernel, shrink_weight, attention_gain, attention_in, groups
    )
    qkv = exchange(qkv, LON).reshape(lon_size * frame, 3 * width)

    second = (below, above) if row_count == 1 else (state[-2:-1], state[1:2])
    far_below = lax.ppermute(second[0], "lat", shifts(lat_size, 1, False))
    far_above = lax.ppermute(second[1], "lat", shifts(lat_size, -1, False))
    activated, slope, mixed, expand_slope = around(
        jnp.concatenate([far_below, near, far_above], axis=0), input_gain, expand_weight, kernel
    )

    attended = attention(qkv, early, head_width)
    attended = exchange(attended.reshape(lon_size, frame, 4 * width), LON)
    cot = cot.reshape(own, channels)
    output_field, back_inner, unpacked, gain_two = call(
        functools.partial(inner_kernel, groups, norm_factor),
        "back_inner",
        (
            jax.ShapeDtypeStruct((row_count, lon_count, channels), BF16),
            jax.ShapeDtypeStruct((own, channels), BF16),
            jax.ShapeDtypeStruct((own, 4 * channels), BF16),
            jax.ShapeDtypeStruct((1, channels), F32),
        ),
        attended,
        inner,
        cot,
        attention_out,
        attention_in,
        attention_gain,
        flops=8 * own * channels * channels,
    )

    back = back_inner.reshape(row_count, frame, channels)
    centre = back[:, SIDE : SIDE + lon_count]
    low, high = from_sides(centre, 1, 1, LON, True)
    edge = jnp.zeros((row_count, SIDE - 1, channels), BF16)
    back = jnp.concatenate([edge, low, centre, high, edge], axis=1)
    below, above = from_sides(back, 1, 0, "lat", False)
    back = jnp.concatenate([below, back, above], axis=0).reshape(-1, channels)

    def both_cores(parts):
        parts = parts.reshape((lat_size, z_size, 2) + parts.shape[2:])
        mine = lax.dynamic_index_in_dim(parts, core, 2, False)
        theirs = lax.dynamic_index_in_dim(parts, 1 - core, 2, False)
        return (mine.astype(F32) + core_swap(theirs).astype(F32)).astype(BF16)

    def over_lat(parts):
        parts = parts.reshape((lat_size, -1) + parts.shape[3:])
        return jnp.sum(exchange(parts, "lat").astype(F32), axis=0)

    def over_z(parts):
        parts = parts.reshape((z_size, -1) + parts.shape[1:]).astype(BF16)
        return jnp.sum(exchange(parts, "z").astype(F32), axis=0)

    block = channels // lat_size
    in_split, out_split = 3 * channels // lon_size, channels // lon_size
    attention_part = call(
        functools.partial(attention_grads_kernel, norm_factor),
        "attention_grads",
        jax.ShapeDtypeStruct((lat_size, lon_size, in_split + out_split, block), BF16),
        unpacked,
        inner,
        attention_gain,
        cot,
        scratch=[pltpu.VMEM((3 * channels, own), BF16), pltpu.VMEM((channels, own), BF16)],
        flops=8 * own * channels * channels,
    )
    attention_part = over_z(over_lat(both_cores(attention_part)))
    shrink_part = call(
        functools.partial(shrink_grads_kernel, norm_factor),
        "shrink_grads",
        jax.ShapeDtypeStruct((lat_size, channels, wide // lat_size), BF16),
        back_inner,
        mixed,
        scratch=[pltpu.VMEM((channels, own), BF16)],
        flops=2 * own * channels * wide,
    )
    shrink_part = over_z(
        over_lat(both_cores(shrink_part.reshape(lat_size, lon_size, out_split, wide // lat_size)))
    )

    columns = lax.broadcasted_iota(jnp.int32, (row_count, frame, 1), 1).reshape(own, 1)
    inside = ((columns >= SIDE) & (columns < SIDE + lon_count)).astype(F32)
    expand_part, depth_part, input_grad, gain_one = backward(
        back,
        state.reshape(own, channels),
        input_gain,
        inside,
        shrink_weight,
        slope,
        activated,
        expand_weight,
        expand_slope,
        kernel,
        norm_factor,
        lat_size,
        row_count,
        lon_count,
    )

    split = wide // lon_size
    if expand_part.shape[1] != lon_size:
        expand_part = (
            expand_part.reshape(lat_size, expand_part.shape[1], block, -1, split)
            .transpose(0, 1, 3, 2, 4)
            .reshape(lat_size, lon_size, block, split)
        )
    expand_part = both_cores(expand_part).reshape(lat_size, z_size * block, split)
    small = jnp.concatenate([depth_part.reshape(-1), gain_one.reshape(-1), gain_two.reshape(-1)])
    small = (small + core_swap(small)).astype(BF16).reshape(-1, split)
    expand_part = jnp.concatenate(
        [expand_part, jnp.broadcast_to(small, (lat_size,) + small.shape)], axis=1
    )
    expand_part = jnp.sum(exchange(expand_part, "lat").astype(F32), axis=0).astype(BF16)
    small = expand_part[z_size * block :]
    expand_part = jnp.concatenate(
        [
            expand_part[: z_size * block].reshape(z_size, block, split),
            jnp.broadcast_to(small, (z_size,) + small.shape),
        ],
        axis=1,
    )
    expand_part = jnp.sum(exchange(expand_part, "z").astype(F32), axis=0)
    small = expand_part[block:].reshape(-1)
    return (
        output_field,
        input_grad,
        expand_part[:block],
        shrink_part.T,
        attention_part[:in_split].T,
        attention_part[in_split:].T,
        small[: 9 * wide].reshape(3, 3, wide),
        small[9 * wide : 9 * wide + channels],
        small[9 * wide + channels : 9 * wide + 2 * channels],
    )


def solution(mesh):
    lat_size, lon_size = mesh.devices.shape
    split = Mesh(mesh.devices.reshape(lat_size, lon_size // 2, 2), ("lat", "z", "core"))
    grid = P("lat", LON, None)
    weight = P("lat", LON)

    def step(*arrays):
        outputs = jax.shard_map(
            per_device,
            mesh=split,
            in_specs=(grid, grid, grid) + (P(),) * 7,
            out_specs=(grid, grid, weight, weight, weight, weight, P(), P(), P()),
            check_vma=False,
        )(*arrays)
        return outputs

    return step
```

time: 265 us -> 248 us (0.936)
  waiting for transfers between devices: 51 us -> 81.5 us
  Pallas kernels: 18.6 us -> 46.1 us
  matrix products: 26.4 us -> 0 us
  local copies, waits for them, and re-layouts: 68.5 us -> 44.6 us
  other arithmetic: 36.8 us -> 14.1 us
    pallas_call x0 -> x7, Pallas kernels: none -> 28.4 us  [the longest x1 10.1 us: backward(): pl.pallas_call(functools.partial(backward_kernel, frame, norm_factor), gr...]
    dot_general x12 -> x0, matrix products: 26.4 us -> none  [the longest x4 11.9 us: times_transpose(): lax.dot_general(values, weights, (((values.ndim - 1,), (1,)), ((), ())),...]
    all_to_all x9, waiting for transfers between devices: 50.8 us -> 72.9 us  [exchange(): return lax.all_to_all(values, axis, 0, 0, tiled=True)]
    unnamed x120 -> x81, local copies, waits for them, and re-layouts: 14.5 us -> 28.5 us
    slice x21 -> x5, local copies, waits for them, and re-layouts: 14.5 us -> 0.74 us  [the longest x1 0.66 us: per_device(): expand_part[:block]]
    reduce_sum x8 -> x6, other arithmetic: 14 us -> 4.2 us  [the longest x2 3.09 us: over_lat(): return jnp.sum(exchange(parts, 'lat').astype(F32), axis=0)]
    another operation x10 -> x0, local copies, waits for them, and re-layouts: 9.13 us -> none  [the longest x4 7.96 us: own_columns(): view = values.reshape(cells, blocks, 2, -1)]
    concatenate x10 -> x6, local copies, waits for them, and re-layouts: 12 us -> 4.04 us  [the longest x2 3.54 us: per_device(): jnp.concatenate([far_below, near, far_above], axis=0)]
  transfers between devices with their start and end apart: 26 -> 23, of which waited for: 8 -> 11; matrix products, arithmetic and copies ran while one was open for 47% -> 13% of each run, Pallas kernels for 0% -> 12%
where the time goes in v2:
time: 248 us; the launch traced here: 246 us
  waiting for transfers between devices  81.5 us (33%)
  starting transfers between devices  58.7 us (24%)
  Pallas kernels  46.1 us (19%)
  local copies, waits for them, and re-layouts  44.6 us (18%)
  other arithmetic  14.1 us (6%)
    all_to_all x9, waiting for transfers between devices, exchange(): return lax.all_to_all(values, axis, 0, 0, tiled=True)  72.9 us
    all_to_all x9, starting transfers between devices, exchange(): return lax.all_to_all(values, axis, 0, 0, tiled=True)  34.2 us
    unnamed x81, local copies, waits for them, and re-layouts  28.5 us
    pallas_call x1, Pallas kernels, attention(): pl.pallas_call(functools.partial(attention_kernel, head_width, query_bloc...  17.8 us
    pallas_call x1, Pallas kernels, backward(): pl.pallas_call(functools.partial(backward_kernel, frame, norm_factor), gr...  10.1 us
    ppermute x4, starting transfers between devices, from_sides(): lax.ppermute(lax.slice_in_dim(block, size - width, size, axis=dim), axis,...  8.35 us
    ppermute x4, starting transfers between devices, from_sides(): lax.ppermute(lax.slice_in_dim(block, 0, width, axis=dim), axis, shifts(co...  8.08 us
    pallas_call x1, Pallas kernels, forward(): pl.pallas_call(functools.partial(forward_kernel, frame, groups), grid=(wi...  7.42 us
  transfers between devices with their start and end apart: 23, of which 11 were waited for; matrix products, arithmetic and copies ran while one was open for 13% of the time, Pallas kernels for 12%

profile of v2, /device:TPU:0, one launch (start us, length us, event | category | flops | bytes accessed | tf_op | source)
XLA Modules:
  0.0 246.3 jit_solution(11619382746620650791)
XLA Ops:
  1.9 4.1 %collective-permute-start.1 = (bf16[2,3,512]{2,0,1:T(2,128)(2,1)S(1)}, bf16[2,3,512]{2,0,1:T(2,128)(2,1)S(1)}, u32[]{:S(2)}, u32[]{:S(2)}) collective-permute-start(bf16[2,3,512]{2,0,1:T(2,128)(2,1)S(1)} %get-tuple-element.94), channel_id=1, source_target_pairs={{0,7},{1,0},{2,1},{3,2},{4,3},{5,4},{6,5},{7,6},{8,15},{9,8},{10,9... | collective-permute-start | bytes 18440 | tf_op jit(solution)/shard_map/ppermute | solution.py:42
  10.0 4.0 %collective-permute-start.2 = (bf16[1,96,512]{2,0,1:T(2,128)(2,1)}, bf16[1,96,512]{2,0,1:T(2,128)(2,1)S(1)}, u32[]{:S(2)}, u32[]{:S(2)}) collective-permute-start(bf16[1,96,512]{2,0,1:T(2,128)(2,1)} %get-tuple-element.92), channel_id=1, source_target_pairs={{0,8},{8,16},{16,24},{1,9},{9,17},{17,25},{2,10},{10,18},{18,26},{... | collective-permute-start | bytes 294920 | tf_op jit(solution)/shard_map/ppermute | solution.py:39
  18.3 3.4 %all-to-all-start.1 = ((bf16[8,96,132]{1,2,0:T(8,128)(2,1)}), bf16[8,96,132]{1,2,0:T(8,128)(2,1)S(1)}, u32[]{:S(2)}, u32[]{:S(2)}) async-start(bf16[8,96,132]{1,2,0:T(8,128)(2,1)} %copy.57), calls=%async_computation.1 | async-start | bytes 557056 | tf_op jit(solution)/shard_map/all_to_all | solution.py:53
  25.6 7.4 %forward.1 = (bf16[8,96,384]{2,1,0:T(8,128)(2,1)}, bf16[192,512]{1,0:T(8,128)(2,1)S(1)}) custom-call(bf16[384,512]{1,0:T(8,128)(2,1)S(1)} %bitcast.57, f32[1,512]{1,0:T(1,128)S(1)} %bitcast.70, bf16[512,2048]{1,0:T(8,128)(2,1)S(1)} %copy-done.1, f32[9,2048]{1,0:T(8,128)S(1)} %reshape.169.kernel_ref, bf16[2048,512]{1,0:T(8,128)(2,1)S(1)} %copy-done.3, ...), custom_call_target="tpu_custom_call" | custom-call | flops 1509949440 | bytes 5767168 | tf_op jit(solution)/shard_map/forward/pallas_call | solution.py:200
  34.4 5.0 %all-to-all-start = ((bf16[8,96,384]{2,1,0:T(8,128)(2,1)}), bf16[8,96,384]{2,1,0:T(8,128)(2,1)S(1)}, u32[]{:S(2)}, u32[]{:S(2)}) async-start(bf16[8,96,384]{2,1,0:T(8,128)(2,1)} %get-tuple-element.25), calls=%async_computation | async-start | bytes 1179648 | tf_op jit(solution)/shard_map/all_to_all | solution.py:53
  41.3 14.9 %all-to-all-done = bf16[8,96,384]{2,1,0:T(8,128)(2,1)S(1)} async-done(((bf16[8,96,384]{2,1,0:T(8,128)(2,1)}), bf16[8,96,384]{2,1,0:T(8,128)(2,1)S(1)}, u32[]{:S(2)}, u32[]{:S(2)}) %all-to-all-start) | async-done | bytes 589856 | tf_op jit(solution)/shard_map/all_to_all | solution.py:53
  57.2 17.8 %attention.1 = bf16[768,512]{1,0:T(8,128)(2,1)S(1)} custom-call(bf16[768,384]{1,0:T(8,128)(2,1)S(1)} %bitcast.64, bf16[768,132]{1,0:T(8,128)(2,1)S(1)} %bitcast.66), custom_call_target="tpu_custom_call" | custom-call | flops 1056964608 | bytes 1572864 | tf_op jit(solution)/shard_map/attention/pallas_call | solution.py:548
  75.9 3.5 %all-to-all-start.2 = ((bf16[8,96,512]{2,1,0:T(8,128)(2,1)}), bf16[8,96,512]{2,1,0:T(8,128)(2,1)S(1)}, u32[]{:S(2)}, u32[]{:S(2)}) async-start(bf16[8,96,512]{2,1,0:T(8,128)(2,1)} %bitcast.62), calls=%async_computation.2 | async-start | bytes 1572864 | tf_op jit(solution)/shard_map/all_to_all | solution.py:53
  80.7 5.3 %collective-permute-start.8 = (bf16[1,96,512]{2,0,1:T(2,128)(2,1)}, bf16[1,96,512]{2,0,1:T(2,128)(2,1)}, u32[]{:S(2)}, u32[]{:S(2)}) collective-permute-start(bf16[1,96,512]{2,0,1:T(2,128)(2,1)} %get-tuple-element.93), channel_id=1, source_target_pairs={{0,8},{8,16},{16,24},{1,9},{9,17},{17,25},{2,10},{10,18},{18,26},{... | collective-permute-start | bytes 294920 | tf_op jit(solution)/shard_map/ppermute | solution.py:617
  86.0 14.3 %all-to-all-done.2.attended_ref = bf16[8,96,512]{2,1,0:T(8,128)(2,1)S(1)} async-done(((bf16[8,96,512]{2,1,0:T(8,128)(2,1)}), bf16[8,96,512]{2,1,0:T(8,128)(2,1)S(1)}, u32[]{:S(2)}, u32[]{:S(2)}) %all-to-all-start.2) | async-done | bytes 786464 | tf_op jit(solution)/shard_map/all_to_all | solution.py:53
  112.6 7.3 %forward_around.1 = (bf16[384,2048]{1,0:T(8,128)(2,1)S(1)}, f32[384,2048]{1,0:T(8,128)S(1)}, bf16[192,2048]{1,0:T(8,128)(2,1)S(1)}, f32[192,2048]{1,0:T(8,128)S(1)}) custom-call(bf16[576,512]{1,0:T(8,128)(2,1)S(1)} %bitcast.65, f32[1,512]{1,0:T(1,128)S(1)} %bitcast.71, bf16[512,2048]{1,0:T(8,128)(2,1)S(1)} %copy-done.1, f32[9,2048]{1,0:T(8,128)S(1)} %reshape.169.kernel_ref), custom_call_target="tpu_custom_call" | custom-call | flops 1207959552 | bytes 13107200 | tf_op jit(solution)/shard_map/forward_around/pallas_call | solution.py:276
  128.2 3.9 %collective-permute-start.6 = (bf16[1,96,512]{2,1,0:T(8,128)(2,1)S(1)}, bf16[1,96,512]{2,1,0:T(8,128)(2,1)S(1)}, u32[]{:S(2)}, u32[]{:S(2)}) collective-permute-start(bf16[1,96,512]{2,1,0:T(8,128)(2,1)S(1)} %get-tuple-element.88), channel_id=1, source_target_pairs={{0,8},{8,16},{16,24},{1,9},{9,17},{17,25},{2,10},{10,18},{18,26},{... | collective-permute-start | bytes 294920 | tf_op jit(solution)/shard_map/ppermute | solution.py:39
  134.2 4.7 %collective-permute-done.7 = bf16[1,96,512]{2,1,0:T(8,128)(2,1)S(1)} collective-permute-done((bf16[1,96,512]{2,1,0:T(8,128)(2,1)S(1)}, bf16[1,96,512]{2,1,0:T(8,128)(2,1)S(1)}, u32[]{:S(2)}, u32[]{:S(2)}) %collective-permute-start.7) | collective-permute-done | bytes 98336 | tf_op jit(solution)/shard_map/ppermute | solution.py:42
  141.8 4.2 %all-to-all-start.7 = ((bf16[4,1024,128]{2,1,0:T(8,128)(2,1)}), bf16[4,1024,128]{2,1,0:T(8,128)(2,1)}, u32[]{:S(2)}, u32[]{:S(2)}) async-start(bf16[4,1024,128]{2,1,0:T(8,128)(2,1)} %bitcast.78), calls=%async_computation.7 | async-start | bytes 2097152 | tf_op jit(solution)/shard_map/all_to_all | solution.py:53
  153.9 10.1 %backward.1 = (bf16[4,8,128,256]{3,2,1,0:T(8,128)(2,1)S(1)}, f32[9,2048]{1,0:T(8,128)S(1)}, bf16[2,90,512]{2,1,0:T(8,128)(2,1)S(1)}, f32[1,512]{1,0:T(1,128)S(1)}) custom-call(bf16[384,512]{1,0:T(8,128)(2,1)S(1)} %bitcast.56, bf16[192,512]{1,0:T(8,128)(2,1)S(1)} %bitcast.63, f32[1,512]{1,0:T(1,128)S(1)} %bitcast.72, f32[192,1]{1,0:T(8,128)S(1)} %reshape.174.inside_ref, ...), custom_call_target="tpu_custom_call" | custom-call | flops 1610612736 | bytes 15728640 | tf_op jit(solution)/shard_map/backward/pallas_call | solution.py:427
  170.9 4.2 %all-to-all-start.5 = ((bf16[4,256,512]{2,1,0:T(8,128)(2,1)}), bf16[4,256,512]{2,1,0:T(8,128)(2,1)S(1)}, u32[]{:S(2)}, u32[]{:S(2)}) async-start(bf16[4,256,512]{2,1,0:T(8,128)(2,1)} %bitcast.79), calls=%async_computation.5 | async-start | bytes 2097152 | tf_op jit(solution)/shard_map/all_to_all | solution.py:53
  178.2 11.5 %all-to-all-done.5 = bf16[4,256,512]{2,1,0:T(8,128)(2,1)S(1)} async-done(((bf16[4,256,512]{2,1,0:T(8,128)(2,1)}), bf16[4,256,512]{2,1,0:T(8,128)(2,1)S(1)}, u32[]{:S(2)}, u32[]{:S(2)}) %all-to-all-start.5) | async-done | bytes 1048608 | tf_op jit(solution)/shard_map/all_to_all | solution.py:53
  189.7 3.5 %all-to-all-start.3 = ((bf16[4,588,256]{2,1,0:T(8,128)(2,1)}), bf16[4,588,256]{2,1,0:T(8,128)(2,1)S(1)}, u32[]{:S(2)}, u32[]{:S(2)}) async-start(bf16[4,588,256]{2,1,0:T(8,128)(2,1)} %pad_maximum_fusion), calls=%async_computation.3 | async-start | bytes 2424832 | tf_op jit(solution)/shard_map/all_to_all | solution.py:53
  195.4 13.1 %all-to-all-done.3 = bf16[4,588,256]{2,1,0:T(8,128)(2,1)S(1)} async-done(((bf16[4,588,256]{2,1,0:T(8,128)(2,1)}), bf16[4,588,256]{2,1,0:T(8,128)(2,1)S(1)}, u32[]{:S(2)}, u32[]{:S(2)}) %all-to-all-start.3) | async-done | bytes 1204256 | tf_op jit(solution)/shard_map/all_to_all | solution.py:53
  208.6 3.4 %all-to-all-start.8 = ((bf16[4,256,128]{2,1,0:T(8,128)(2,1)}), bf16[4,256,128]{2,1,0:T(8,128)(2,1)S(1)}, u32[]{:S(2)}, u32[]{:S(2)}) async-start(bf16[4,256,128]{2,1,0:T(8,128)(2,1)} %bitcast.28), calls=%async_computation.8 | async-start | bytes 524288 | tf_op jit(solution)/shard_map/all_to_all | solution.py:53
  212.9 7.4 %all-to-all-done.8 = bf16[4,256,128]{2,1,0:T(8,128)(2,1)S(1)} async-done(((bf16[4,256,128]{2,1,0:T(8,128)(2,1)}), bf16[4,256,128]{2,1,0:T(8,128)(2,1)S(1)}, u32[]{:S(2)}, u32[]{:S(2)}) %all-to-all-start.8) | async-done | bytes 262176 | tf_op jit(solution)/shard_map/all_to_all | solution.py:53
  226.6 4.0 %all-to-all-done.6 = bf16[4,64,512]{2,1,0:T(8,128)(2,1)S(1)} async-done(((bf16[4,64,512]{2,1,0:T(8,128)(2,1)}), bf16[4,64,512]{2,1,0:T(8,128)(2,1)S(1)}, u32[]{:S(2)}, u32[]{:S(2)}) %all-to-all-start.6) | async-done | bytes 262176 | tf_op jit(solution)/shard_map/all_to_all | solution.py:53
  230.6 3.5 %all-to-all-start.4 = ((bf16[4,204,256]{2,1,0:T(8,128)(2,1)}), bf16[4,204,256]{2,1,0:T(8,128)(2,1)S(1)}, u32[]{:S(2)}, u32[]{:S(2)}) async-start(bf16[4,204,256]{2,1,0:T(8,128)(2,1)} %pad_maximum_fusion.1), calls=%async_computation.4 | async-start | bytes 851968 | tf_op jit(solution)/shard_map/all_to_all | solution.py:53
  236.0 7.6 %all-to-all-done.4 = bf16[4,204,256]{2,1,0:T(8,128)(2,1)S(1)} async-done(((bf16[4,204,256]{2,1,0:T(8,128)(2,1)}), bf16[4,204,256]{2,1,0:T(8,128)(2,1)S(1)}, u32[]{:S(2)}, u32[]{:S(2)}) %all-to-all-start.4) | async-done | bytes 417824 | tf_op jit(solution)/shard_map/all_to_all | solution.py:53
  (157 shorter events, 76.9 us)
Async XLA Ops:
  1.4 6.4 %collective-permute-start = (bf16[2,3,512]{2,0,1:T(2,128)(2,1)S(1)}, bf16[2,3,512]{2,0,1:T(2,128)(2,1)S(1)}, u32[]{:S(2)}, u32[]{:S(2)}) collective-permute-start(bf16[2,3,512]{2,0,1:T(2,128)(2,1)S(1)} %get-tuple-element.95), channel_id=1, source_target_pairs={{0,1},{1,2},{2,3},{3,4},{4,5},{5,6},{6,7},{7,0},{8,9},{9,10},{10,1... | collective-permute-start | bytes 18440 | tf_op jit(solution)/shard_map/ppermute | solution.py:39
  1.9 7.0 %collective-permute-start.1 = (bf16[2,3,512]{2,0,1:T(2,128)(2,1)S(1)}, bf16[2,3,512]{2,0,1:T(2,128)(2,1)S(1)}, u32[]{:S(2)}, u32[]{:S(2)}) collective-permute-start(bf16[2,3,512]{2,0,1:T(2,128)(2,1)S(1)} %get-tuple-element.94), channel_id=1, source_target_pairs={{0,7},{1,0},{2,1},{3,2},{4,3},{5,4},{6,5},{7,6},{8,15},{9,8},{10,9... | collective-permute-start | bytes 18440 | tf_op jit(solution)/shard_map/ppermute | solution.py:42
  10.0 11.9 %collective-permute-start.2 = (bf16[1,96,512]{2,0,1:T(2,128)(2,1)}, bf16[1,96,512]{2,0,1:T(2,128)(2,1)S(1)}, u32[]{:S(2)}, u32[]{:S(2)}) collective-permute-start(bf16[1,96,512]{2,0,1:T(2,128)(2,1)} %get-tuple-element.92), channel_id=1, source_target_pairs={{0,8},{8,16},{16,24},{1,9},{9,17},{17,25},{2,10},{10,18},{18,26},{... | collective-permute-start | bytes 294920 | tf_op jit(solution)/shard_map/ppermute | solution.py:39
  13.9 9.3 %collective-permute-start.3 = (bf16[1,96,512]{2,0,1:T(2,128)(2,1)}, bf16[1,96,512]{2,0,1:T(2,128)(2,1)S(1)}, u32[]{:S(2)}, u32[]{:S(2)}) collective-permute-start(bf16[1,96,512]{2,0,1:T(2,128)(2,1)} %get-tuple-element.93), channel_id=1, source_target_pairs={{8,0},{16,8},{24,16},{9,1},{17,9},{25,17},{10,2},{18,10},{26,18},{... | collective-permute-start | bytes 294920 | tf_op jit(solution)/shard_map/ppermute | solution.py:42
  18.3 15.4 %all-to-all-start.1 = ((bf16[8,96,132]{1,2,0:T(8,128)(2,1)}), bf16[8,96,132]{1,2,0:T(8,128)(2,1)S(1)}, u32[]{:S(2)}, u32[]{:S(2)}) async-start(bf16[8,96,132]{1,2,0:T(8,128)(2,1)} %copy.57), calls=%async_computation.1 | async-start | bytes 557056 | tf_op jit(solution)/shard_map/all_to_all | solution.py:53
  34.4 21.8 %all-to-all-start = ((bf16[8,96,384]{2,1,0:T(8,128)(2,1)}), bf16[8,96,384]{2,1,0:T(8,128)(2,1)S(1)}, u32[]{:S(2)}, u32[]{:S(2)}) async-start(bf16[8,96,384]{2,1,0:T(8,128)(2,1)} %get-tuple-element.25), calls=%async_computation | async-start | bytes 1179648 | tf_op jit(solution)/shard_map/all_to_all | solution.py:53
  57.2 43.1 %copy-start.11 = (bf16[512,512]{1,0:T(8,128)(2,1)S(1)}, bf16[512,512]{1,0:T(8,128)(2,1)}, u32[]{:S(2)}) copy-start(bf16[512,512]{1,0:T(8,128)(2,1)} %out_weight_ref.3) | copy-start | bytes 1572868
  75.9 24.4 %all-to-all-start.2 = ((bf16[8,96,512]{2,1,0:T(8,128)(2,1)}), bf16[8,96,512]{2,1,0:T(8,128)(2,1)S(1)}, u32[]{:S(2)}, u32[]{:S(2)}) async-start(bf16[8,96,512]{2,1,0:T(8,128)(2,1)} %bitcast.62), calls=%async_computation.2 | async-start | bytes 1572864 | tf_op jit(solution)/shard_map/all_to_all | solution.py:53
  79.4 29.6 %collective-permute-start.9 = (bf16[1,96,512]{2,0,1:T(2,128)(2,1)}, bf16[1,96,512]{2,0,1:T(2,128)(2,1)}, u32[]{:S(2)}, u32[]{:S(2)}) collective-permute-start(bf16[1,96,512]{2,0,1:T(2,128)(2,1)} %get-tuple-element.92), channel_id=1, source_target_pairs={{8,0},{16,8},{24,16},{9,1},{17,9},{25,17},{10,2},{18,10},{26,18},{... | collective-permute-start | bytes 294920 | tf_op jit(solution)/shard_map/ppermute | solution.py:618
  80.7 28.3 %collective-permute-start.8 = (bf16[1,96,512]{2,0,1:T(2,128)(2,1)}, bf16[1,96,512]{2,0,1:T(2,128)(2,1)}, u32[]{:S(2)}, u32[]{:S(2)}) collective-permute-start(bf16[1,96,512]{2,0,1:T(2,128)(2,1)} %get-tuple-element.93), channel_id=1, source_target_pairs={{0,8},{8,16},{16,24},{1,9},{9,17},{17,25},{2,10},{10,18},{18,26},{... | collective-permute-start | bytes 294920 | tf_op jit(solution)/shard_map/ppermute | solution.py:617
  109.0 30.0 %collective-permute-start.13 = (bf16[4,4,256,128]{3,2,1,0:T(8,128)(2,1)}, bf16[4,4,256,128]{3,2,1,0:T(8,128)(2,1)}, u32[]{:S(2)}, u32[]{:S(2)}) collective-permute-start(bf16[4,4,256,128]{3,2,1,0:T(8,128)(2,1)} %dynamic-slice_bitcast_fusion), channel_id=1, source_target_pairs={{0,1},{1,0},{2,3},{3,2},{4,5},{5,4},{6,7},{7,6},{8,9},{9,8},{10,11... | collective-permute-start | bytes 3145736 | tf_op jit(solution)/shard_map/ppermute | solution.py:49
  121.5 4.3 %collective-permute-start.5 = (bf16[2,1,512]{2,1,0:T(2,128)(2,1)S(1)}, bf16[2,1,512]{2,1,0:T(2,128)(2,1)S(1)}, u32[]{:S(2)}, u32[]{:S(2)}) collective-permute-start(bf16[2,1,512]{2,1,0:T(2,128)(2,1)S(1)} %get-tuple-element.90), channel_id=1, source_target_pairs={{0,7},{1,0},{2,1},{3,2},{4,3},{5,4},{6,5},{7,6},{8,15},{9,8},{10,9... | collective-permute-start | bytes 6152 | tf_op jit(solution)/shard_map/ppermute | solution.py:42
  122.9 4.8 %collective-permute-start.4 = (bf16[2,1,512]{2,1,0:T(2,128)(2,1)S(1)}, bf16[2,1,512]{2,1,0:T(2,128)(2,1)S(1)}, u32[]{:S(2)}, u32[]{:S(2)}) collective-permute-start(bf16[2,1,512]{2,1,0:T(2,128)(2,1)S(1)} %get-tuple-element.91), channel_id=1, source_target_pairs={{0,1},{1,2},{2,3},{3,4},{4,5},{5,6},{6,7},{7,0},{8,9},{9,10},{10,1... | collective-permute-start | bytes 6152 | tf_op jit(solution)/shard_map/ppermute | solution.py:39
  124.9 43.4 %collective-permute-start.12 = (bf16[4,4,64,512]{3,2,1,0:T(8,128)(2,1)}, bf16[4,4,64,512]{3,2,1,0:T(8,128)(2,1)}, u32[]{:S(2)}, u32[]{:S(2)}) collective-permute-start(bf16[4,4,64,512]{3,2,1,0:T(8,128)(2,1)} %dynamic-slice_bitcast_fusion.1), channel_id=1, source_target_pairs={{0,1},{1,0},{2,3},{3,2},{4,5},{5,4},{6,7},{7,6},{8,9},{9,8},{10,11... | collective-permute-start | bytes 3145736 | tf_op jit(solution)/shard_map/ppermute | solution.py:49
  128.2 6.1 %collective-permute-start.6 = (bf16[1,96,512]{2,1,0:T(8,128)(2,1)S(1)}, bf16[1,96,512]{2,1,0:T(8,128)(2,1)S(1)}, u32[]{:S(2)}, u32[]{:S(2)}) collective-permute-start(bf16[1,96,512]{2,1,0:T(8,128)(2,1)S(1)} %get-tuple-element.88), channel_id=1, source_target_pairs={{0,8},{8,16},{16,24},{1,9},{9,17},{17,25},{2,10},{10,18},{18,26},{... | collective-permute-start | bytes 294920 | tf_op jit(solution)/shard_map/ppermute | solution.py:39
  132.1 6.9 %collective-permute-start.7 = (bf16[1,96,512]{2,1,0:T(8,128)(2,1)S(1)}, bf16[1,96,512]{2,1,0:T(8,128)(2,1)S(1)}, u32[]{:S(2)}, u32[]{:S(2)}) collective-permute-start(bf16[1,96,512]{2,1,0:T(8,128)(2,1)S(1)} %get-tuple-element.89), channel_id=1, source_target_pairs={{8,0},{16,8},{24,16},{9,1},{17,9},{25,17},{10,2},{18,10},{26,18},{... | collective-permute-start | bytes 294920 | tf_op jit(solution)/shard_map/ppermute | solution.py:42
  141.8 29.1 %all-to-all-start.7 = ((bf16[4,1024,128]{2,1,0:T(8,128)(2,1)}), bf16[4,1024,128]{2,1,0:T(8,128)(2,1)}, u32[]{:S(2)}, u32[]{:S(2)}) async-start(bf16[4,1024,128]{2,1,0:T(8,128)(2,1)} %bitcast.78), calls=%async_computation.7 | async-start | bytes 2097152 | tf_op jit(solution)/shard_map/all_to_all | solution.py:53
  167.8 7.3 %collective-permute-start.10 = (bf16[4,4,128,256]{3,2,1,0:T(8,128)(2,1)}, bf16[4,4,128,256]{3,2,1,0:T(8,128)(2,1)}, u32[]{:S(2)}, u32[]{:S(2)}) collective-permute-start(bf16[4,4,128,256]{3,2,1,0:T(8,128)(2,1)} %dynamic-slice_bitcast_fusion.2), channel_id=1, source_target_pairs={{0,1},{1,0},{2,3},{3,2},{4,5},{5,4},{6,7},{7,6},{8,9},{9,8},{10,11... | collective-permute-start | bytes 3145736 | tf_op jit(solution)/shard_map/ppermute | solution.py:49
  167.8 7.3 %collective-permute-start.11 = (f32[19456]{0:T(1024)S(1)}, f32[19456]{0:T(1024)S(1)}, u32[]{:S(2)}, u32[]{:S(2)}) collective-permute-start(f32[19456]{0:T(1024)S(1)} %pad_maximum_fusion.4), channel_id=1, source_target_pairs={{0,1},{1,0},{2,3},{3,2},{4,5},{5,4},{6,7},{7,6},{8,9},{9,8},{10,11... | collective-permute-start | bytes 233480 | tf_op jit(solution)/shard_map/ppermute | solution.py:49
  170.9 18.8 %all-to-all-start.5 = ((bf16[4,256,512]{2,1,0:T(8,128)(2,1)}), bf16[4,256,512]{2,1,0:T(8,128)(2,1)S(1)}, u32[]{:S(2)}, u32[]{:S(2)}) async-start(bf16[4,256,512]{2,1,0:T(8,128)(2,1)} %bitcast.79), calls=%async_computation.5 | async-start | bytes 2097152 | tf_op jit(solution)/shard_map/all_to_all | solution.py:53
  189.7 18.9 %all-to-all-start.3 = ((bf16[4,588,256]{2,1,0:T(8,128)(2,1)}), bf16[4,588,256]{2,1,0:T(8,128)(2,1)S(1)}, u32[]{:S(2)}, u32[]{:S(2)}) async-start(bf16[4,588,256]{2,1,0:T(8,128)(2,1)} %pad_maximum_fusion), calls=%async_computation.3 | async-start | bytes 2424832 | tf_op jit(solution)/shard_map/all_to_all | solution.py:53
  208.6 11.7 %all-to-all-start.8 = ((bf16[4,256,128]{2,1,0:T(8,128)(2,1)}), bf16[4,256,128]{2,1,0:T(8,128)(2,1)S(1)}, u32[]{:S(2)}, u32[]{:S(2)}) async-start(bf16[4,256,128]{2,1,0:T(8,128)(2,1)} %bitcast.28), calls=%async_computation.8 | async-start | bytes 524288 | tf_op jit(solution)/shard_map/all_to_all | solution.py:53
  220.3 10.3 %all-to-all-start.6 = ((bf16[4,64,512]{2,1,0:T(8,128)(2,1)}), bf16[4,64,512]{2,1,0:T(8,128)(2,1)S(1)}, u32[]{:S(2)}, u32[]{:S(2)}) async-start(bf16[4,64,512]{2,1,0:T(8,128)(2,1)} %bitcast.22), calls=%async_computation.6 | async-start | bytes 524288 | tf_op jit(solution)/shard_map/all_to_all | solution.py:53
  230.6 13.1 %all-to-all-start.4 = ((bf16[4,204,256]{2,1,0:T(8,128)(2,1)}), bf16[4,204,256]{2,1,0:T(8,128)(2,1)S(1)}, u32[]{:S(2)}, u32[]{:S(2)}) async-start(bf16[4,204,256]{2,1,0:T(8,128)(2,1)} %pad_maximum_fusion.1), calls=%async_computation.4 | async-start | bytes 851968 | tf_op jit(solution)/shard_map/all_to_all | solution.py:53
  (35 other events, 185.4 us)

commit v3 on v2

v3 whole, which is shorter than its diff:
```python
import functools
import math

import jax
import jax.numpy as jnp
from jax import lax
from jax.experimental import pallas as pl
from jax.experimental.pallas import tpu as pltpu
from jax.sharding import Mesh
from jax.sharding import PartitionSpec as P

EPSILON = 1e-06
LON = ("z", "core")
BF16 = jnp.bfloat16
F32 = jnp.float32
MASKED = -1e30
SIDE = 3
BIAS_ROWS = 16
LOG2E = math.log2(math.e)


def inverse_rms(values):
    return lax.rsqrt(jnp.mean(values * values, axis=-1, keepdims=True) + EPSILON)


def norm_back(back_normed, state, inverse, gain):
    scaled = back_normed * gain
    return inverse * scaled - inverse * inverse * inverse * state * jnp.mean(
        scaled * state, axis=-1, keepdims=True
    )


def shifts(count, step, periodic):
    return [(i, (i + step) % count) for i in range(count) if periodic or 0 <= i + step < count]


def from_sides(block, width, dim, axis, periodic):
    count = lax.axis_size(axis)
    size = block.shape[dim]
    low = lax.ppermute(
        lax.slice_in_dim(block, size - width, size, axis=dim), axis, shifts(count, 1, periodic)
    )
    high = lax.ppermute(
        lax.slice_in_dim(block, 0, width, axis=dim), axis, shifts(count, -1, periodic)
    )
    return low, high


def core_swap(values):
    return lax.ppermute(values, "core", [(0, 1), (1, 0)])


def exchange(values, axis):
    return lax.all_to_all(values, axis, 0, 0, tiled=True)


def matmul(left, right):
    return jnp.dot(left, right, preferred_element_type=F32)


def cross_cells(left, right):
    return lax.dot_general(left, right, (((0,), (0,)), ((), ())), preferred_element_type=F32)


def times_transpose(values, weights):
    return lax.dot_general(
        values, weights, (((values.ndim - 1,), (1,)), ((), ())), preferred_element_type=F32
    )


def sigmoid(values):
    return 0.5 + 0.5 * jnp.tanh(0.5 * values)


def silu(values):
    return values * sigmoid(values)


def silu_slope(values):
    gate = sigmoid(values)
    return gate * (1.0 + values * (1.0 - gate))


def call(kernel, name, out_shape, *operands, scratch=(), megabytes=16, flops=0, specs=None):
    return pl.pallas_call(
        kernel,
        out_shape=out_shape,
        scratch_shapes=scratch,
        in_specs=specs or [pl.BlockSpec(memory_space=pltpu.VMEM)] * len(operands),
        compiler_params=pltpu.CompilerParams(vmem_limit_bytes=megabytes * 1024 * 1024),
        cost_estimate=pl.CostEstimate(
            flops=flops,
            bytes_accessed=sum(x.size * x.dtype.itemsize for x in operands),
            transcendentals=0,
        ),
        name=name,
    )(*operands)


def early_kernel(
    groups, cot_ref, bias_ref, out_weight_ref, order_ref, early_ref, framed_ref, bias_frame
):
    row_count, lon_count, channels = cot_ref.shape
    frame = framed_ref.shape[1]
    width = channels // groups
    head_count = bias_ref.shape[2]
    items = head_count // groups
    in_rows = early_ref.shape[2] == width
    framed_ref[...] = jnp.zeros_like(framed_ref)
    bias_frame[...] = jnp.full_like(bias_frame, MASKED)
    for row in range(row_count):
        framed_ref[row, SIDE : SIDE + lon_count, :] = cot_ref[row]
        bias_frame[row, SIDE : SIDE + lon_count, 0:head_count] = bias_ref[row].astype(F32)
    for row in range(row_count):
        back_heads = times_transpose(framed_ref[row], out_weight_ref[...]).astype(BF16)
        bias = bias_frame[row].T if in_rows else bias_frame[row]
        for group in range(groups):
            target = row * groups + group
            early_ref[target, 0:frame, 0:width] = back_heads[:, group * width : (group + 1) * width]
            if in_rows:
                early_ref[target, frame:, :] = bias[
                    group * items : group * items + BIAS_ROWS
                ].astype(BF16)
            else:
                early_ref[target, :, width:] = bias[
                    0:frame, group * items : (group + 1) * items
                ].astype(BF16)


def early_parts(cotangent, key_bias, attention_out, order, groups):
    row_count, lon_count, channels = cotangent.shape
    frame = lon_count + 2 * SIDE
    head_count = key_bias.shape[2]
    width = channels // groups
    if frame <= width and width % 128 == 0:
        shape = (row_count * groups, frame + BIAS_ROWS, width)
        bias_shape = (row_count, width, max(128, head_count + BIAS_ROWS))
    else:
        shape = (row_count * groups, frame, width + head_count // groups)
        bias_shape = (row_count, frame, head_count)
    return call(
        functools.partial(early_kernel, groups),
        "back_heads",
        (
            jax.ShapeDtypeStruct(shape, BF16),
            jax.ShapeDtypeStruct((row_count, frame, channels), BF16),
        ),
        cotangent,
        key_bias,
        attention_out,
        order,
        scratch=[pltpu.VMEM(bias_shape, F32)],
        flops=2 * row_count * frame * channels * channels,
    )


def normalise(values, gain):
    return (values * inverse_rms(values) * gain).astype(BF16)


def convolve(values, kernel, rows, frame):
    size = rows * frame
    total = None
    for b in range(3):
        part = kernel[b : b + 1] * values[0:size]
        for a in range(1, 3):
            part = part + kernel[3 * a + b : 3 * a + b + 1] * values[a * frame : a * frame + size]
        if b != 1:
            part = pltpu.roll(part, 1 if b == 0 else size - 1, 0)
        total = part if total is None else total + part
    return total


def forward_kernel(
    frame, groups, state_ref, gain_ref, expand_ref, kernel_ref, shrink_ref, second_gain_ref, in_ref,
    qkv_ref, inner_ref, normed, total,
):
    step = pl.program_id(0)
    cells, channels = inner_ref.shape
    rows = cells // frame
    width = channels // groups

    @pl.when(step == 0)
    def _():
        near = state_ref[frame : frame + normed.shape[0], :].astype(F32)
        normed[...] = normalise(near, gain_ref[...])
        total[...] = jnp.zeros_like(total)

    activated = silu(matmul(normed[...], expand_ref[...])).astype(BF16).astype(F32)
    mixed = silu(convolve(activated, kernel_ref[...], rows, frame)).astype(BF16)
    total[...] += matmul(mixed, shrink_ref[...])

    @pl.when(step == pl.num_programs(0) - 1)
    def _():
        inner = state_ref[2 * frame : 2 * frame + cells, :].astype(F32)
        inner = (inner + total[...]).astype(BF16)
        inner_ref[...] = inner
        normed_second = normalise(inner.astype(F32), second_gain_ref[...])
        projected = matmul(normed_second, in_ref[...]).astype(BF16)
        for row in range(rows):
            for group in range(groups):
                for kind in range(3):
                    start = kind * channels + group * width
                    qkv_ref[row * groups + group, :, kind * width : (kind + 1) * width] = projected[
                        row * frame : (row + 1) * frame, start : start + width
                    ]


def step_width(wide):
    return 256 if wide % 256 == 0 else wide


def forward(state, input_gain, expand_weight, kernel, shrink_weight, gain, attention_in, groups):
    all_rows, frame, channels = state.shape
    rows = all_rows - 4
    cells = rows * frame
    wide = expand_weight.shape[1]
    part = step_width(wide)
    fixed = lambda shape: pl.BlockSpec(shape, lambda step: (0,) * len(shape))
    return pl.pallas_call(
        functools.partial(forward_kernel, frame, groups),
        grid=(wide // part,),
        out_shape=(
            jax.ShapeDtypeStruct((rows * groups, frame, 3 * channels // groups), BF16),
            jax.ShapeDtypeStruct((cells, channels), BF16),
        ),
        in_specs=[
            fixed((all_rows * frame, channels)),
            fixed((1, channels)),
            pl.BlockSpec((channels, part), lambda step: (0, step)),
            pl.BlockSpec((9, part), lambda step: (0, step)),
            pl.BlockSpec((part, channels), lambda step: (step, 0)),
            fixed((1, channels)),
            fixed(attention_in.shape),
        ],
        out_specs=(
            fixed((rows * groups, frame, 3 * channels // groups)),
            fixed((cells, channels)),
        ),
        scratch_shapes=[
            pltpu.VMEM((cells + 2 * frame, channels), BF16),
            pltpu.VMEM((cells, channels), F32),
        ],
        compiler_params=pltpu.CompilerParams(
            vmem_limit_bytes=16 * 1024 * 1024, dimension_semantics=("arbitrary",)
        ),
        cost_estimate=pl.CostEstimate(
            flops=2 * cells * channels * (3 * wide + 3 * channels),
            bytes_accessed=4 * channels * wide + 6 * channels * channels,
            transcendentals=3 * cells * wide,
        ),
        name="forward",
    )(
        state.reshape(all_rows * frame, channels),
        input_gain,
        expand_weight,
        kernel,
        shrink_weight,
        gain,
        attention_in,
    )


def around_kernel(
    frame, state_ref, gain_ref, expand_ref, kernel_ref, order_ref, activated_ref, slope_ref, mixed_ref,
    expand_slope_ref, normed,
):
    size = activated_ref.shape[1]
    cells = mixed_ref.shape[1]

    @pl.when(pl.program_id(0) == 0)
    def _():
        normed[...] = normalise(state_ref[...].astype(F32), gain_ref[...])

    expanded = matmul(normed[...], expand_ref[...])
    gate = sigmoid(expanded)
    activated = (expanded * gate).astype(BF16)
    activated_ref[0] = activated[frame : frame + size]
    own_gate, own = gate[2 * frame : 2 * frame + cells], expanded[2 * frame : 2 * frame + cells]
    expand_slope_ref[0] = (own_gate * (1.0 + own * (1.0 - own_gate))).astype(BF16)
    convolved = convolve(activated.astype(F32), kernel_ref[...], size // frame, frame)
    gate = sigmoid(convolved)
    slope_ref[0] = (gate * (1.0 + convolved * (1.0 - gate))).astype(BF16)
    mixed_ref[0] = (
        convolved[frame : frame + cells] * gate[frame : frame + cells]
    ).astype(BF16)


def around(state, input_gain, expand_weight, kernel, order):
    all_rows, frame, channels = state.shape
    size, cells = (all_rows - 2) * frame, (all_rows - 4) * frame
    wide = expand_weight.shape[1]
    part = step_width(wide)
    fixed = lambda shape: pl.BlockSpec(shape, lambda step: (0,) * len(shape))
    moving = lambda rows: pl.BlockSpec((rows, part), lambda step: (0, step))
    block = lambda rows: pl.BlockSpec((1, rows, part), lambda step: (step, 0, 0))
    steps = wide // part
    return pl.pallas_call(
        functools.partial(around_kernel, frame),
        grid=(steps,),
        out_shape=(
            jax.ShapeDtypeStruct((steps, size, part), BF16),
            jax.ShapeDtypeStruct((steps, size, part), BF16),
            jax.ShapeDtypeStruct((steps, cells, part), BF16),
            jax.ShapeDtypeStruct((steps, cells, part), BF16),
        ),
        in_specs=[
            fixed((all_rows * frame, channels)),
            fixed((1, channels)),
            moving(channels),
            moving(9),
            pl.BlockSpec(memory_space=pl.ANY),
        ],
        out_specs=(block(size), block(size), block(cells), block(cells)),
        scratch_shapes=[pltpu.VMEM((all_rows * frame, channels), BF16)],
        compiler_params=pltpu.CompilerParams(
            vmem_limit_bytes=16 * 1024 * 1024, dimension_semantics=("arbitrary",)
        ),
        cost_estimate=pl.CostEstimate(
            flops=2 * all_rows * frame * channels * wide,
            bytes_accessed=2 * channels * wide + 14 * size * wide,
            transcendentals=2 * size * wide,
        ),
        name="forward_around",
    )(state.reshape(all_rows * frame, channels), input_gain, expand_weight, kernel, order)


def inner_kernel(
    groups, norm_factor, attended_ref, inner_ref, cot_ref, out_weight_ref, in_weight_ref, gain_ref,
    output_ref, back_inner_ref, unpacked_ref, gain_grad_ref,
):
    targets, frame, width = attended_ref.shape
    width = width // 4
    row_count, lon_count, channels = output_ref.shape
    for target in range(targets):
        row, group = divmod(target, groups)
        for kind in range(4):
            start = kind * channels + group * width
            unpacked_ref[row * frame : (row + 1) * frame, start : start + width] = attended_ref[
                target, :, kind * width : (kind + 1) * width
            ]
    inner = inner_ref[...].astype(F32)
    output = (inner + matmul(unpacked_ref[:, :channels], out_weight_ref[...])).astype(BF16)
    for row in range(row_count):
        start = row * frame + SIDE
        output_ref[row] = output[start : start + lon_count]
    back_second = times_transpose(unpacked_ref[:, channels:], in_weight_ref[...])
    inverse = inverse_rms(inner)
    gain_grad_ref[...] = norm_factor * jnp.sum(back_second * inner * inverse, axis=0, keepdims=True)
    back_inner_ref[...] = (
        cot_ref[...].astype(F32) + norm_back(back_second, inner, inverse, gain_ref[...])
    ).astype(BF16)


def weight_grads_kernel(
    norm_factor, z_size, which_ref, unpacked_ref, inner_ref, gain_ref, cot_ref, back_inner_ref,
    mixed_ref, order_ref, *refs
):
    added_ref = refs[0] if len(refs) == 8 else None
    out_ref, whole_in, whole_out, whole_back, in_t, out_t, back_t = refs[-7:]
    lat_size, _, lane = out_ref.shape
    channels = inner_ref.shape[1]
    blocks, _, part = mixed_ref.shape
    blocks = blocks // lat_size
    in_split, out_split = in_t.shape[0] // z_size, out_t.shape[0] // z_size
    first_rows = out_ref.shape[1] // z_size
    normed_second = normalise(inner_ref[...].astype(F32), gain_ref[...])
    whole_in[...] = unpacked_ref[:, channels:].T
    whole_out[...] = cot_ref[...].T
    whole_back[...] = back_inner_ref[...].T
    for z in range(z_size):
        lon = 2 * z + which_ref[0]
        for source, target, split in (
            (whole_in, in_t, in_split),
            (whole_out, out_t, out_split),
            (whole_back, back_t, out_split),
        ):
            target[z * split : (z + 1) * split, :] = source[
                pl.ds(pl.multiple_of(lon * split, split), split), :
            ]

    def put(lat, start, split, values):
        values = values * norm_factor
        for z in range(z_size):
            rows = slice(z * first_rows + start, z * first_rows + start + split)
            value = values[z * split : (z + 1) * split]
            if added_ref is not None:
                value = value + added_ref[lat, rows, :].astype(F32)
            out_ref[lat, rows, :] = value.astype(BF16)

    for lat in range(lat_size):
        cols = slice(lat * lane, (lat + 1) * lane)
        put(lat, 0, in_split, matmul(in_t[...], normed_second[:, cols]))
        put(lat, in_split, out_split, matmul(out_t[...], unpacked_ref[:, cols]))
        start = in_split + out_split
        for block in range(blocks):
            values = matmul(back_t[...], mixed_ref[lat * blocks + block])
            for piece in range(part // lane):
                put(lat, start, out_split, values[:, piece * lane : (piece + 1) * lane])
                start += out_split


def weight_grads(
    which, unpacked, inner, gain, cot, back_inner, mixed, order, added, norm_factor, lat_size, z_size
):
    own, channels = inner.shape
    lane = channels // lat_size
    wide = mixed.shape[0] * mixed.shape[2]
    rows = 2 * channels + channels // 2 * (wide // channels)
    operands = (unpacked, inner, gain, cot, back_inner, mixed, order)
    if added is not None:
        operands += (added,)
    in_specs = [pl.BlockSpec(memory_space=pltpu.VMEM)] * len(operands)
    in_specs[6] = pl.BlockSpec(memory_space=pl.ANY)
    tall, short = pltpu.VMEM((3 * channels, own), BF16), pltpu.VMEM((channels, own), BF16)
    return pl.pallas_call(
        functools.partial(weight_grads_kernel, norm_factor, z_size),
        out_shape=jax.ShapeDtypeStruct((lat_size, rows, lane), BF16),
        in_specs=[pl.BlockSpec(memory_space=pltpu.SMEM)] + in_specs,
        scratch_shapes=[
            tall,
            short,
            short,
            pltpu.VMEM((3 * channels // 2, own), BF16),
            pltpu.VMEM((channels // 2, own), BF16),
            pltpu.VMEM((channels // 2, own), BF16),
        ],
        compiler_params=pltpu.CompilerParams(vmem_limit_bytes=20 * 1024 * 1024),
        cost_estimate=pl.CostEstimate(
            flops=own * channels * (4 * channels + wide),
            bytes_accessed=2 * channels * (8 * channels + 2 * wide),
            transcendentals=0,
        ),
        name="weight_grads",
    )(which.reshape(1), *operands)


def sum_kernel(parts_ref, out_ref):
    out_ref[...] = summed(parts_ref, slice(None)).astype(BF16)


def sum_parts(parts, steps):
    count, rows, lane = parts.shape
    block = rows // steps
    return pl.pallas_call(
        sum_kernel,
        grid=(steps,),
        out_shape=jax.ShapeDtypeStruct((rows, lane), BF16),
        in_specs=[pl.BlockSpec((count, block, lane), lambda step: (0, step, 0))],
        out_specs=pl.BlockSpec((block, lane), lambda step: (step, 0)),
        name="sum_bands",
    )(parts)


def pack_kernel(
    left_ref, right_ref, mine_ref, theirs_ref, first_gain_ref, second_gain_ref, out_ref
):
    rows, lane = left_ref.shape[1:]
    out_ref[:, 0:rows, :] = (left_ref[...].astype(F32) + right_ref[...].astype(F32)).astype(BF16)
    small = []
    for ref in (mine_ref, theirs_ref):
        for z in range(ref.shape[0]):
            for start in range(0, ref.shape[2], lane):
                small.append(ref[z, :, start : start + lane])
    for ref in (first_gain_ref, second_gain_ref):
        for start in range(0, ref.shape[1], lane):
            small.append(ref[:, start : start + lane])
    small = jnp.concatenate(small, axis=0).astype(BF16)
    for lat in range(out_ref.shape[0]):
        out_ref[lat, rows:, :] = small


def summed(ref, rows):
    total = ref[0, rows, :].astype(F32)
    for part in range(1, ref.shape[0]):
        total = total + ref[part, rows, :].astype(F32)
    return total


def merge_kernel(parts_ref, output_ref, input_ref, out_ref):
    z_size, out_rows, _ = out_ref.shape
    rows = parts_ref.shape[1]
    block = (rows - out_rows) // (z_size - 1)
    small = summed(parts_ref, slice(z_size * block, rows)).astype(BF16)
    for z in range(z_size):
        out_ref[z, 0:block, :] = summed(parts_ref, slice(z * block, (z + 1) * block)).astype(BF16)
        out_ref[z, block:, :] = small


def first_kernel(parts_ref, shrink_ref, in_ref, out_ref):
    lane = parts_ref.shape[1]
    in_split, out_split = in_ref.shape[0], out_ref.shape[0]
    at = in_split + out_split
    in_ref[...] = parts_ref[0:in_split, :].astype(F32)
    out_ref[...] = parts_ref[in_split:at, :].astype(F32)
    for piece in range(shrink_ref.shape[1] // lane):
        shrink_ref[:, piece * lane : (piece + 1) * lane] = parts_ref[at : at + out_split, :].astype(
            F32
        )
        at += out_split


def second_kernel(parts_ref, expand_ref, small_ref):
    block, split = expand_ref.shape
    lane = parts_ref.shape[2]
    at = 0
    for piece in range(split // lane):
        expand_ref[:, piece * lane : (piece + 1) * lane] = summed(parts_ref, slice(at, at + block))
        at += block
    small_ref[...] = summed(parts_ref, slice(at, parts_ref.shape[1]))


def small_kernel(
    split, core_ref, mine_ref, theirs_ref, depth_ref, first_gain_ref, second_gain_ref
):
    lane = mine_ref.shape[1]
    wide = depth_ref.shape[2]
    channels = first_gain_ref.shape[1]
    half_rows = 9 * wide // 2 // lane
    core = core_ref[0]
    pieces = wide // lane
    in_block = split // lane
    for side in range(2):
        which = core if side == 0 else 1 - core
        for piece in range(pieces // 2):
            own_at = side * half_rows + piece * 9
            other_at = (1 - side) * half_rows + piece * 9
            block = mine_ref[own_at : own_at + 9, :] + theirs_ref[other_at : other_at + 9, :]
            z, rest = divmod(piece, in_block)
            start = pl.multiple_of((2 * z + which) * split, lane) + rest * lane
            for a in range(3):
                depth_ref[a, :, pl.ds(pl.multiple_of(start, lane), lane)] = block[3 * a : 3 * a + 3]
    at = 2 * half_rows
    for ref in (first_gain_ref, second_gain_ref):
        for start in range(0, channels, lane):
            ref[:, start : start + lane] = mine_ref[at : at + 1, :] + theirs_ref[at : at + 1, :]
            at += 1


def backward_kernel(
    frame, norm_factor, which_ref, back_ref, state_ref, gain_ref, inside_ref, earlier_ref, order_ref,
    shrink_ref, slope_ref, activated_ref, expand_ref, expand_slope_ref, kernel_ref, part_ref,
    depth_ref, input_ref, gain_grad_ref, back_normed, normed,
):
    step = pl.program_id(0)
    cells, channels = state_ref.shape
    row_count, lon_count, _ = input_ref.shape
    lat_size, _, _, lane = part_ref.shape
    block = channels // lat_size
    inside = inside_ref[...]

    @pl.when(step == 0)
    def _():
        normed[...] = normalise(state_ref[...].astype(F32), gain_ref[...]).T
        back_normed[...] = earlier_ref[...]

    kernel = kernel_ref[...]
    back_convolved = (
        (times_transpose(back_ref[...], shrink_ref[...]) * slope_ref[0].astype(F32))
        .astype(BF16)
        .astype(F32)
    )
    flipped = jnp.concatenate([kernel[8 - i : 9 - i] for i in range(9)], axis=0)
    back_activated = convolve(back_convolved, flipped, row_count, frame)
    back_expanded = jnp.where(inside > 0, back_activated * expand_slope_ref[0].astype(F32), 0.0).astype(BF16)
    expand_grad = (matmul(normed[...], back_expanded) * norm_factor).astype(BF16)
    for lat in range(lat_size):
        for piece in range(expand_grad.shape[1] // lane):
            part_ref[lat, 0, piece * block : (piece + 1) * block, :] = expand_grad[
                lat * block : (lat + 1) * block, piece * lane : (piece + 1) * lane
            ]
    back_normed[...] += times_transpose(back_expanded, expand_ref[...])
    own_back = jnp.where(inside > 0, back_convolved[frame : frame + cells], 0.0)
    activated = activated_ref[0].astype(F32)
    for b in range(3):
        moved = own_back
        if b != 1:
            moved = pltpu.roll(own_back, cells - 1 if b == 0 else 1, 0)
        for a in range(3):
            depth_ref[0, 3 * a + b : 3 * a + b + 1, :] = norm_factor * jnp.sum(
                activated[a * frame : a * frame + cells] * moved, axis=0, keepdims=True
            )

    @pl.when(step == pl.num_programs(0) - 1)
    def _():
        state = state_ref[...].astype(F32)
        inverse = inverse_rms(state)
        grads = back_normed[...]
        gain_grad_ref[...] = norm_factor * jnp.sum(grads * state * inverse, axis=0, keepdims=True)
        result = (
            back_ref[frame : frame + cells, :].astype(F32)
            + norm_back(grads, state, inverse, gain_ref[...])
        ).astype(BF16)
        for row in range(row_count):
            start = row * frame + SIDE
            input_ref[row] = result[start : start + lon_count]


def backward(
    which, back, state, gain, inside, earlier, order, shrink_weight, slope, activated, expand_weight,
    expand_slope, kernel, norm_factor, lat_size, row_count, lon_count,
):
    cells, channels = state.shape
    frame = cells // row_count
    size = activated.shape[1]
    wide = expand_weight.shape[1]
    part = step_width(wide)
    steps = wide // part
    place = lambda step, which: step
    if which is not None:
        steps = steps // 2
        place = lambda step, which: 2 * step + which[0]
    else:
        which = 0
    fixed = lambda shape: pl.BlockSpec(shape, lambda step, which: (0,) * len(shape))
    moving = lambda rows: pl.BlockSpec((rows, part), lambda step, which: (0, place(step, which)))
    whole = lambda rows: pl.BlockSpec((1, rows, part), lambda step, which: (place(step, which), 0, 0))
    block = channels // lat_size
    lane = block
    pieces = part // lane
    return pl.pallas_call(
        functools.partial(backward_kernel, frame, norm_factor),
        grid_spec=pltpu.PrefetchScalarGridSpec(
            num_scalar_prefetch=1,
            grid=(steps,),
            in_specs=[
                fixed((size, channels)),
                fixed((cells, channels)),
                fixed((1, channels)),
                fixed((cells, 1)),
                fixed((cells, channels)),
                pl.BlockSpec(memory_space=pl.ANY),
                pl.BlockSpec((part, channels), lambda step, which: (place(step, which), 0)),
                whole(size),
                whole(size),
                moving(channels),
                whole(cells),
                moving(9),
            ],
            out_specs=(
                pl.BlockSpec((lat_size, 1, pieces * block, lane), lambda step, which: (0, step, 0, 0)),
                pl.BlockSpec((1, 9, part), lambda step, which: (step, 0, 0)),
                fixed((row_count, lon_count, channels)),
                fixed((1, channels)),
                fixed((cells, channels)),
            ),
            scratch_shapes=[pltpu.VMEM((channels, cells), BF16)],
        ),
        out_shape=(
            jax.ShapeDtypeStruct((lat_size, steps, pieces * block, lane), BF16),
            jax.ShapeDtypeStruct((steps, 9, part), F32),
            jax.ShapeDtypeStruct((row_count, lon_count, channels), BF16),
            jax.ShapeDtypeStruct((1, channels), F32),
            jax.ShapeDtypeStruct((cells, channels), F32),
        ),
        compiler_params=pltpu.CompilerParams(
            vmem_limit_bytes=56 * 1024 * 1024, dimension_semantics=("arbitrary",)
        ),
        cost_estimate=pl.CostEstimate(
            flops=8 * cells * channels * part * steps,
            bytes_accessed=(6 * channels + 12 * size) * part * steps,
            transcendentals=0,
        ),
        name="backward",
    )(
        jnp.reshape(which, (1,)).astype(jnp.int32), back, state, gain, inside, earlier, order,
        shrink_weight, slope, activated, expand_weight, expand_slope, kernel,
    )


def attention_kernel(
    head_width, query_block, qkv_ref, early_ref, order_ref, out_ref, heads_t, query_grad_t, key_t,
    value_t, back_ref, bias_ref, key_grad, value_grad, score_ref, back_prob_ref, prob_low_ref, back_score_ref,
):
    head = pl.program_id(0)
    cells = qkv_ref.shape[0]
    width = qkv_ref.shape[1] // 3
    sources = early_ref.shape[0]
    frame = cells // sources
    scale = 1.0 / math.sqrt(head_width)
    keys = qkv_ref[:, width : 2 * width]
    values = qkv_ref[:, 2 * width : 3 * width]
    part = 2 * frame

    @pl.when(head == 0)
    def _():
        key_t[...] = keys.T
        value_t[...] = values.T
        for source in range(sources):
            at = slice(source * frame, (source + 1) * frame)
            back_ref[at, :] = early_ref[source, 0:frame, 0:width]
            if early_ref.shape[1] > frame:
                bias_ref[at, :] = early_ref[source, frame:, :].astype(F32).T[0:frame]
            else:
                bias_ref[at, :] = early_ref[source, :, width:].astype(F32)
        key_grad[...] = jnp.zeros_like(key_grad)
        value_grad[...] = jnp.zeros_like(value_grad)

    lanes = lax.broadcasted_iota(jnp.int32, (1, width), 1) // head_width == head
    zero = jnp.zeros((), BF16)
    heads = lax.broadcasted_iota(jnp.int32, bias_ref.shape, 1)
    bias = LOG2E * jnp.sum(
        jnp.where(heads == head, bias_ref[...], 0.0), axis=1, keepdims=True
    )
    rows = pl.ds(pl.multiple_of(head * head_width, head_width), head_width)
    head_key_t = key_t[rows, :]
    head_value_t = value_t[rows, :]
    last_dims = (((1,), (1,)), ((), ()))

    def fold(values, combine):
        result = values[0:8]
        for start in range(8, values.shape[0], 8):
            result = combine(result, values[start : start + 8])
        return result

    def block(start):
        cols = pl.ds(start, query_block)
        queries = jnp.where(lanes, qkv_ref[cols, 0:width], zero)
        backs = jnp.where(lanes, back_ref[cols, :], zero)
        parts = [slice(i, i + part) for i in range(0, cells, part)]
        highest = jnp.full((8, query_block), -jnp.inf, F32)
        for at in parts:
            scores = lax.dot_general(
                qkv_ref[at, width : 2 * width], queries, last_dims, preferred_element_type=F32
            )
            scores = scores * (scale * LOG2E) + bias[at]
            score_ref[at, :] = scores
            highest = jnp.maximum(highest, fold(scores, jnp.maximum))
        highest = jnp.max(highest, axis=0, keepdims=True)
        total = jnp.zeros((8, query_block), F32)
        centred = jnp.zeros((8, query_block), F32)
        for at in parts:
            back_probs = lax.dot_general(
                qkv_ref[at, 2 * width : 3 * width], backs, last_dims, preferred_element_type=F32
            )
            exponent = jnp.exp2(score_ref[at, :] - highest)
            total = total + fold(exponent, jnp.add)
            centred = centred + fold(exponent * back_probs, jnp.add)
            score_ref[at, :] = exponent
            back_prob_ref[at, :] = back_probs
        inverse = 1.0 / jnp.sum(total, axis=0, keepdims=True)
        centred = jnp.sum(centred, axis=0, keepdims=True) * inverse
        for at in parts:
            probs = score_ref[at, :] * inverse
            probs_low = probs.astype(BF16)
            back_scores = (probs * (back_prob_ref[at, :] - centred)).astype(BF16)
            prob_low_ref[at, :] = probs_low
            back_score_ref[at, :] = back_scores
            value_grad[at, :] += matmul(probs_low, backs)
            key_grad[at, :] += matmul(back_scores, queries)
        heads_t[rows, cols] = matmul(head_value_t, prob_low_ref[...])
        query_grad_t[rows, cols] = matmul(head_key_t, back_score_ref[...])

    block_count = cells // query_block
    if block_count <= 4:
        for index in range(block_count):
            block(index * query_block)
    else:

        def step(index, carry):
            block(pl.multiple_of(index * query_block, query_block))
            return carry

        lax.fori_loop(0, block_count, step, 0)

    @pl.when(head == pl.num_programs(0) - 1)
    def _():
        out_ref[:, 0:width] = heads_t[...].T.astype(BF16)
        out_ref[:, width : 2 * width] = (query_grad_t[...] * scale).T.astype(BF16)
        out_ref[:, 2 * width : 3 * width] = (key_grad[...] * scale).astype(BF16)
        out_ref[:, 3 * width : 4 * width] = value_grad[...].astype(BF16)


def attention(qkv, early, order, head_width):
    cells = qkv.shape[0]
    width = qkv.shape[1] // 3
    items = width // head_width
    bias_columns = BIAS_ROWS if early.shape[2] == width else items
    query_block = cells if cells <= 1024 else 256
    whole = lambda shape: pl.BlockSpec(shape, lambda head: (0,) * len(shape))
    return pl.pallas_call(
        functools.partial(attention_kernel, head_width, query_block),
        grid=(items,),
        out_shape=jax.ShapeDtypeStruct((cells, 4 * width), BF16),
        in_specs=[whole(qkv.shape), whole(early.shape), pl.BlockSpec(memory_space=pl.ANY)],
        out_specs=whole((cells, 4 * width)),
        scratch_shapes=[
            pltpu.VMEM((width, cells), F32),
            pltpu.VMEM((width, cells), F32),
            pltpu.VMEM((width, cells), BF16),
            pltpu.VMEM((width, cells), BF16),
            pltpu.VMEM((cells, width), BF16),
            pltpu.VMEM((cells, bias_columns), F32),
            pltpu.VMEM((cells, width), F32),
            pltpu.VMEM((cells, width), F32),
            pltpu.VMEM((cells, query_block), F32),
            pltpu.VMEM((cells, query_block), F32),
            pltpu.VMEM((cells, query_block), BF16),
            pltpu.VMEM((cells, query_block), BF16),
        ],
        compiler_params=pltpu.CompilerParams(
            vmem_limit_bytes=(20 if cells <= 1024 else 48) * 1024 * 1024, dimension_semantics=("arbitrary",)
        ),
        cost_estimate=pl.CostEstimate(
            flops=items * cells * cells * 32 * 14,
            bytes_accessed=cells * width * 16,
            transcendentals=items * cells * cells,
        ),
        name="attention",
    )(qkv, early, order)


def per_device(
    state_field,
    cotangent,
    key_bias,
    input_gain,
    expand_weight,
    depth_weight,
    shrink_weight,
    attention_gain,
    attention_in,
    attention_out,
):
    row_count, lon_count, channels = state_field.shape
    head_count = key_bias.shape[2]
    head_width = channels // head_count
    wide = expand_weight.shape[1]
    lat_size, z_size = lax.axis_size("lat"), lax.axis_size("z")
    lon_size = 2 * z_size
    core = lax.axis_index("core")
    norm_factor = 1.0 / math.sqrt(row_count * lon_count * lat_size * lon_size)
    items = row_count * head_count // lon_size
    groups = head_count // items
    width = items * head_width
    frame = lon_count + 2 * SIDE
    own = row_count * frame
    kernel = depth_weight.astype(F32).reshape(9, wide)
    input_gain = input_gain.reshape(1, channels)
    attention_gain = attention_gain.reshape(1, channels)

    low, high = from_sides(state_field, SIDE, 1, LON, True)
    state = jnp.concatenate([low, state_field, high], axis=1)
    if row_count == 1:
        below, above = from_sides(state, 1, 0, "lat", False)
        far_below = lax.ppermute(below, "lat", shifts(lat_size, 1, False))
        far_above = lax.ppermute(above, "lat", shifts(lat_size, -1, False))
        all_rows = [far_below, below, state, above, far_above]
    else:
        below, above = from_sides(state, 2, 0, "lat", False)
        all_rows = [below, state, above]
    all_rows = jnp.concatenate(all_rows, axis=0)

    early, cot = early_parts(cotangent, key_bias, attention_out, state, groups)
    early = exchange(early, LON)

    qkv, inner = forward(
        all_rows, input_gain, expand_weight, kernel, shrink_weight, attention_gain, attention_in,
        groups,
    )
    activated, slope, mixed, expand_slope = around(
        all_rows, input_gain, expand_weight, kernel, inner
    )
    qkv = exchange(qkv, LON).reshape(lon_size * frame, 3 * width)

    attended = attention(qkv, early, mixed, head_width)
    attended = exchange(attended.reshape(lon_size, frame, 4 * width), LON)
    cot = cot.reshape(own, channels)
    output_field, back_inner, unpacked, gain_two = call(
        functools.partial(inner_kernel, groups, norm_factor),
        "back_inner",
        (
            jax.ShapeDtypeStruct((row_count, lon_count, channels), BF16),
            jax.ShapeDtypeStruct((own, channels), BF16),
            jax.ShapeDtypeStruct((own, 4 * channels), BF16),
            jax.ShapeDtypeStruct((1, channels), F32),
        ),
        attended,
        inner,
        cot,
        attention_out,
        attention_in,
        attention_gain,
        flops=8 * own * channels * channels,
    )

    back = back_inner.reshape(row_count, frame, channels)
    centre = back[:, SIDE : SIDE + lon_count]
    low, high = from_sides(centre, 1, 1, LON, True)
    edge = jnp.zeros((row_count, SIDE - 1, channels), BF16)
    back_sides = jnp.concatenate([edge, low, centre, high, edge], axis=1)
    below, above = from_sides(back_sides, 1, 0, "lat", False)
    back = jnp.concatenate([below, back_sides, above], axis=0).reshape(-1, channels)

    lane = channels // lat_size
    in_split, out_split, split = 3 * channels // lon_size, channels // lon_size, wide // lon_size
    grads = lambda which, order, added: weight_grads(
        which, unpacked, inner, attention_gain, cot, back_inner, mixed, order, added, norm_factor,
        lat_size, z_size,
    )
    theirs = grads(1 - core, back_sides, None)
    first = grads(core, back, core_swap(theirs))
    first_sums = sum_parts(exchange(first, "lat"), z_size)
    first_sums = lax.psum_scatter(first_sums, "z", scatter_dimension=0, tiled=True)
    flat = lambda parts: parts.reshape(lat_size, -1, lane)

    columns = lax.broadcasted_iota(jnp.int32, (row_count, frame, 1), 1).reshape(own, 1)
    inside = ((columns >= SIDE) & (columns < SIDE + lon_count)).astype(F32)
    state = state.reshape(own, channels)

    def backward_part(which, earlier, order):
        return backward(
            which, back, state, input_gain, inside, earlier, order, shrink_weight, slope, activated,
            expand_weight, expand_slope, kernel, norm_factor, lat_size, row_count, lon_count,
        )

    start = jnp.zeros((own, channels), F32)
    if split == step_width(wide):
        theirs, depth_theirs, _, _, partial = backward_part(1 - core, start, first)
        theirs = core_swap(theirs)
        mine, depth_mine, input_grad, gain_one, _ = backward_part(core, partial, first)
    else:
        parts, depth, input_grad, gain_one, _ = backward_part(None, start, first)
        steps = parts.shape[1]
        parts = parts.reshape(lat_size, steps, -1, split // lane, lane, lane)
        parts = parts.reshape(lat_size, z_size, 2, split // lane * lane, lane)
        theirs = core_swap(lax.dynamic_index_in_dim(parts, 1 - core, 2, False))
        mine = lax.dynamic_index_in_dim(parts, core, 2, False)
        depth = depth.reshape(steps, 9, -1, split).transpose(0, 2, 1, 3)
        depth = depth.reshape(z_size, 2, 9, split)
        depth_theirs = lax.dynamic_index_in_dim(depth, 1 - core, 1, False)
        depth_mine = lax.dynamic_index_in_dim(depth, core, 1, False)

    mine, theirs = flat(mine), flat(theirs)
    block_rows = mine.shape[1] // z_size
    small_rows = (9 * wide + 2 * channels) // lane
    output_field = output_field.transpose(1, 0, 2)
    input_grad = input_grad.transpose(1, 0, 2)
    second = call(
        pack_kernel,
        "pack",
        jax.ShapeDtypeStruct((lat_size, z_size * block_rows + small_rows, lane), BF16),
        mine,
        theirs,
        depth_mine,
        depth_theirs,
        gain_one,
        gain_two,
    )
    second = call(
        merge_kernel,
        "merge",
        jax.ShapeDtypeStruct((z_size, block_rows + small_rows, lane), BF16),
        exchange(second, "lat"),
        output_field,
        input_grad,
        specs=[pl.BlockSpec(memory_space=pltpu.VMEM)] + [pl.BlockSpec(memory_space=pl.ANY)] * 2,
    )
    weight = lambda rows, cols: jax.ShapeDtypeStruct((rows, cols), F32)
    expand_grad, small = call(
        second_kernel,
        "expand_grad",
        (weight(lane, split), weight(small_rows, lane)),
        exchange(second, "z"),
    )
    other = core_swap(small)
    if split % 128 == 0:
        depth_grad, input_gain_grad, attention_gain_grad = pl.pallas_call(
            functools.partial(small_kernel, split),
            out_shape=(
                jax.ShapeDtypeStruct((3, 3, wide), F32),
                weight(1, channels),
                weight(1, channels),
            ),
            in_specs=[
                pl.BlockSpec(memory_space=pltpu.SMEM),
                pl.BlockSpec(memory_space=pltpu.VMEM),
                pl.BlockSpec(memory_space=pltpu.VMEM),
            ],
            name="small_grads",
        )(core.reshape(1), small, other)
    else:
        rows = 9 * wide // 2 // lane
        own_half = small[:rows] + other[rows : 2 * rows]
        other_half = small[rows : 2 * rows] + other[:rows]
        depth_grad = jnp.where(
            core == 0, jnp.stack([own_half, other_half]), jnp.stack([other_half, own_half])
        )
        depth_grad = depth_grad.reshape(2, z_size, split // lane, 9, lane).transpose(3, 1, 0, 2, 4)
        depth_grad = depth_grad.reshape(3, 3, wide)
        gains = (small[2 * rows :] + other[2 * rows :]).reshape(2, channels)
        input_gain_grad, attention_gain_grad = gains[0], gains[1]
    shrink_grad, attention_in_grad, attention_out_grad = call(
        first_kernel,
        "shrink_and_attention_grads",
        (
            weight(out_split, wide // lat_size),
            weight(in_split, lane),
            weight(out_split, lane),
        ),
        first_sums,
    )
    return (
        output_field.transpose(1, 0, 2),
        input_grad.transpose(1, 0, 2),
        expand_grad,
        shrink_grad.T,
        attention_in_grad.T,
        attention_out_grad.T,
        depth_grad,
        input_gain_grad.reshape(channels),
        attention_gain_grad.reshape(channels),
    )


def solution(mesh):
    lat_size, lon_size = mesh.devices.shape
    split = Mesh(mesh.devices.reshape(lat_size, lon_size // 2, 2), ("lat", "z", "core"))
    grid = P("lat", LON, None)
    weight = P("lat", LON)

    def step(*arrays):
        outputs = jax.shard_map(
            per_device,
            mesh=split,
            in_specs=(grid, grid, grid) + (P(),) * 7,
            out_specs=(grid, grid, weight, weight, weight, weight, P(), P(), P()),
            check_vma=False,
        )(*arrays)
        return outputs

    return step
```

time: 248 us -> 200 us (0.81)
  waiting for transfers between devices: 81.5 us -> 30.1 us
  blocking collectives: 0 us -> 40.6 us
  starting transfers between devices: 58.7 us -> 35 us
  local copies, waits for them, and re-layouts: 44.6 us -> 21.7 us
  between operations: 1.27 us -> 14.5 us
  other arithmetic: 14.1 us -> 1.3 us
  Pallas kernels: 46.1 us -> 55.9 us
    all_to_all x9 -> x4, waiting for transfers between devices: 72.9 us -> 19.9 us  [exchange(): return lax.all_to_all(values, axis, 0, 0, tiled=True)]
    all_to_all x0 -> x2, blocking collectives: none -> 40.6 us  [exchange(): return lax.all_to_all(values, axis, 0, 0, tiled=True)]
    all_to_all x9 -> x4, starting transfers between devices: 34.2 us -> 16 us  [exchange(): return lax.all_to_all(values, axis, 0, 0, tiled=True)]
    pallas_call x5 -> x11, Pallas kernels: 10.8 us -> 21 us  [the longest x1 6.72 us: around(): pl.pallas_call(functools.partial(around_kernel, frame), grid=(steps,), ou...]
    unnamed x81 -> x71, local copies, waits for them, and re-layouts: 28.5 us -> 19.6 us
    convert_element_type x4 -> x0, other arithmetic: 7.23 us -> none  [the longest x3 7.22 us: both_cores(): return (mine.astype(F32) + core_swap(theirs).astype(F32)).astype(BF16)]
    ppermute x2 -> x0, starting transfers between devices: 6.55 us -> none  [the longest x1 5.26 us: per_device(): far_below = lax.ppermute(second[0], 'lat', shifts(lat_size, 1, False))]
    pallas_call x1, Pallas kernels: 17.8 us -> 11.7 us  [attention(): pl.pallas_call(functools.partial(attention_kernel, head_width, query_bloc...]
  transfers between devices with their start and end apart: 23 -> 16, of which waited for: 11 -> 9; matrix products, arithmetic and copies ran while one was open for 13% -> 3% of each run, Pallas kernels for 12% -> 19%
where the time goes in v3:
time: 200 us; the launch traced here: 199 us
  Pallas kernels  55.9 us (28%)
  blocking collectives  40.6 us (20%)
  starting transfers between devices  35 us (18%)
  waiting for transfers between devices  30.1 us (15%)
  local copies, waits for them, and re-layouts  21.7 us (11%)
  between operations  14.5 us (7%)
    all_to_all x2, blocking collectives, exchange(): return lax.all_to_all(values, axis, 0, 0, tiled=True)  40.6 us
    all_to_all x4, waiting for transfers between devices, exchange(): return lax.all_to_all(values, axis, 0, 0, tiled=True)  19.9 us
    unnamed x71, local copies, waits for them, and re-layouts  19.6 us
    all_to_all x4, starting transfers between devices, exchange(): return lax.all_to_all(values, axis, 0, 0, tiled=True)  16 us
    pallas_call x2, Pallas kernels, backward(): pl.pallas_call(functools.partial(backward_kernel, frame, norm_factor), gr...  15.7 us
    pallas_call x1, Pallas kernels, attention(): pl.pallas_call(functools.partial(attention_kernel, head_width, query_bloc...  11.7 us
    ppermute x4, starting transfers between devices, from_sides(): lax.ppermute(lax.slice_in_dim(block, 0, width, axis=dim), axis, shifts(co...  10.2 us
    ppermute x4, starting transfers between devices, from_sides(): lax.ppermute(lax.slice_in_dim(block, size - width, size, axis=dim), axis,...  8.59 us
  transfers between devices with their start and end apart: 16, of which 9 were waited for; matrix products, arithmetic and copies ran while one was open for 3% of the time, Pallas kernels for 19%

profile of v3, /device:TPU:0, one launch (start us, length us, event | category | flops | bytes accessed | tf_op | source)
XLA Modules:
  0.0 199.1 jit_solution(1904235010944504019)
XLA Ops:
  8.8 4.1 %collective-permute-start.1 = (bf16[2,3,512]{2,1,0:T(4,128)(2,1)S(1)}, bf16[2,3,512]{2,1,0:T(4,128)(2,1)S(1)}, u32[]{:S(2)}, u32[]{:S(2)}) collective-permute-start(bf16[2,3,512]{2,1,0:T(4,128)(2,1)S(1)} %get-tuple-element.86), channel_id=1, source_target_pairs={{0,7},{1,0},{2,1},{3,2},{4,3},{5,4},{6,5},{7,6},{8,15},{9,8},{10,9... | collective-permute-start | bytes 18440 | tf_op jit(solution)/shard_map/ppermute | solution.py:43
  14.3 4.5 %collective-permute-start.2 = (bf16[2,96,512]{2,1,0:T(8,128)(2,1)S(1)}, bf16[2,96,512]{2,1,0:T(8,128)(2,1)}, u32[]{:S(2)}, u32[]{:S(2)}) collective-permute-start(bf16[2,96,512]{2,1,0:T(8,128)(2,1)S(1)} %pad_maximum_fusion.2.order_ref), channel_id=1, source_target_pairs={{0,8},{8,16},{16,24},{1,9},{9,17},{17,25},{2,10},{10,18},{18,26},{... | collective-permute-start | bytes 589832 | tf_op jit(solution)/shard_map/ppermute | solution.py:40
  22.4 4.5 %all-to-all-start.1 = ((bf16[8,112,128]{2,1,0:T(8,128)(2,1)}), bf16[8,112,128]{2,1,0:T(8,128)(2,1)S(1)}, u32[]{:S(2)}, u32[]{:S(2)}) async-start(bf16[8,112,128]{2,1,0:T(8,128)(2,1)} %get-tuple-element.37), calls=%async_computation.1 | async-start | bytes 458752 | tf_op jit(solution)/shard_map/all_to_all | solution.py:54
  27.0 1.8 collective-permute-done.3
  30.0 1.6 copy-done.1
  33.0 7.4 %forward.1 = (bf16[8,96,384]{2,1,0:T(8,128)(2,1)}, bf16[192,512]{1,0:T(8,128)(2,1)S(1)}) custom-call(bf16[576,512]{1,0:T(8,128)(2,1)S(1)} %bitcast.31, f32[1,512]{1,0:T(1,128)S(1)} %bitcast.49, bf16[512,2048]{1,0:T(8,128)(2,1)S(1)} %copy-done, f32[9,2048]{1,0:T(8,128)S(1)} %reshape.130.kernel_ref, bf16[2048,512]{1,0:T(8,128)(2,1)S(1)} %copy-done.1, ...), custom_call_target="tpu_custom_call" | custom-call | flops 1509949440 | bytes 5767168 | tf_op jit(solution)/shard_map/forward/pallas_call | solution.py:220
  41.3 4.2 %all-to-all-start = ((bf16[8,96,384]{2,1,0:T(8,128)(2,1)}), bf16[8,96,384]{2,1,0:T(8,128)(2,1)}, u32[]{:S(2)}, u32[]{:S(2)}) async-start(bf16[8,96,384]{2,1,0:T(8,128)(2,1)} %get-tuple-element.36), calls=%async_computation | async-start | bytes 1179648 | tf_op jit(solution)/shard_map/all_to_all | solution.py:54
  46.5 6.7 %forward_around.1 = (bf16[8,384,256]{2,1,0:T(8,128)(2,1)S(1)}, bf16[8,384,256]{2,1,0:T(8,128)(2,1)S(1)}, bf16[8,192,256]{2,1,0:T(8,128)(2,1)S(1)}, bf16[8,192,256]{2,1,0:T(8,128)(2,1)S(1)}) custom-call(bf16[576,512]{1,0:T(8,128)(2,1)S(1)} %bitcast.32, f32[1,512]{1,0:T(1,128)S(1)} %bitcast.50, bf16[512,2048]{1,0:T(8,128)(2,1)S(1)} %copy-done, ...), custom_call_target="tpu_custom_call" | custom-call | flops 1207959552 | bytes 13107200 | tf_op jit(solution)/shard_map/forward_around/pallas_call | solution.py:298
  56.5 5.7 %all-to-all-done = bf16[8,96,384]{2,1,0:T(8,128)(2,1)} async-done(((bf16[8,96,384]{2,1,0:T(8,128)(2,1)}), bf16[8,96,384]{2,1,0:T(8,128)(2,1)}, u32[]{:S(2)}, u32[]{:S(2)}) %all-to-all-start) | async-done | bytes 589856 | tf_op jit(solution)/shard_map/all_to_all | solution.py:54
  63.2 11.7 %attention.1 = bf16[768,512]{1,0:T(8,128)(2,1)S(1)} custom-call(bf16[768,384]{1,0:T(8,128)(2,1)} %bitcast.3.qkv_ref, bf16[8,112,128]{2,1,0:T(8,128)(2,1)S(1)} %copy-done.18, bf16[8,192,256]{2,1,0:T(8,128)(2,1)S(1)} %get-tuple-element.39.order_ref.mixed_ref), custom_call_target="tpu_custom_call" | custom-call | flops 1056964608 | bytes 1572864 | tf_op jit(solution)/shard_map/attention/pallas_call | solution.py:781
  74.8 23.5 %all_to_all.30.attended_ref = bf16[8,96,512]{2,1,0:T(8,128)(2,1)S(1)} all-to-all(bf16[8,96,512]{2,1,0:T(8,128)(2,1)S(1)} %bitcast.40), channel_id=1, replica_groups=mesh['lat'=4,'z'=4,'core'=2] {'z','core'}, dimensions={0} | all-to-all | bytes 1572864 | tf_op jit(solution)/shard_map/all_to_all | solution.py:54
  100.1 3.5 %collective-permute-start.5 = (bf16[2,1,512]{2,1,0:T(2,128)(2,1)S(1)}, bf16[2,1,512]{2,1,0:T(2,128)(2,1)S(1)}, u32[]{:S(2)}, u32[]{:S(2)}) collective-permute-start(bf16[2,1,512]{2,1,0:T(2,128)(2,1)S(1)} %get-tuple-element.83), channel_id=1, source_target_pairs={{0,7},{1,0},{2,1},{3,2},{4,3},{5,4},{6,5},{7,6},{8,15},{9,8},{10,9... | collective-permute-start | bytes 6152 | tf_op jit(solution)/shard_map/ppermute | solution.py:43
  106.8 3.5 %collective-permute-start.6 = (bf16[1,96,512]{2,1,0:T(8,128)(2,1)S(1)}, bf16[1,96,512]{2,1,0:T(8,128)(2,1)S(1)}, u32[]{:S(2)}, u32[]{:S(2)}) collective-permute-start(bf16[1,96,512]{2,1,0:T(8,128)(2,1)S(1)} %get-tuple-element.81), channel_id=1, source_target_pairs={{0,8},{8,16},{16,24},{1,9},{9,17},{17,25},{2,10},{10,18},{18,26},{... | collective-permute-start | bytes 294920 | tf_op jit(solution)/shard_map/ppermute | solution.py:40
  113.0 4.3 %collective-permute-done.7 = bf16[1,96,512]{2,1,0:T(8,128)(2,1)S(1)} collective-permute-done((bf16[1,96,512]{2,1,0:T(8,128)(2,1)S(1)}, bf16[1,96,512]{2,1,0:T(8,128)(2,1)S(1)}, u32[]{:S(2)}, u32[]{:S(2)}) %collective-permute-start.7) | collective-permute-done | bytes 98336 | tf_op jit(solution)/shard_map/ppermute | solution.py:43
  117.4 2.7 %weight_grads.3.order_ref = bf16[4,2048,128]{2,1,0:T(8,128)(2,1)} custom-call(s32[1]{0:T(128)} %bitcast.6.which_ref.core_ref, bf16[192,2048]{1,0:T(8,128)(2,1)S(1)} %get-tuple-element.43.unpacked_ref, bf16[192,512]{1,0:T(8,128)(2,1)S(1)} %get-tuple-element.38.order_ref.inner_ref, f32[1,512]{1,0:T(1,128)S(1)} %bitcast.46, bf16[192,512]{1,0:T(8,128)(2,1)S(1)} %bitcast.37, ...), custom_call_target="tpu_custom_call" | custom-call | flops 402653184 | bytes 8388608 | tf_op jit(solution)/shard_map/weight_grads/pallas_call | solution.py:416
  120.1 3.8 %all-to-all-start.5 = ((bf16[4,2048,128]{2,1,0:T(8,128)(2,1)}), bf16[4,2048,128]{2,1,0:T(8,128)(2,1)S(1)}, u32[]{:S(2)}, u32[]{:S(2)}) async-start(bf16[4,2048,128]{2,1,0:T(8,128)(2,1)} %weight_grads.3.order_ref), calls=%async_computation.5 | async-start | bytes 4194304 | tf_op jit(solution)/shard_map/all_to_all | solution.py:54
  125.5 7.9 %backward.2 = (bf16[4,4,256,128]{3,2,1,0:T(8,128)(2,1)}, f32[4,9,256]{2,1,0:T(8,128)}, bf16[2,90,512]{2,1,0:T(8,128)(2,1)}, f32[1,512]{1,0:T(1,128)}, f32[192,512]{1,0:T(8,128)}) custom-call(s32[1]{0:T(128)} %bitcast.10.which_ref, bf16[384,512]{1,0:T(8,128)(2,1)} %bitcast.27, bf16[192,512]{1,0:T(8,128)(2,1)} %bitcast.29, f32[1,512]{1,0:T(1,128)} %bitcast.47, ...), custom_call_target="tpu_custom_call" | custom-call | flops 805306368 | bytes 7864320 | tf_op jit(solution)/shard_map/backward/pallas_call | solution.py:621
  133.5 7.9 %backward.3 = (bf16[4,4,256,128]{3,2,1,0:T(8,128)(2,1)}, f32[4,9,256]{2,1,0:T(8,128)}, bf16[2,90,512]{2,1,0:T(8,128)(2,1)}, f32[1,512]{1,0:T(1,128)}, f32[192,512]{1,0:T(8,128)}) custom-call(s32[1]{0:T(128)} %bitcast.6.which_ref.core_ref, bf16[384,512]{1,0:T(8,128)(2,1)} %bitcast.28, bf16[192,512]{1,0:T(8,128)(2,1)} %bitcast.30, f32[1,512]{1,0:T(1,128)} %bitcast.48, ...), custom_call_target="tpu_custom_call" | custom-call | flops 805306368 | bytes 7864320 | tf_op jit(solution)/shard_map/backward/pallas_call | solution.py:621
  145.4 3.9 %all-to-all-done.5.parts_ref = bf16[4,2048,128]{2,1,0:T(8,128)(2,1)S(1)} async-done(((bf16[4,2048,128]{2,1,0:T(8,128)(2,1)}), bf16[4,2048,128]{2,1,0:T(8,128)(2,1)S(1)}, u32[]{:S(2)}, u32[]{:S(2)}) %all-to-all-start.5) | async-done | bytes 2097184 | tf_op jit(solution)/shard_map/all_to_all | solution.py:54
  150.6 3.5 %all-to-all-start.3 = ((bf16[4,1176,128]{2,1,0:T(8,128)(2,1)}), bf16[4,1176,128]{2,1,0:T(8,128)(2,1)S(1)}, u32[]{:S(2)}, u32[]{:S(2)}) async-start(bf16[4,1176,128]{2,1,0:T(8,128)(2,1)} %pack.1), calls=%async_computation.3 | async-start | bytes 2408448 | tf_op jit(solution)/shard_map/all_to_all | solution.py:54
  154.2 3.7 %sum_bands.1 = bf16[2048,128]{1,0:T(8,128)(2,1)} custom-call(bf16[4,2048,128]{2,1,0:T(8,128)(2,1)} %copy-done.26), custom_call_target="tpu_custom_call" | custom-call | tf_op jit(solution)/shard_map/sum_bands/pallas_call | solution.py:445
  158.4 10.4 %all-to-all-done.3.parts_ref = bf16[4,1176,128]{2,1,0:T(8,128)(2,1)S(1)} async-done(((bf16[4,1176,128]{2,1,0:T(8,128)(2,1)}), bf16[4,1176,128]{2,1,0:T(8,128)(2,1)S(1)}, u32[]{:S(2)}, u32[]{:S(2)}) %all-to-all-start.3) | async-done | bytes 1204256 | tf_op jit(solution)/shard_map/all_to_all | solution.py:54
  168.9 17.1 %all_to_all.31.parts_ref = bf16[4,408,128]{2,1,0:T(8,128)(2,1)S(1)} all-to-all(bf16[4,408,128]{2,1,0:T(8,128)(2,1)S(1)} %merge.1), channel_id=1, replica_groups=mesh['lat'=4,'z'=4,'core'=2] {'z'}, dimensions={0} | all-to-all | bytes 835584 | tf_op jit(solution)/shard_map/all_to_all | solution.py:54
  190.6 1.6 small_grads.1
  (110 shorter events, 35.1 us)
Async XLA Ops:
  7.2 13.9 %copy-start.31 = (bf16[2,90,16]{1,2,0:T(8,128)(2,1)S(1)}, bf16[2,90,16]{1,2,0:T(8,128)(2,1)}, u32[]{:S(2)}) copy-start(bf16[2,90,16]{1,2,0:T(8,128)(2,1)} %param.12) | copy-start | bytes 17284
  7.2 14.0 %copy-start.12 = (bf16[512,512]{1,0:T(8,128)(2,1)S(1)}, bf16[512,512]{1,0:T(8,128)(2,1)}, u32[]{:S(2)}) copy-start(bf16[512,512]{1,0:T(8,128)(2,1)} %out_weight_ref.3) | copy-start | bytes 1572868
  8.2 11.9 %copy-start.27 = (bf16[2,90,512]{2,1,0:T(8,128)(2,1)}, bf16[2,90,512]{2,1,0:T(8,128)(2,1)S(1)}, u32[]{:S(2)}) copy-start(bf16[2,90,512]{2,1,0:T(8,128)(2,1)S(1)} %copy.28) | copy-start | bytes 552964
  8.2 18.7 %copy-start.30 = (bf16[3,3,2048]{2,1,0:T(4,128)(2,1)S(1)}, bf16[3,3,2048]{2,1,0:T(4,128)(2,1)}, u32[]{:S(2)}) copy-start(bf16[3,3,2048]{2,1,0:T(4,128)(2,1)} %param.15) | copy-start | bytes 110596
  8.2 5.9 %collective-permute-start = (bf16[2,3,512]{2,1,0:T(4,128)(2,1)S(1)}, bf16[2,3,512]{2,1,0:T(4,128)(2,1)S(1)}, u32[]{:S(2)}, u32[]{:S(2)}) collective-permute-start(bf16[2,3,512]{2,1,0:T(4,128)(2,1)S(1)} %get-tuple-element.85), channel_id=1, source_target_pairs={{0,1},{1,2},{2,3},{3,4},{4,5},{5,6},{6,7},{7,0},{8,9},{9,10},{10,1... | collective-permute-start | bytes 18440 | tf_op jit(solution)/shard_map/ppermute | solution.py:40
  8.8 5.5 %collective-permute-start.1 = (bf16[2,3,512]{2,1,0:T(4,128)(2,1)S(1)}, bf16[2,3,512]{2,1,0:T(4,128)(2,1)S(1)}, u32[]{:S(2)}, u32[]{:S(2)}) collective-permute-start(bf16[2,3,512]{2,1,0:T(4,128)(2,1)S(1)} %get-tuple-element.86), channel_id=1, source_target_pairs={{0,7},{1,0},{2,1},{3,2},{4,3},{5,4},{6,5},{7,6},{8,15},{9,8},{10,9... | collective-permute-start | bytes 18440 | tf_op jit(solution)/shard_map/ppermute | solution.py:43
  14.3 15.7 %copy-start.8 = (bf16[2,96,512]{2,1,0:T(8,128)(2,1)}, bf16[2,96,512]{2,1,0:T(8,128)(2,1)S(1)}, u32[]{:S(2)}) copy-start(bf16[2,96,512]{2,1,0:T(8,128)(2,1)S(1)} %pad_maximum_fusion.2.order_ref) | copy-start | bytes 589828
  14.3 12.7 %collective-permute-start.2 = (bf16[2,96,512]{2,1,0:T(8,128)(2,1)S(1)}, bf16[2,96,512]{2,1,0:T(8,128)(2,1)}, u32[]{:S(2)}, u32[]{:S(2)}) collective-permute-start(bf16[2,96,512]{2,1,0:T(8,128)(2,1)S(1)} %pad_maximum_fusion.2.order_ref), channel_id=1, source_target_pairs={{0,8},{8,16},{16,24},{1,9},{9,17},{17,25},{2,10},{10,18},{18,26},{... | collective-permute-start | bytes 589832 | tf_op jit(solution)/shard_map/ppermute | solution.py:40
  18.8 10.0 %collective-permute-start.3 = (bf16[2,96,512]{2,1,0:T(8,128)(2,1)S(1)}, bf16[2,96,512]{2,1,0:T(8,128)(2,1)}, u32[]{:S(2)}, u32[]{:S(2)}) collective-permute-start(bf16[2,96,512]{2,1,0:T(8,128)(2,1)S(1)} %pad_maximum_fusion.2.order_ref), channel_id=1, source_target_pairs={{8,0},{16,8},{24,16},{9,1},{17,9},{25,17},{10,2},{18,10},{26,18},{... | collective-permute-start | bytes 589832 | tf_op jit(solution)/shard_map/ppermute | solution.py:43
  22.4 18.9 %all-to-all-start.1 = ((bf16[8,112,128]{2,1,0:T(8,128)(2,1)}), bf16[8,112,128]{2,1,0:T(8,128)(2,1)S(1)}, u32[]{:S(2)}, u32[]{:S(2)}) async-start(bf16[8,112,128]{2,1,0:T(8,128)(2,1)} %get-tuple-element.37), calls=%async_computation.1 | async-start | bytes 458752 | tf_op jit(solution)/shard_map/all_to_all | solution.py:54
  26.9 18.5 %copy-start.11 = (f32[9,2048]{1,0:T(8,128)}, f32[9,2048]{1,0:T(8,128)S(1)}, u32[]{:S(2)}) copy-start(f32[9,2048]{1,0:T(8,128)S(1)} %reshape.130.kernel_ref) | copy-start | bytes 221188
  41.3 21.0 %all-to-all-start = ((bf16[8,96,384]{2,1,0:T(8,128)(2,1)}), bf16[8,96,384]{2,1,0:T(8,128)(2,1)}, u32[]{:S(2)}, u32[]{:S(2)}) async-start(bf16[8,96,384]{2,1,0:T(8,128)(2,1)} %get-tuple-element.36), calls=%async_computation | async-start | bytes 1179648 | tf_op jit(solution)/shard_map/all_to_all | solution.py:54
  63.2 35.2 %copy-start.13 = (bf16[512,512]{1,0:T(8,128)(2,1)S(1)}, bf16[512,512]{1,0:T(8,128)(2,1)}, u32[]{:S(2)}) copy-start(bf16[512,512]{1,0:T(8,128)(2,1)} %out_weight_ref.3) | copy-start | bytes 1572868
  74.8 23.5 %copy-start.6 = (bf16[512,1536]{1,0:T(8,128)(2,1)S(1)}, bf16[512,1536]{1,0:T(8,128)(2,1)}, u32[]{:S(2)}) copy-start(bf16[512,1536]{1,0:T(8,128)(2,1)} %in_weight_ref.1) | copy-start | bytes 4718596
  100.0 4.9 %collective-permute-start.4 = (bf16[2,1,512]{2,1,0:T(2,128)(2,1)S(1)}, bf16[2,1,512]{2,1,0:T(2,128)(2,1)S(1)}, u32[]{:S(2)}, u32[]{:S(2)}) collective-permute-start(bf16[2,1,512]{2,1,0:T(2,128)(2,1)S(1)} %get-tuple-element.84), channel_id=1, source_target_pairs={{0,1},{1,2},{2,3},{3,4},{4,5},{5,6},{6,7},{7,0},{8,9},{9,10},{10,1... | collective-permute-start | bytes 6152 | tf_op jit(solution)/shard_map/ppermute | solution.py:40
  100.1 4.9 %collective-permute-start.5 = (bf16[2,1,512]{2,1,0:T(2,128)(2,1)S(1)}, bf16[2,1,512]{2,1,0:T(2,128)(2,1)S(1)}, u32[]{:S(2)}, u32[]{:S(2)}) collective-permute-start(bf16[2,1,512]{2,1,0:T(2,128)(2,1)S(1)} %get-tuple-element.83), channel_id=1, source_target_pairs={{0,7},{1,0},{2,1},{3,2},{4,3},{5,4},{6,5},{7,6},{8,15},{9,8},{10,9... | collective-permute-start | bytes 6152 | tf_op jit(solution)/shard_map/ppermute | solution.py:43
  106.7 10.6 %collective-permute-start.8 = (bf16[4,2048,128]{2,1,0:T(8,128)(2,1)S(1)}, bf16[4,2048,128]{2,1,0:T(8,128)(2,1)S(1)}, u32[]{:S(2)}, u32[]{:S(2)}) collective-permute-start(bf16[4,2048,128]{2,1,0:T(8,128)(2,1)S(1)} %weight_grads.2), channel_id=1, source_target_pairs={{0,1},{1,0},{2,3},{3,2},{4,5},{5,4},{6,7},{7,6},{8,9},{9,8},{10,11... | collective-permute-start | bytes 6291464 | tf_op jit(solution)/shard_map/ppermute | solution.py:50
  106.8 6.2 %collective-permute-start.6 = (bf16[1,96,512]{2,1,0:T(8,128)(2,1)S(1)}, bf16[1,96,512]{2,1,0:T(8,128)(2,1)S(1)}, u32[]{:S(2)}, u32[]{:S(2)}) collective-permute-start(bf16[1,96,512]{2,1,0:T(8,128)(2,1)S(1)} %get-tuple-element.81), channel_id=1, source_target_pairs={{0,8},{8,16},{16,24},{1,9},{9,17},{17,25},{2,10},{10,18},{18,26},{... | collective-permute-start | bytes 294920 | tf_op jit(solution)/shard_map/ppermute | solution.py:40
  110.3 7.0 %collective-permute-start.7 = (bf16[1,96,512]{2,1,0:T(8,128)(2,1)S(1)}, bf16[1,96,512]{2,1,0:T(8,128)(2,1)S(1)}, u32[]{:S(2)}, u32[]{:S(2)}) collective-permute-start(bf16[1,96,512]{2,1,0:T(8,128)(2,1)S(1)} %get-tuple-element.82), channel_id=1, source_target_pairs={{8,0},{16,8},{24,16},{9,1},{17,9},{25,17},{10,2},{18,10},{26,18},{... | collective-permute-start | bytes 294920 | tf_op jit(solution)/shard_map/ppermute | solution.py:43
  120.1 29.2 %all-to-all-start.5 = ((bf16[4,2048,128]{2,1,0:T(8,128)(2,1)}), bf16[4,2048,128]{2,1,0:T(8,128)(2,1)S(1)}, u32[]{:S(2)}, u32[]{:S(2)}) async-start(bf16[4,2048,128]{2,1,0:T(8,128)(2,1)} %weight_grads.3.order_ref), calls=%async_computation.5 | async-start | bytes 4194304 | tf_op jit(solution)/shard_map/all_to_all | solution.py:54
  133.4 8.0 %collective-permute-start.9 = (bf16[4,4,256,128]{3,2,1,0:T(8,128)(2,1)}, bf16[4,4,256,128]{3,2,1,0:T(8,128)(2,1)S(1)}, u32[]{:S(2)}, u32[]{:S(2)}) collective-permute-start(bf16[4,4,256,128]{3,2,1,0:T(8,128)(2,1)} %get-tuple-element.50), channel_id=1, source_target_pairs={{0,1},{1,0},{2,3},{3,2},{4,5},{5,4},{6,7},{7,6},{8,9},{9,8},{10,11... | collective-permute-start | bytes 3145736 | tf_op jit(solution)/shard_map/ppermute | solution.py:50
  150.6 18.1 %all-to-all-start.3 = ((bf16[4,1176,128]{2,1,0:T(8,128)(2,1)}), bf16[4,1176,128]{2,1,0:T(8,128)(2,1)S(1)}, u32[]{:S(2)}, u32[]{:S(2)}) async-start(bf16[4,1176,128]{2,1,0:T(8,128)(2,1)} %pack.1), calls=%async_computation.3 | async-start | bytes 2408448 | tf_op jit(solution)/shard_map/all_to_all | solution.py:54
  154.2 34.2 %reduce-scatter.2.cloned.1.call-start = ((), (), s32[]{:S(2)}) async-start(), calls=%async_computation.7 | async-start | bytes 655360 | tf_op jit(solution)/shard_map/reduce_scatter | solution.py:904
  186.6 3.4 %collective-permute-start.10 = (f32[152,128]{1,0:T(8,128)S(1)}, f32[152,128]{1,0:T(8,128)S(1)}, u32[]{:S(2)}, u32[]{:S(2)}) collective-permute-start(f32[152,128]{1,0:T(8,128)S(1)} %get-tuple-element.59.mine_ref), channel_id=1, source_target_pairs={{0,1},{1,0},{2,3},{3,2},{4,5},{5,4},{6,7},{7,6},{8,9},{9,8},{10,11... | collective-permute-start | bytes 233480 | tf_op jit(solution)/shard_map/ppermute | solution.py:50
  (24 other events, 67.7 us)
Sparse Core Ops, SparseCore 0:
  158.1 24.1 reduce-scatter.1

commit v4 on v3

--- a/solution.py
+++ b/solution.py
@@ -16,6 +16,7 @@
 MASKED = -1e30
 SIDE = 3
 BIAS_ROWS = 16
+FORWARD_WIDTH = 512
 LOG2E = math.log2(math.e)
 
 
@@ -58,10 +59,6 @@
     return jnp.dot(left, right, preferred_element_type=F32)
 
 
-def cross_cells(left, right):
-    return lax.dot_general(left, right, (((0,), (0,)), ((), ())), preferred_element_type=F32)
-
-
 def times_transpose(values, weights):
     return lax.dot_general(
         values, weights, (((values.ndim - 1,), (1,)), ((), ())), preferred_element_type=F32
@@ -76,17 +73,15 @@
     return values * sigmoid(values)
 
 
-def silu_slope(values):
-    gate = sigmoid(values)
-    return gate * (1.0 + values * (1.0 - gate))
-
-
-def call(kernel, name, out_shape, *operands, scratch=(), megabytes=16, flops=0, specs=None):
+def call(kernel, name, out_shape, *operands, scratch=(), megabytes=16, flops=0, specs=None, out_specs=None, aliases=None):
     return pl.pallas_call(
         kernel,
         out_shape=out_shape,
         scratch_shapes=scratch,
         in_specs=specs or [pl.BlockSpec(memory_space=pltpu.VMEM)] * len(operands),
+        out_specs=out_specs
+        or jax.tree.map(lambda _: pl.BlockSpec(memory_space=pltpu.VMEM), out_shape),
+        input_output_aliases=aliases or {},
         compiler_params=pltpu.CompilerParams(vmem_limit_bytes=megabytes * 1024 * 1024),
         cost_estimate=pl.CostEstimate(
             flops=flops,
@@ -172,38 +167,49 @@
 
 
 def forward_kernel(
-    frame, groups, state_ref, gain_ref, expand_ref, kernel_ref, shrink_ref, second_gain_ref, in_ref,
-    qkv_ref, inner_ref, normed, total,
-):
-    step = pl.program_id(0)
+    frame, groups, steps, state_ref, gain_ref, kernel_ref, second_gain_ref, expand_hbm, shrink_hbm,
+    in_hbm, qkv_ref, inner_ref, expand_ref, shrink_ref, in_ref, normed, total, arrived,
+):
     cells, channels = inner_ref.shape
+    wide = expand_ref.shape[1]
     rows = cells // frame
     width = channels // groups
-
-    @pl.when(step == 0)
-    def _():
-        near = state_ref[frame : frame + normed.shape[0], :].astype(F32)
-        normed[...] = normalise(near, gain_ref[...])
-        total[...] = jnp.zeros_like(total)
-
-    activated = silu(matmul(normed[...], expand_ref[...])).astype(BF16).astype(F32)
-    mixed = silu(convolve(activated, kernel_ref[...], rows, frame)).astype(BF16)
-    total[...] += matmul(mixed, shrink_ref[...])
-
-    @pl.when(step == pl.num_programs(0) - 1)
-    def _():
-        inner = state_ref[2 * frame : 2 * frame + cells, :].astype(F32)
-        inner = (inner + total[...]).astype(BF16)
-        inner_ref[...] = inner
-        normed_second = normalise(inner.astype(F32), second_gain_ref[...])
-        projected = matmul(normed_second, in_ref[...]).astype(BF16)
-        for row in range(rows):
-            for group in range(groups):
-                for kind in range(3):
-                    start = kind * channels + group * width
-                    qkv_ref[row * groups + group, :, kind * width : (kind + 1) * width] = projected[
-                        row * frame : (row + 1) * frame, start : start + width
-                    ]
+    part = wide // steps
+    parts = [slice(i * part, (i + 1) * part) for i in range(steps)]
+    expand_copies, shrink_copies = [], []
+    for i, cols in enumerate(parts):
+        expand_copies.append(
+            pltpu.make_async_copy(expand_hbm.at[:, cols], expand_ref.at[:, cols], arrived.at[i])
+        )
+        shrink_copies.append(
+            pltpu.make_async_copy(shrink_hbm.at[cols], shrink_ref.at[cols], arrived.at[steps + i])
+        )
+        expand_copies[i].start()
+        shrink_copies[i].start()
+    in_copy = pltpu.make_async_copy(in_hbm, in_ref, arrived.at[2 * steps])
+    in_copy.start()
+    near = state_ref[frame : frame + normed.shape[0], :].astype(F32)
+    normed[...] = normalise(near, gain_ref[...])
+    for i, cols in enumerate(parts):
+        expand_copies[i].wait()
+        activated = silu(matmul(normed[...], expand_ref[:, cols])).astype(BF16).astype(F32)
+        mixed = silu(convolve(activated, kernel_ref[:, cols], rows, frame)).astype(BF16)
+        shrink_copies[i].wait()
+        product = matmul(mixed, shrink_ref[cols])
+        total[...] = product if i == 0 else total[...] + product
+    inner = state_ref[2 * frame : 2 * frame + cells, :].astype(F32)
+    inner = (inner + total[...]).astype(BF16)
+    inner_ref[...] = inner
+    normed_second = normalise(inner.astype(F32), second_gain_ref[...])
+    in_copy.wait()
+    projected = matmul(normed_second, in_ref[...]).astype(BF16)
+    for row in range(rows):
+        for group in range(groups):
+            for kind in range(3):
+                start = kind * channels + group * width
+                qkv_ref[row * groups + group, :, kind * width : (kind + 1) * width] = projected[
+                    row * frame : (row + 1) * frame, start : start + width
+                ]
 
 
 def step_width(wide):
@@ -215,35 +221,24 @@
     rows = all_rows - 4
     cells = rows * frame
     wide = expand_weight.shape[1]
-    part = step_width(wide)
-    fixed = lambda shape: pl.BlockSpec(shape, lambda step: (0,) * len(shape))
+    steps = wide // FORWARD_WIDTH
+    here, away = pl.BlockSpec(memory_space=pltpu.VMEM), pl.BlockSpec(memory_space=pl.ANY)
     return pl.pallas_call(
-        functools.partial(forward_kernel, frame, groups),
-        grid=(wide // part,),
+        functools.partial(forward_kernel, frame, groups, steps),
         out_shape=(
             jax.ShapeDtypeStruct((rows * groups, frame, 3 * channels // groups), BF16),
             jax.ShapeDtypeStruct((cells, channels), BF16),
         ),
-        in_specs=[
-            fixed((all_rows * frame, channels)),
-            fixed((1, channels)),
-            pl.BlockSpec((channels, part), lambda step: (0, step)),
-            pl.BlockSpec((9, part), lambda step: (0, step)),
-            pl.BlockSpec((part, channels), lambda step: (step, 0)),
-            fixed((1, channels)),
-            fixed(attention_in.shape),
-        ],
-        out_specs=(
-            fixed((rows * groups, frame, 3 * channels // groups)),
-            fixed((cells, channels)),
-        ),
+        in_specs=[here] * 4 + [away] * 3,
         scratch_shapes=[
+            pltpu.VMEM(expand_weight.shape, BF16),
+            pltpu.VMEM(shrink_weight.shape, BF16),
+            pltpu.VMEM(attention_in.shape, BF16),
             pltpu.VMEM((cells + 2 * frame, channels), BF16),
             pltpu.VMEM((cells, channels), F32),
+            pltpu.SemaphoreType.DMA((2 * steps + 1,)),
         ],
-        compiler_params=pltpu.CompilerParams(
-            vmem_limit_bytes=16 * 1024 * 1024, dimension_semantics=("arbitrary",)
-        ),
+        compiler_params=pltpu.CompilerParams(vmem_limit_bytes=56 * 1024 * 1024),
         cost_estimate=pl.CostEstimate(
             flops=2 * cells * channels * (3 * wide + 3 * channels),
             bytes_accessed=4 * channels * wide + 6 * channels * channels,
@@ -253,10 +248,10 @@
     )(
         state.reshape(all_rows * frame, channels),
         input_gain,
+        kernel,
+        gain,
         expand_weight,
-        kernel,
         shrink_weight,
-        gain,
         attention_in,
     )
 
@@ -278,7 +273,7 @@
     activated_ref[0] = activated[frame : frame + size]
     own_gate, own = gate[2 * frame : 2 * frame + cells], expanded[2 * frame : 2 * frame + cells]
     expand_slope_ref[0] = (own_gate * (1.0 + own * (1.0 - own_gate))).astype(BF16)
-    convolved = convolve(activated.astype(F32), kernel_ref[...], size // frame, frame)
+    convolved = convolve(activated.astype(F32), kernel_ref[0], size // frame, frame)
     gate = sigmoid(convolved)
     slope_ref[0] = (gate * (1.0 + convolved * (1.0 - gate))).astype(BF16)
     mixed_ref[0] = (
@@ -308,7 +303,7 @@
             fixed((all_rows * frame, channels)),
             fixed((1, channels)),
             moving(channels),
-            moving(9),
+            block(9),
             pl.BlockSpec(memory_space=pl.ANY),
         ],
         out_specs=(block(size), block(size), block(cells), block(cells)),
@@ -435,6 +430,22 @@
     )(which.reshape(1), *operands)
 
 
+def after_kernel(*refs):
+    pass
+
+
+def after(values, *others):
+    away = pl.BlockSpec(memory_space=pl.ANY)
+    return pl.pallas_call(
+        after_kernel,
+        out_shape=jax.ShapeDtypeStruct(values.shape, values.dtype),
+        in_specs=[away] * (1 + len(others)),
+        out_specs=away,
+        input_output_aliases={0: 0},
+        name="after",
+    )(values, *others)
+
+
 def sum_kernel(parts_ref, out_ref):
     out_ref[...] = summed(parts_ref, slice(None)).astype(BF16)
 
@@ -448,6 +459,7 @@
         out_shape=jax.ShapeDtypeStruct((rows, lane), BF16),
         in_specs=[pl.BlockSpec((count, block, lane), lambda step: (0, step, 0))],
         out_specs=pl.BlockSpec((block, lane), lambda step: (step, 0)),
+        compiler_params=pltpu.CompilerParams(vmem_limit_bytes=56 * 1024 * 1024),
         name="sum_bands",
     )(parts)
 
@@ -455,13 +467,13 @@
 def pack_kernel(
     left_ref, right_ref, mine_ref, theirs_ref, first_gain_ref, second_gain_ref, out_ref
 ):
+    depth = mine_ref[...] + theirs_ref[...]
     rows, lane = left_ref.shape[1:]
     out_ref[:, 0:rows, :] = (left_ref[...].astype(F32) + right_ref[...].astype(F32)).astype(BF16)
     small = []
-    for ref in (mine_ref, theirs_ref):
-        for z in range(ref.shape[0]):
-            for start in range(0, ref.shape[2], lane):
-                small.append(ref[z, :, start : start + lane])
+    for z in range(depth.shape[0]):
+        for start in range(0, depth.shape[2], lane):
+            small.append(depth[z, :, start : start + lane])
     for ref in (first_gain_ref, second_gain_ref):
         for start in range(0, ref.shape[1], lane):
             small.append(ref[:, start : start + lane])
@@ -477,7 +489,7 @@
     return total
 
 
-def merge_kernel(parts_ref, output_ref, input_ref, out_ref):
+def merge_kernel(parts_ref, output_ref, input_ref, out_ref, output_out, input_out):
     z_size, out_rows, _ = out_ref.shape
     rows = parts_ref.shape[1]
     block = (rows - out_rows) // (z_size - 1)
@@ -523,14 +535,13 @@
     for side in range(2):
         which = core if side == 0 else 1 - core
         for piece in range(pieces // 2):
-            own_at = side * half_rows + piece * 9
-            other_at = (1 - side) * half_rows + piece * 9
-            block = mine_ref[own_at : own_at + 9, :] + theirs_ref[other_at : other_at + 9, :]
+            source = mine_ref if side == 0 else theirs_ref
+            block = source[piece * 9 : piece * 9 + 9, :]
             z, rest = divmod(piece, in_block)
             start = pl.multiple_of((2 * z + which) * split, lane) + rest * lane
             for a in range(3):
                 depth_ref[a, :, pl.ds(pl.multiple_of(start, lane), lane)] = block[3 * a : 3 * a + 3]
-    at = 2 * half_rows
+    at = half_rows
     for ref in (first_gain_ref, second_gain_ref):
         for start in range(0, channels, lane):
             ref[:, start : start + lane] = mine_ref[at : at + 1, :] + theirs_ref[at : at + 1, :]
@@ -538,124 +549,141 @@
 
 
 def backward_kernel(
-    frame, norm_factor, which_ref, back_ref, state_ref, gain_ref, inside_ref, earlier_ref, order_ref,
-    shrink_ref, slope_ref, activated_ref, expand_ref, expand_slope_ref, kernel_ref, part_ref,
-    depth_ref, input_ref, gain_grad_ref, back_normed, normed,
-):
-    step = pl.program_id(0)
+    frame, norm_factor, stride, which_ref, *refs
+):
+    earlier_ref = refs[0] if len(refs) == 25 else None
+    (
+        back_ref, state_ref, gain_ref, kernel_ref, order_ref, shrink_hbm, slope_hbm,
+        expand_slope_hbm, expand_hbm, activated_hbm, part_hbm, depth_ref, input_ref, gain_grad_ref,
+        back_normed, shrink_all, slope_all, expand_slope_all, expand_all, activated_all, part_ref,
+        normed, arrived, sent,
+    ) = refs[-24:]
     cells, channels = state_ref.shape
     row_count, lon_count, _ = input_ref.shape
-    lat_size, _, _, lane = part_ref.shape
+    lat_size, steps, _, lane = part_ref.shape
+    part = slope_all.shape[2]
     block = channels // lat_size
-    inside = inside_ref[...]
-
-    @pl.when(step == 0)
-    def _():
-        normed[...] = normalise(state_ref[...].astype(F32), gain_ref[...]).T
-        back_normed[...] = earlier_ref[...]
-
-    kernel = kernel_ref[...]
-    back_convolved = (
-        (times_transpose(back_ref[...], shrink_ref[...]) * slope_ref[0].astype(F32))
-        .astype(BF16)
-        .astype(F32)
-    )
-    flipped = jnp.concatenate([kernel[8 - i : 9 - i] for i in range(9)], axis=0)
-    back_activated = convolve(back_convolved, flipped, row_count, frame)
-    back_expanded = jnp.where(inside > 0, back_activated * expand_slope_ref[0].astype(F32), 0.0).astype(BF16)
-    expand_grad = (matmul(normed[...], back_expanded) * norm_factor).astype(BF16)
-    for lat in range(lat_size):
-        for piece in range(expand_grad.shape[1] // lane):
-            part_ref[lat, 0, piece * block : (piece + 1) * block, :] = expand_grad[
-                lat * block : (lat + 1) * block, piece * lane : (piece + 1) * lane
+    copies = []
+    for step in range(steps):
+        place = stride * step + which_ref[0]
+        here = pl.ds(pl.multiple_of(place * part, part), part)
+        pairs = (
+            (shrink_hbm.at[here], shrink_all.at[step]),
+            (slope_hbm.at[place], slope_all.at[step]),
+            (expand_slope_hbm.at[place], expand_slope_all.at[step]),
+            (expand_hbm.at[:, here], expand_all.at[step]),
+            (activated_hbm.at[place], activated_all.at[step]),
+        )
+        copies.append(
+            [
+                pltpu.make_async_copy(source, target, arrived.at[step, i])
+                for i, (source, target) in enumerate(pairs)
             ]
-    back_normed[...] += times_transpose(back_expanded, expand_ref[...])
-    own_back = jnp.where(inside > 0, back_convolved[frame : frame + cells], 0.0)
-    activated = activated_ref[0].astype(F32)
-    for b in range(3):
-        moved = own_back
-        if b != 1:
-            moved = pltpu.roll(own_back, cells - 1 if b == 0 else 1, 0)
-        for a in range(3):
-            depth_ref[0, 3 * a + b : 3 * a + b + 1, :] = norm_factor * jnp.sum(
-                activated[a * frame : a * frame + cells] * moved, axis=0, keepdims=True
-            )
-
-    @pl.when(step == pl.num_programs(0) - 1)
-    def _():
-        state = state_ref[...].astype(F32)
-        inverse = inverse_rms(state)
-        grads = back_normed[...]
-        gain_grad_ref[...] = norm_factor * jnp.sum(grads * state * inverse, axis=0, keepdims=True)
-        result = (
-            back_ref[frame : frame + cells, :].astype(F32)
-            + norm_back(grads, state, inverse, gain_ref[...])
-        ).astype(BF16)
-        for row in range(row_count):
-            start = row * frame + SIDE
-            input_ref[row] = result[start : start + lon_count]
+        )
+        for copy in copies[step]:
+            copy.start()
+    column = lax.broadcasted_iota(jnp.int32, (frame, part), 0)
+    outside = (column < SIDE) | (column >= SIDE + lon_count)
+    outside = jnp.concatenate([outside] * row_count, axis=0)
+    normed[...] = normalise(state_ref[...].astype(F32), gain_ref[...]).T
+    sends = []
+    for step in range(steps):
+        place = stride * step + which_ref[0]
+        kernel = kernel_ref[place]
+        copies[step][0].wait()
+        copies[step][1].wait()
+        back_convolved = times_transpose(back_ref[...], shrink_all[step])
+        back_convolved = (back_convolved * slope_all[step].astype(F32)).astype(BF16).astype(F32)
+        flipped = jnp.concatenate([kernel[8 - i : 9 - i] for i in range(9)], axis=0)
+        back_activated = convolve(back_convolved, flipped, row_count, frame)
+        copies[step][2].wait()
+        back_expanded = back_activated * expand_slope_all[step].astype(F32)
+        back_expanded = jnp.where(outside, 0.0, back_expanded).astype(BF16)
+        expand_grad = (matmul(normed[...], back_expanded) * norm_factor).astype(BF16)
+        for lat in range(lat_size):
+            for piece in range(part // lane):
+                part_ref[lat, step, piece * block : (piece + 1) * block, :] = expand_grad[
+                    lat * block : (lat + 1) * block, piece * lane : (piece + 1) * lane
+                ]
+        sends.append(
+            pltpu.make_async_copy(part_ref.at[:, step], part_hbm.at[:, step], sent.at[step])
+        )
+        sends[step].start()
+        copies[step][3].wait()
+        product = times_transpose(back_expanded, expand_all[step])
+        if step > 0:
+            product = product + back_normed[...]
+        elif earlier_ref is not None:
+            product = product + earlier_ref[...]
+        back_normed[...] = product
+        own_back = jnp.where(outside, 0.0, back_convolved[frame : frame + cells])
+        copies[step][4].wait()
+        activated = activated_all[step].astype(F32)
+        for b in range(3):
+            moved = own_back
+            if b != 1:
+                moved = pltpu.roll(own_back, cells - 1 if b == 0 else 1, 0)
+            for a in range(3):
+                depth_ref[step, 3 * a + b : 3 * a + b + 1, :] = norm_factor * jnp.sum(
+                    activated[a * frame : a * frame + cells] * moved, axis=0, keepdims=True
+                )
+    state = state_ref[...].astype(F32)
+    inverse = inverse_rms(state)
+    grads = back_normed[...]
+    gain_grad_ref[...] = norm_factor * jnp.sum(grads * state * inverse, axis=0, keepdims=True)
+    result = (
+        back_ref[frame : frame + cells, :].astype(F32)
+        + norm_back(grads, state, inverse, gain_ref[...])
+    ).astype(BF16)
+    for row in range(row_count):
+        start = row * frame + SIDE
+        input_ref[row] = result[start : start + lon_count]
+    for send in sends:
+        send.wait()
 
 
 def backward(
-    which, back, state, gain, inside, earlier, order, shrink_weight, slope, activated, expand_weight,
+    which, back, state, gain, earlier, order, shrink_weight, slope, activated, expand_weight,
     expand_slope, kernel, norm_factor, lat_size, row_count, lon_count,
 ):
     cells, channels = state.shape
     frame = cells // row_count
-    size = activated.shape[1]
-    wide = expand_weight.shape[1]
-    part = step_width(wide)
-    steps = wide // part
-    place = lambda step, which: step
-    if which is not None:
-        steps = steps // 2
-        place = lambda step, which: 2 * step + which[0]
+    steps, size, part = activated.shape
+    stride = 1
+    if which is None:
+        which = 0
     else:
-        which = 0
-    fixed = lambda shape: pl.BlockSpec(shape, lambda step, which: (0,) * len(shape))
-    moving = lambda rows: pl.BlockSpec((rows, part), lambda step, which: (0, place(step, which)))
-    whole = lambda rows: pl.BlockSpec((1, rows, part), lambda step, which: (place(step, which), 0, 0))
+        steps, stride = steps // 2, 2
     block = channels // lat_size
     lane = block
-    pieces = part // lane
+    part_shape = (lat_size, steps, part // lane * block, lane)
+    here, away = pl.BlockSpec(memory_space=pltpu.VMEM), pl.BlockSpec(memory_space=pl.ANY)
+    operands = (back, state, gain, kernel)
+    if earlier is not None:
+        operands = (earlier,) + operands
     return pl.pallas_call(
-        functools.partial(backward_kernel, frame, norm_factor),
-        grid_spec=pltpu.PrefetchScalarGridSpec(
-            num_scalar_prefetch=1,
-            grid=(steps,),
-            in_specs=[
-                fixed((size, channels)),
-                fixed((cells, channels)),
-                fixed((1, channels)),
-                fixed((cells, 1)),
-                fixed((cells, channels)),
-                pl.BlockSpec(memory_space=pl.ANY),
-                pl.BlockSpec((part, channels), lambda step, which: (place(step, which), 0)),
-                whole(size),
-                whole(size),
-                moving(channels),
-                whole(cells),
-                moving(9),
-            ],
-            out_specs=(
-                pl.BlockSpec((lat_size, 1, pieces * block, lane), lambda step, which: (0, step, 0, 0)),
-                pl.BlockSpec((1, 9, part), lambda step, which: (step, 0, 0)),
-                fixed((row_count, lon_count, channels)),
-                fixed((1, channels)),
-                fixed((cells, channels)),
-            ),
-            scratch_shapes=[pltpu.VMEM((channels, cells), BF16)],
-        ),
+        functools.partial(backward_kernel, frame, norm_factor, stride),
+        in_specs=[pl.BlockSpec(memory_space=pltpu.SMEM)] + [here] * len(operands) + [away] * 6,
+        out_specs=(away,) + (here,) * 4,
+        scratch_shapes=[
+            pltpu.VMEM((steps, part, channels), BF16),
+            pltpu.VMEM((steps, size, part), BF16),
+            pltpu.VMEM((steps, cells, part), BF16),
+            pltpu.VMEM((steps, channels, part), BF16),
+            pltpu.VMEM((steps, size, part), BF16),
+            pltpu.VMEM(part_shape, BF16),
+            pltpu.VMEM((channels, cells), BF16),
+            pltpu.SemaphoreType.DMA((steps, 5)),
+            pltpu.SemaphoreType.DMA((steps,)),
+        ],
         out_shape=(
-            jax.ShapeDtypeStruct((lat_size, steps, pieces * block, lane), BF16),
+            jax.ShapeDtypeStruct(part_shape, BF16),
             jax.ShapeDtypeStruct((steps, 9, part), F32),
             jax.ShapeDtypeStruct((row_count, lon_count, channels), BF16),
             jax.ShapeDtypeStruct((1, channels), F32),
             jax.ShapeDtypeStruct((cells, channels), F32),
         ),
-        compiler_params=pltpu.CompilerParams(
-            vmem_limit_bytes=56 * 1024 * 1024, dimension_semantics=("arbitrary",)
-        ),
+        compiler_params=pltpu.CompilerParams(vmem_limit_bytes=56 * 1024 * 1024),
         cost_estimate=pl.CostEstimate(
             flops=8 * cells * channels * part * steps,
             bytes_accessed=(6 * channels + 12 * size) * part * steps,
@@ -663,8 +691,8 @@
         ),
         name="backward",
     )(
-        jnp.reshape(which, (1,)).astype(jnp.int32), back, state, gain, inside, earlier, order,
-        shrink_weight, slope, activated, expand_weight, expand_slope, kernel,
+        jnp.reshape(which, (1,)).astype(jnp.int32), *operands, order, shrink_weight, slope,
+        expand_slope, expand_weight, activated,
     )
 
 
@@ -836,6 +864,7 @@
     frame = lon_count + 2 * SIDE
     own = row_count * frame
     kernel = depth_weight.astype(F32).reshape(9, wide)
+    kernel_blocks = kernel.reshape(9, -1, step_width(wide)).transpose(1, 0, 2)
     input_gain = input_gain.reshape(1, channels)
     attention_gain = attention_gain.reshape(1, channels)
 
@@ -859,7 +888,7 @@
         groups,
     )
     activated, slope, mixed, expand_slope = around(
-        all_rows, input_gain, expand_weight, kernel, inner
+        all_rows, input_gain, expand_weight, kernel_blocks, inner
     )
     qkv = exchange(qkv, LON).reshape(lon_size * frame, 3 * width)
 
@@ -899,28 +928,26 @@
         lat_size, z_size,
     )
     theirs = grads(1 - core, back_sides, None)
-    first = grads(core, back, core_swap(theirs))
-    first_sums = sum_parts(exchange(first, "lat"), z_size)
+    first = after(grads(core, back_sides, core_swap(theirs)), below, above)
+    first_sums = sum_parts(exchange(first, "lat"), 2)
     first_sums = lax.psum_scatter(first_sums, "z", scatter_dimension=0, tiled=True)
     flat = lambda parts: parts.reshape(lat_size, -1, lane)
 
-    columns = lax.broadcasted_iota(jnp.int32, (row_count, frame, 1), 1).reshape(own, 1)
-    inside = ((columns >= SIDE) & (columns < SIDE + lon_count)).astype(F32)
     state = state.reshape(own, channels)
 
     def backward_part(which, earlier, order):
         return backward(
-            which, back, state, input_gain, inside, earlier, order, shrink_weight, slope, activated,
-            expand_weight, expand_slope, kernel, norm_factor, lat_size, row_count, lon_count,
+            which, back, state, input_gain, earlier, order, shrink_weight, slope, activated,
+            expand_weight, expand_slope, kernel_blocks, norm_factor, lat_size, row_count, lon_count,
         )
 
-    start = jnp.zeros((own, channels), F32)
     if split == step_width(wide):
-        theirs, depth_theirs, _, _, partial = backward_part(1 - core, start, first)
+        theirs, depth_theirs, _, _, partial = backward_part(1 - core, None, first)
         theirs = core_swap(theirs)
+        depth_theirs = core_swap(depth_theirs)
         mine, depth_mine, input_grad, gain_one, _ = backward_part(core, partial, first)
     else:
-        parts, depth, input_grad, gain_one, _ = backward_part(None, start, first)
+        parts, depth, input_grad, gain_one, _ = backward_part(None, None, first)
         steps = parts.shape[1]
         parts = parts.reshape(lat_size, steps, -1, split // lane, lane, lane)
         parts = parts.reshape(lat_size, z_size, 2, split // lane * lane, lane)
@@ -928,12 +955,12 @@
         mine = lax.dynamic_index_in_dim(parts, core, 2, False)
         depth = depth.reshape(steps, 9, -1, split).transpose(0, 2, 1, 3)
         depth = depth.reshape(z_size, 2, 9, split)
-        depth_theirs = lax.dynamic_index_in_dim(depth, 1 - core, 1, False)
+        depth_theirs = core_swap(lax.dynamic_index_in_dim(depth, 1 - core, 1, False))
         depth_mine = lax.dynamic_index_in_dim(depth, core, 1, False)
 
     mine, theirs = flat(mine), flat(theirs)
     block_rows = mine.shape[1] // z_size
-    small_rows = (9 * wide + 2 * channels) // lane
+    small_rows = (9 * wide // 2 + 2 * channels) // lane
     output_field = output_field.transpose(1, 0, 2)
     input_grad = input_grad.transpose(1, 0, 2)
     second = call(
@@ -947,14 +974,18 @@
         gain_one,
         gain_two,
     )
-    second = call(
+    field = jax.ShapeDtypeStruct(output_field.shape, BF16)
+    second, output_field, input_grad = call(
         merge_kernel,
         "merge",
-        jax.ShapeDtypeStruct((z_size, block_rows + small_rows, lane), BF16),
+        (jax.ShapeDtypeStruct((z_size, block_rows + small_rows, lane), BF16), field, field),
         exchange(second, "lat"),
         output_field,
         input_grad,
         specs=[pl.BlockSpec(memory_space=pltpu.VMEM)] + [pl.BlockSpec(memory_space=pl.ANY)] * 2,
+        out_specs=(pl.BlockSpec(memory_space=pltpu.VMEM),)
+        + (pl.BlockSpec(memory_space=pl.ANY),) * 2,
+        aliases={1: 1, 2: 2},
     )
     weight = lambda rows, cols: jax.ShapeDtypeStruct((rows, cols), F32)
     expand_grad, small = call(
@@ -977,18 +1008,18 @@
                 pl.BlockSpec(memory_space=pltpu.VMEM),
                 pl.BlockSpec(memory_space=pltpu.VMEM),
             ],
-            name="small_grads",
+            compiler_params=pltpu.CompilerParams(vmem_limit_bytes=56 * 1024 * 1024),
+        name="small_grads",
         )(core.reshape(1), small, other)
     else:
         rows = 9 * wide // 2 // lane
-        own_half = small[:rows] + other[rows : 2 * rows]
-        other_half = small[rows : 2 * rows] + other[:rows]
+        own_half, other_half = small[:rows], other[:rows]
         depth_grad = jnp.where(
             core == 0, jnp.stack([own_half, other_half]), jnp.stack([other_half, own_half])
         )
         depth_grad = depth_grad.reshape(2, z_size, split // lane, 9, lane).transpose(3, 1, 0, 2, 4)
         depth_grad = depth_grad.reshape(3, 3, wide)
-        gains = (small[2 * rows :] + other[2 * rows :]).reshape(2, channels)
+        gains = (small[rows:] + other[rows:]).reshape(2, channels)
         input_gain_grad, attention_gain_grad = gains[0], gains[1]
     shrink_grad, attention_in_grad, attention_out_grad = call(
         first_kernel,
@@ -999,6 +1030,7 @@
             weight(out_split, lane),
         ),
         first_sums,
+        megabytes=56,
     )
     return (
         output_field.transpose(1, 0, 2),

time: 200 us -> 193 us (0.965)
  waiting for transfers between devices: 30.1 us -> 26.5 us
  local copies, waits for them, and re-layouts: 21.7 us -> 18.2 us
    unnamed x71 -> x67, local copies, waits for them, and re-layouts: 19.6 us -> 15.3 us
    pallas_call x3 -> x4, Pallas kernels: 23.1 us -> 24.3 us  [the longest x2 16.5 us: backward(): pl.pallas_call(functools.partial(backward_kernel, frame, norm_factor, str...]
  transfers between devices with their start and end apart: 16 -> 17, of which waited for: 9 -> 9; matrix products, arithmetic and copies ran while one was open for 3% -> 3% of each run, Pallas kernels for 19% -> 21%
where the time goes in v4:
time: 193 us; the launch traced here: 191 us
  Pallas kernels  55.2 us (29%)
  blocking collectives  39.7 us (21%)
  starting transfers between devices  35.7 us (18%)
  waiting for transfers between devices  26.5 us (14%)
  local copies, waits for them, and re-layouts  18.2 us (9%)
  between operations  14.5 us (8%)
    all_to_all x2, blocking collectives, exchange(): return lax.all_to_all(values, axis, 0, 0, tiled=True)  39.7 us
    all_to_all x4, waiting for transfers between devices, exchange(): return lax.all_to_all(values, axis, 0, 0, tiled=True)  18 us
    pallas_call x2, Pallas kernels, backward(): pl.pallas_call(functools.partial(backward_kernel, frame, norm_factor, str...  16.5 us
    all_to_all x4, starting transfers between devices, exchange(): return lax.all_to_all(values, axis, 0, 0, tiled=True)  16.2 us
    unnamed x67, local copies, waits for them, and re-layouts  15.3 us
    pallas_call x1, Pallas kernels, attention(): pl.pallas_call(functools.partial(attention_kernel, head_width, query_bloc...  11.7 us
    ppermute x4, starting transfers between devices, from_sides(): lax.ppermute(lax.slice_in_dim(block, 0, width, axis=dim), axis, shifts(co...  10.2 us
    ppermute x4, starting transfers between devices, from_sides(): lax.ppermute(lax.slice_in_dim(block, size - width, size, axis=dim), axis,...  8.6 us
  transfers between devices with their start and end apart: 17, of which 9 were waited for; matrix products, arithmetic and copies ran while one was open for 3% of the time, Pallas kernels for 21%

profile of v4, /device:TPU:0, one launch (start us, length us, event | category | flops | bytes accessed | tf_op | source)
XLA Modules:
  0.0 191.5 jit_solution(8151254760178362836)
XLA Ops:
  8.7 4.1 %collective-permute-start.1 = (bf16[2,3,512]{2,1,0:T(4,128)(2,1)S(1)}, bf16[2,3,512]{2,1,0:T(4,128)(2,1)S(1)}, u32[]{:S(2)}, u32[]{:S(2)}) collective-permute-start(bf16[2,3,512]{2,1,0:T(4,128)(2,1)S(1)} %get-tuple-element.74), channel_id=1, source_target_pairs={{0,7},{1,0},{2,1},{3,2},{4,3},{5,4},{6,5},{7,6},{8,15},{9,8},{10,9... | collective-permute-start | bytes 18440 | tf_op jit(solution)/shard_map/ppermute | solution.py:44
  14.3 3.8 %collective-permute-start.2 = (bf16[2,96,512]{2,1,0:T(8,128)(2,1)S(1)}, bf16[2,96,512]{2,1,0:T(8,128)(2,1)S(1)}, u32[]{:S(2)}, u32[]{:S(2)}) collective-permute-start(bf16[2,96,512]{2,1,0:T(8,128)(2,1)S(1)} %pad_maximum_fusion.2.order_ref), channel_id=1, source_target_pairs={{0,8},{8,16},{16,24},{1,9},{9,17},{17,25},{2,10},{10,18},{18,26},{... | collective-permute-start | bytes 589832 | tf_op jit(solution)/shard_map/ppermute | solution.py:41
  22.4 4.5 %all-to-all-start.1 = ((bf16[8,112,128]{2,1,0:T(8,128)(2,1)}), bf16[8,112,128]{2,1,0:T(8,128)(2,1)S(1)}, u32[]{:S(2)}, u32[]{:S(2)}) async-start(bf16[8,112,128]{2,1,0:T(8,128)(2,1)} %get-tuple-element.40), calls=%async_computation.1 | async-start | bytes 458752 | tf_op jit(solution)/shard_map/all_to_all | solution.py:55
  29.6 7.8 %forward.1 = (bf16[8,96,384]{2,1,0:T(8,128)(2,1)}, bf16[192,512]{1,0:T(8,128)(2,1)}) custom-call(bf16[576,512]{1,0:T(8,128)(2,1)} %bitcast.31, f32[1,512]{1,0:T(1,128)} %bitcast.48, f32[9,2048]{1,0:T(8,128)} %reshape.74.kernel_ref, f32[1,512]{1,0:T(1,128)} %bitcast.44, bf16[512,2048]{1,0:T(8,128)(2,1)} %refs_9_.1, bf16[2048,512]{1,0:T(8,128)(2,1)} %refs_6_.1, ...), custom_call_target="tpu_custom_call" | custom-call | flops 1509949440 | bytes 5767168 | tf_op jit(solution)/shard_map/forward/pallas_call | solution.py:226
  37.4 4.3 %all-to-all-start = ((bf16[8,96,384]{2,1,0:T(8,128)(2,1)}), bf16[8,96,384]{2,1,0:T(8,128)(2,1)}, u32[]{:S(2)}, u32[]{:S(2)}) async-start(bf16[8,96,384]{2,1,0:T(8,128)(2,1)} %get-tuple-element.39), calls=%async_computation | async-start | bytes 1179648 | tf_op jit(solution)/shard_map/all_to_all | solution.py:55
  42.8 6.7 %forward_around.1 = (bf16[8,384,256]{2,1,0:T(8,128)(2,1)S(1)}, bf16[8,384,256]{2,1,0:T(8,128)(2,1)S(1)}, bf16[8,192,256]{2,1,0:T(8,128)(2,1)S(1)}, bf16[8,192,256]{2,1,0:T(8,128)(2,1)S(1)}) custom-call(bf16[576,512]{1,0:T(8,128)(2,1)S(1)} %bitcast.32, f32[1,512]{1,0:T(1,128)S(1)} %bitcast.51, bf16[512,2048]{1,0:T(8,128)(2,1)S(1)} %copy-done.1, ...), custom_call_target="tpu_custom_call" | custom-call | flops 1207959552 | bytes 13107200 | tf_op jit(solution)/shard_map/forward_around/pallas_call | solution.py:293
  53.4 5.1 %all-to-all-done = bf16[8,96,384]{2,1,0:T(8,128)(2,1)} async-done(((bf16[8,96,384]{2,1,0:T(8,128)(2,1)}), bf16[8,96,384]{2,1,0:T(8,128)(2,1)}, u32[]{:S(2)}, u32[]{:S(2)}) %all-to-all-start) | async-done | bytes 589856 | tf_op jit(solution)/shard_map/all_to_all | solution.py:55
  59.5 11.7 %attention.1 = bf16[768,512]{1,0:T(8,128)(2,1)S(1)} custom-call(bf16[768,384]{1,0:T(8,128)(2,1)} %bitcast.5.qkv_ref, bf16[8,112,128]{2,1,0:T(8,128)(2,1)S(1)} %copy-done.17, bf16[8,192,256]{2,1,0:T(8,128)(2,1)S(1)} %get-tuple-element.42.order_ref.mixed_ref), custom_call_target="tpu_custom_call" | custom-call | flops 1056964608 | bytes 1572864 | tf_op jit(solution)/shard_map/attention/pallas_call | solution.py:809
  71.2 23.5 %all_to_all.30.attended_ref = bf16[8,96,512]{2,1,0:T(8,128)(2,1)S(1)} all-to-all(bf16[8,96,512]{2,1,0:T(8,128)(2,1)S(1)} %bitcast.43), channel_id=1, replica_groups=mesh['lat'=4,'z'=4,'core'=2] {'z','core'}, dimensions={0} | all-to-all | bytes 1572864 | tf_op jit(solution)/shard_map/all_to_all | solution.py:55
  95.8 3.5 %collective-permute-start.5 = (bf16[2,1,512]{2,1,0:T(2,128)(2,1)S(1)}, bf16[2,1,512]{2,1,0:T(2,128)(2,1)S(1)}, u32[]{:S(2)}, u32[]{:S(2)}) collective-permute-start(bf16[2,1,512]{2,1,0:T(2,128)(2,1)S(1)} %get-tuple-element.71), channel_id=1, source_target_pairs={{0,7},{1,0},{2,1},{3,2},{4,3},{5,4},{6,5},{7,6},{8,15},{9,8},{10,9... | collective-permute-start | bytes 6152 | tf_op jit(solution)/shard_map/ppermute | solution.py:44
  101.0 1.4 weight_grads.2
  102.5 4.2 %collective-permute-start.6 = (bf16[1,96,512]{2,1,0:T(8,128)(2,1)S(1)}, bf16[1,96,512]{2,1,0:T(8,128)(2,1)S(1)}, u32[]{:S(2)}, u32[]{:S(2)}) collective-permute-start(bf16[1,96,512]{2,1,0:T(8,128)(2,1)S(1)} %get-tuple-element.69), channel_id=1, source_target_pairs={{0,8},{8,16},{16,24},{1,9},{9,17},{17,25},{2,10},{10,18},{18,26},{... | collective-permute-start | bytes 294920 | tf_op jit(solution)/shard_map/ppermute | solution.py:41
  108.0 1.4 weight_grads.3.refs_0_
  110.8 3.5 %collective-permute-done.7.refs_2_ = bf16[1,96,512]{2,1,0:T(8,128)(2,1)S(1)} collective-permute-done((bf16[1,96,512]{2,1,0:T(8,128)(2,1)S(1)}, bf16[1,96,512]{2,1,0:T(8,128)(2,1)S(1)}, u32[]{:S(2)}, u32[]{:S(2)}) %collective-permute-start.7) | collective-permute-done | bytes 98336 | tf_op jit(solution)/shard_map/ppermute | solution.py:44
  115.0 3.9 %all-to-all-start.5 = ((bf16[4,2048,128]{2,1,0:T(8,128)(2,1)}), bf16[4,2048,128]{2,1,0:T(8,128)(2,1)S(1)}, u32[]{:S(2)}, u32[]{:S(2)}) async-start(bf16[4,2048,128]{2,1,0:T(8,128)(2,1)} %after.1.refs_4_.refs_5_), calls=%async_computation.5 | async-start | bytes 4194304 | tf_op jit(solution)/shard_map/all_to_all | solution.py:55
  119.7 8.2 %backward.2 = (bf16[4,4,256,128]{3,2,1,0:T(8,128)(2,1)}, f32[4,9,256]{2,1,0:T(8,128)}, bf16[2,90,512]{2,1,0:T(8,128)(2,1)}, f32[1,512]{1,0:T(1,128)}, f32[192,512]{1,0:T(8,128)}) custom-call(s32[1]{0:T(128)} %bitcast.1.which_ref, bf16[384,512]{1,0:T(8,128)(2,1)} %bitcast.52, bf16[192,512]{1,0:T(8,128)(2,1)} %bitcast.29, f32[1,512]{1,0:T(1,128)} %bitcast.49, ...), custom_call_target="tpu_custom_call" | custom-call | flops 805306368 | bytes 7864320 | tf_op jit(solution)/shard_map/backward/pallas_call | solution.py:664
  128.4 8.3 %backward.3 = (bf16[4,4,256,128]{3,2,1,0:T(8,128)(2,1)}, f32[4,9,256]{2,1,0:T(8,128)}, bf16[2,90,512]{2,1,0:T(8,128)(2,1)}, f32[1,512]{1,0:T(1,128)}, f32[192,512]{1,0:T(8,128)}) custom-call(s32[1]{0:T(128)} %bitcast.which_ref.core_ref, f32[192,512]{1,0:T(8,128)} %get-tuple-element.49.refs_0_, bf16[384,512]{1,0:T(8,128)(2,1)} %bitcast.53, ...), custom_call_target="tpu_custom_call" | custom-call | flops 805306368 | bytes 7864320 | tf_op jit(solution)/shard_map/backward/pallas_call | solution.py:664
  140.8 3.3 %all-to-all-done.5.parts_ref = bf16[4,2048,128]{2,1,0:T(8,128)(2,1)S(1)} async-done(((bf16[4,2048,128]{2,1,0:T(8,128)(2,1)}), bf16[4,2048,128]{2,1,0:T(8,128)(2,1)S(1)}, u32[]{:S(2)}, u32[]{:S(2)}) %all-to-all-start.5) | async-done | bytes 2097184 | tf_op jit(solution)/shard_map/all_to_all | solution.py:55
  145.5 3.5 %all-to-all-start.3 = ((bf16[4,1104,128]{2,1,0:T(8,128)(2,1)}), bf16[4,1104,128]{2,1,0:T(8,128)(2,1)S(1)}, u32[]{:S(2)}, u32[]{:S(2)}) async-start(bf16[4,1104,128]{2,1,0:T(8,128)(2,1)} %pack.1), calls=%async_computation.3 | async-start | bytes 2260992 | tf_op jit(solution)/shard_map/all_to_all | solution.py:55
  149.0 2.4 %sum_bands.1 = bf16[2048,128]{1,0:T(8,128)(2,1)} custom-call(bf16[4,2048,128]{2,1,0:T(8,128)(2,1)} %copy-done.23), custom_call_target="tpu_custom_call" | custom-call | tf_op jit(solution)/shard_map/sum_bands/pallas_call | solution.py:456
  153.2 9.5 %all-to-all-done.3.parts_ref = bf16[4,1104,128]{2,1,0:T(8,128)(2,1)S(1)} async-done(((bf16[4,1104,128]{2,1,0:T(8,128)(2,1)}), bf16[4,1104,128]{2,1,0:T(8,128)(2,1)S(1)}, u32[]{:S(2)}, u32[]{:S(2)}) %all-to-all-start.3) | async-done | bytes 1130528 | tf_op jit(solution)/shard_map/all_to_all | solution.py:55
  162.9 16.1 %all_to_all.31.parts_ref = bf16[4,336,128]{2,1,0:T(8,128)(2,1)S(1)} all-to-all(bf16[4,336,128]{2,1,0:T(8,128)(2,1)S(1)} %get-tuple-element.60), channel_id=1, replica_groups=mesh['lat'=4,'z'=4,'core'=2] {'z'}, dimensions={0} | all-to-all | bytes 688128 | tf_op jit(solution)/shard_map/all_to_all | solution.py:55
  181.5 1.5 small_grads.1
  183.0 1.6 shrink_and_attention_grads.1
  (110 shorter events, 33.0 us)
Async XLA Ops:
  8.2 18.7 %copy-start.29 = (bf16[3,3,2048]{2,1,0:T(4,128)(2,1)S(1)}, bf16[3,3,2048]{2,1,0:T(4,128)(2,1)}, u32[]{:S(2)}) copy-start(bf16[3,3,2048]{2,1,0:T(4,128)(2,1)} %param.15) | copy-start | bytes 110596
  8.2 5.9 %collective-permute-start = (bf16[2,3,512]{2,1,0:T(4,128)(2,1)S(1)}, bf16[2,3,512]{2,1,0:T(4,128)(2,1)S(1)}, u32[]{:S(2)}, u32[]{:S(2)}) collective-permute-start(bf16[2,3,512]{2,1,0:T(4,128)(2,1)S(1)} %get-tuple-element.73), channel_id=1, source_target_pairs={{0,1},{1,2},{2,3},{3,4},{4,5},{5,6},{6,7},{7,0},{8,9},{9,10},{10,1... | collective-permute-start | bytes 18440 | tf_op jit(solution)/shard_map/ppermute | solution.py:41
  8.7 5.5 %collective-permute-start.1 = (bf16[2,3,512]{2,1,0:T(4,128)(2,1)S(1)}, bf16[2,3,512]{2,1,0:T(4,128)(2,1)S(1)}, u32[]{:S(2)}, u32[]{:S(2)}) collective-permute-start(bf16[2,3,512]{2,1,0:T(4,128)(2,1)S(1)} %get-tuple-element.74), channel_id=1, source_target_pairs={{0,7},{1,0},{2,1},{3,2},{4,3},{5,4},{6,5},{7,6},{8,15},{9,8},{10,9... | collective-permute-start | bytes 18440 | tf_op jit(solution)/shard_map/ppermute | solution.py:44
  14.3 15.3 %copy-start.6 = (bf16[2,96,512]{2,1,0:T(8,128)(2,1)}, bf16[2,96,512]{2,1,0:T(8,128)(2,1)S(1)}, u32[]{:S(2)}) copy-start(bf16[2,96,512]{2,1,0:T(8,128)(2,1)S(1)} %pad_maximum_fusion.2.order_ref) | copy-start | bytes 589828
  14.3 13.3 %collective-permute-start.2 = (bf16[2,96,512]{2,1,0:T(8,128)(2,1)S(1)}, bf16[2,96,512]{2,1,0:T(8,128)(2,1)S(1)}, u32[]{:S(2)}, u32[]{:S(2)}) collective-permute-start(bf16[2,96,512]{2,1,0:T(8,128)(2,1)S(1)} %pad_maximum_fusion.2.order_ref), channel_id=1, source_target_pairs={{0,8},{8,16},{16,24},{1,9},{9,17},{17,25},{2,10},{10,18},{18,26},{... | collective-permute-start | bytes 589832 | tf_op jit(solution)/shard_map/ppermute | solution.py:41
  18.1 10.5 %collective-permute-start.3 = (bf16[2,96,512]{2,1,0:T(8,128)(2,1)S(1)}, bf16[2,96,512]{2,1,0:T(8,128)(2,1)S(1)}, u32[]{:S(2)}, u32[]{:S(2)}) collective-permute-start(bf16[2,96,512]{2,1,0:T(8,128)(2,1)S(1)} %pad_maximum_fusion.2.order_ref), channel_id=1, source_target_pairs={{8,0},{16,8},{24,16},{9,1},{17,9},{25,17},{10,2},{18,10},{26,18},{... | collective-permute-start | bytes 589832 | tf_op jit(solution)/shard_map/ppermute | solution.py:44
  22.4 15.0 %all-to-all-start.1 = ((bf16[8,112,128]{2,1,0:T(8,128)(2,1)}), bf16[8,112,128]{2,1,0:T(8,128)(2,1)S(1)}, u32[]{:S(2)}, u32[]{:S(2)}) async-start(bf16[8,112,128]{2,1,0:T(8,128)(2,1)} %get-tuple-element.40), calls=%async_computation.1 | async-start | bytes 458752 | tf_op jit(solution)/shard_map/all_to_all | solution.py:55
  37.4 21.1 %all-to-all-start = ((bf16[8,96,384]{2,1,0:T(8,128)(2,1)}), bf16[8,96,384]{2,1,0:T(8,128)(2,1)}, u32[]{:S(2)}, u32[]{:S(2)}) async-start(bf16[8,96,384]{2,1,0:T(8,128)(2,1)} %get-tuple-element.39), calls=%async_computation | async-start | bytes 1179648 | tf_op jit(solution)/shard_map/all_to_all | solution.py:55
  59.5 35.2 %copy-start.9 = (bf16[512,512]{1,0:T(8,128)(2,1)S(1)}, bf16[512,512]{1,0:T(8,128)(2,1)}, u32[]{:S(2)}) copy-start(bf16[512,512]{1,0:T(8,128)(2,1)} %out_weight_ref.3) | copy-start | bytes 1572868
  59.5 35.2 %copy-start.11 = (bf16[2,96,512]{2,1,0:T(8,128)(2,1)S(1)}, bf16[2,96,512]{2,1,0:T(8,128)(2,1)}, u32[]{:S(2)}) copy-start(bf16[2,96,512]{2,1,0:T(8,128)(2,1)} %copy-done.10) | copy-start | bytes 589828
  59.5 35.2 %copy-start.13 = (bf16[192,512]{1,0:T(8,128)(2,1)S(1)}, bf16[192,512]{1,0:T(8,128)(2,1)}, u32[]{:S(2)}) copy-start(bf16[192,512]{1,0:T(8,128)(2,1)} %get-tuple-element.41.order_ref.inner_ref) | copy-start | bytes 589828
  71.2 23.6 %copy-start.4 = (bf16[512,1536]{1,0:T(8,128)(2,1)S(1)}, bf16[512,1536]{1,0:T(8,128)(2,1)}, u32[]{:S(2)}) copy-start(bf16[512,1536]{1,0:T(8,128)(2,1)} %in_weight_ref.1) | copy-start | bytes 4718596
  71.2 23.6 %copy-start.20 = (f32[512]{0:T(512)S(1)}, f32[512]{0:T(512)}, u32[]{:S(2)}) copy-start(f32[512]{0:T(512)} %param.17) | copy-start | bytes 6148
  95.7 4.9 %collective-permute-start.4 = (bf16[2,1,512]{2,1,0:T(2,128)(2,1)S(1)}, bf16[2,1,512]{2,1,0:T(2,128)(2,1)S(1)}, u32[]{:S(2)}, u32[]{:S(2)}) collective-permute-start(bf16[2,1,512]{2,1,0:T(2,128)(2,1)S(1)} %get-tuple-element.72), channel_id=1, source_target_pairs={{0,1},{1,2},{2,3},{3,4},{4,5},{5,6},{6,7},{7,0},{8,9},{9,10},{10,1... | collective-permute-start | bytes 6152 | tf_op jit(solution)/shard_map/ppermute | solution.py:41
  95.8 4.9 %collective-permute-start.5 = (bf16[2,1,512]{2,1,0:T(2,128)(2,1)S(1)}, bf16[2,1,512]{2,1,0:T(2,128)(2,1)S(1)}, u32[]{:S(2)}, u32[]{:S(2)}) collective-permute-start(bf16[2,1,512]{2,1,0:T(2,128)(2,1)S(1)} %get-tuple-element.71), channel_id=1, source_target_pairs={{0,7},{1,0},{2,1},{3,2},{4,3},{5,4},{6,5},{7,6},{8,15},{9,8},{10,9... | collective-permute-start | bytes 6152 | tf_op jit(solution)/shard_map/ppermute | solution.py:44
  102.4 5.6 %collective-permute-start.8 = (bf16[4,2048,128]{2,1,0:T(8,128)(2,1)S(1)}, bf16[4,2048,128]{2,1,0:T(8,128)(2,1)S(1)}, u32[]{:S(2)}, u32[]{:S(2)}) collective-permute-start(bf16[4,2048,128]{2,1,0:T(8,128)(2,1)S(1)} %weight_grads.2), channel_id=1, source_target_pairs={{0,1},{1,0},{2,3},{3,2},{4,5},{5,4},{6,7},{7,6},{8,9},{9,8},{10,11... | collective-permute-start | bytes 6291464 | tf_op jit(solution)/shard_map/ppermute | solution.py:51
  102.5 8.3 %collective-permute-start.6 = (bf16[1,96,512]{2,1,0:T(8,128)(2,1)S(1)}, bf16[1,96,512]{2,1,0:T(8,128)(2,1)S(1)}, u32[]{:S(2)}, u32[]{:S(2)}) collective-permute-start(bf16[1,96,512]{2,1,0:T(8,128)(2,1)S(1)} %get-tuple-element.69), channel_id=1, source_target_pairs={{0,8},{8,16},{16,24},{1,9},{9,17},{17,25},{2,10},{10,18},{18,26},{... | collective-permute-start | bytes 294920 | tf_op jit(solution)/shard_map/ppermute | solution.py:41
  106.7 7.6 %collective-permute-start.7 = (bf16[1,96,512]{2,1,0:T(8,128)(2,1)S(1)}, bf16[1,96,512]{2,1,0:T(8,128)(2,1)S(1)}, u32[]{:S(2)}, u32[]{:S(2)}) collective-permute-start(bf16[1,96,512]{2,1,0:T(8,128)(2,1)S(1)} %get-tuple-element.70), channel_id=1, source_target_pairs={{8,0},{16,8},{24,16},{9,1},{17,9},{25,17},{10,2},{18,10},{26,18},{... | collective-permute-start | bytes 294920 | tf_op jit(solution)/shard_map/ppermute | solution.py:44
  115.0 29.1 %all-to-all-start.5 = ((bf16[4,2048,128]{2,1,0:T(8,128)(2,1)}), bf16[4,2048,128]{2,1,0:T(8,128)(2,1)S(1)}, u32[]{:S(2)}, u32[]{:S(2)}) async-start(bf16[4,2048,128]{2,1,0:T(8,128)(2,1)} %after.1.refs_4_.refs_5_), calls=%async_computation.5 | async-start | bytes 4194304 | tf_op jit(solution)/shard_map/all_to_all | solution.py:55
  127.9 8.9 %collective-permute-start.9 = (bf16[4,4,256,128]{3,2,1,0:T(8,128)(2,1)}, bf16[4,4,256,128]{3,2,1,0:T(8,128)(2,1)S(1)}, u32[]{:S(2)}, u32[]{:S(2)}) collective-permute-start(bf16[4,4,256,128]{3,2,1,0:T(8,128)(2,1)} %get-tuple-element.51), channel_id=1, source_target_pairs={{0,1},{1,0},{2,3},{3,2},{4,5},{5,4},{6,7},{7,6},{8,9},{9,8},{10,11... | collective-permute-start | bytes 3145736 | tf_op jit(solution)/shard_map/ppermute | solution.py:51
  127.9 8.8 %collective-permute-start.10 = (f32[4,9,256]{2,1,0:T(8,128)}, f32[4,9,256]{2,1,0:T(8,128)S(1)}, u32[]{:S(2)}, u32[]{:S(2)}) collective-permute-start(f32[4,9,256]{2,1,0:T(8,128)} %get-tuple-element.53), channel_id=1, source_target_pairs={{0,1},{1,0},{2,3},{3,2},{4,5},{5,4},{6,7},{7,6},{8,9},{9,8},{10,11... | collective-permute-start | bytes 110600 | tf_op jit(solution)/shard_map/ppermute | solution.py:51
  145.5 17.3 %all-to-all-start.3 = ((bf16[4,1104,128]{2,1,0:T(8,128)(2,1)}), bf16[4,1104,128]{2,1,0:T(8,128)(2,1)S(1)}, u32[]{:S(2)}, u32[]{:S(2)}) async-start(bf16[4,1104,128]{2,1,0:T(8,128)(2,1)} %pack.1), calls=%async_computation.3 | async-start | bytes 2260992 | tf_op jit(solution)/shard_map/all_to_all | solution.py:55
  149.0 34.0 %reduce-scatter.2.cloned.1.call-start = ((), (), s32[]{:S(2)}) async-start(), calls=%async_computation.7 | async-start | bytes 655360 | tf_op jit(solution)/shard_map/reduce_scatter | solution.py:933
  179.7 1.2 collective-permute-start.11
  (25 other events, 81.3 us)
Sparse Core Ops, SparseCore 0:
  152.1 23.7 reduce-scatter.1

commit v5 on v4

--- a/solution.py
+++ b/solution.py
@@ -16,7 +16,7 @@
 MASKED = -1e30
 SIDE = 3
 BIAS_ROWS = 16
-FORWARD_WIDTH = 512
+FORWARD_WIDTH = 1024
 LOG2E = math.log2(math.e)
 
 
@@ -193,7 +193,8 @@
     for i, cols in enumerate(parts):
         expand_copies[i].wait()
         activated = silu(matmul(normed[...], expand_ref[:, cols])).astype(BF16).astype(F32)
-        mixed = silu(convolve(activated, kernel_ref[:, cols], rows, frame)).astype(BF16)
+        kernel = jnp.concatenate([kernel_ref[a, :, cols] for a in range(3)], axis=0).astype(F32)
+        mixed = silu(convolve(activated, kernel, rows, frame)).astype(BF16)
         shrink_copies[i].wait()
         product = matmul(mixed, shrink_ref[cols])
         total[...] = product if i == 0 else total[...] + product
@@ -450,18 +451,8 @@
     out_ref[...] = summed(parts_ref, slice(None)).astype(BF16)
 
 
-def sum_parts(parts, steps):
-    count, rows, lane = parts.shape
-    block = rows // steps
-    return pl.pallas_call(
-        sum_kernel,
-        grid=(steps,),
-        out_shape=jax.ShapeDtypeStruct((rows, lane), BF16),
-        in_specs=[pl.BlockSpec((count, block, lane), lambda step: (0, step, 0))],
-        out_specs=pl.BlockSpec((block, lane), lambda step: (step, 0)),
-        compiler_params=pltpu.CompilerParams(vmem_limit_bytes=56 * 1024 * 1024),
-        name="sum_bands",
-    )(parts)
+def sum_parts(parts):
+    return call(sum_kernel, "sum_bands", jax.ShapeDtypeStruct(parts.shape[1:], BF16), parts, megabytes=8)
 
 
 def pack_kernel(
@@ -499,31 +490,31 @@
         out_ref[z, block:, :] = small
 
 
-def first_kernel(parts_ref, shrink_ref, in_ref, out_ref):
-    lane = parts_ref.shape[1]
+def small_sum_kernel(parts_ref, small_ref):
+    rows = parts_ref.shape[1] - small_ref.shape[0]
+    small_ref[...] = summed(parts_ref, slice(rows, parts_ref.shape[1]))
+
+
+def finish_kernel(parts_ref, first_ref, expand_ref, shrink_ref, in_ref, out_ref):
+    block, split = expand_ref.shape
+    lane = parts_ref.shape[2]
+    for piece in range(split // lane):
+        expand_ref[:, piece * lane : (piece + 1) * lane] = summed(
+            parts_ref, slice(piece * block, (piece + 1) * block)
+        )
     in_split, out_split = in_ref.shape[0], out_ref.shape[0]
     at = in_split + out_split
-    in_ref[...] = parts_ref[0:in_split, :].astype(F32)
-    out_ref[...] = parts_ref[in_split:at, :].astype(F32)
+    in_ref[...] = first_ref[0:in_split, :].astype(F32)
+    out_ref[...] = first_ref[in_split:at, :].astype(F32)
     for piece in range(shrink_ref.shape[1] // lane):
-        shrink_ref[:, piece * lane : (piece + 1) * lane] = parts_ref[at : at + out_split, :].astype(
+        shrink_ref[:, piece * lane : (piece + 1) * lane] = first_ref[at : at + out_split, :].astype(
             F32
         )
         at += out_split
 
 
-def second_kernel(parts_ref, expand_ref, small_ref):
-    block, split = expand_ref.shape
-    lane = parts_ref.shape[2]
-    at = 0
-    for piece in range(split // lane):
-        expand_ref[:, piece * lane : (piece + 1) * lane] = summed(parts_ref, slice(at, at + block))
-        at += block
-    small_ref[...] = summed(parts_ref, slice(at, parts_ref.shape[1]))
-
-
 def small_kernel(
-    split, core_ref, mine_ref, theirs_ref, depth_ref, first_gain_ref, second_gain_ref
+    split, core_ref, mine_ref, theirs_ref, order_ref, depth_ref, first_gain_ref, second_gain_ref
 ):
     lane = mine_ref.shape[1]
     wide = depth_ref.shape[2]
@@ -884,7 +875,8 @@
     early = exchange(early, LON)
 
     qkv, inner = forward(
-        all_rows, input_gain, expand_weight, kernel, shrink_weight, attention_gain, attention_in,
+        all_rows, input_gain, expand_weight, depth_weight, shrink_weight, attention_gain,
+        attention_in,
         groups,
     )
     activated, slope, mixed, expand_slope = around(
@@ -929,7 +921,7 @@
     )
     theirs = grads(1 - core, back_sides, None)
     first = after(grads(core, back_sides, core_swap(theirs)), below, above)
-    first_sums = sum_parts(exchange(first, "lat"), 2)
+    first_sums = sum_parts(exchange(first, "lat"))
     first_sums = lax.psum_scatter(first_sums, "z", scatter_dimension=0, tiled=True)
     flat = lambda parts: parts.reshape(lat_size, -1, lane)
 
@@ -973,6 +965,7 @@
         depth_theirs,
         gain_one,
         gain_two,
+        megabytes=56,
     )
     field = jax.ShapeDtypeStruct(output_field.shape, BF16)
     second, output_field, input_grad = call(
@@ -988,11 +981,19 @@
         aliases={1: 1, 2: 2},
     )
     weight = lambda rows, cols: jax.ShapeDtypeStruct((rows, cols), F32)
-    expand_grad, small = call(
-        second_kernel,
-        "expand_grad",
-        (weight(lane, split), weight(small_rows, lane)),
-        exchange(second, "z"),
+    second = exchange(second, "z")
+    small = call(small_sum_kernel, "small_sums", weight(small_rows, lane), second)
+    expand_grad, shrink_grad, attention_in_grad, attention_out_grad = call(
+        finish_kernel,
+        "finish",
+        (
+            weight(lane, split),
+            weight(out_split, wide // lat_size),
+            weight(in_split, lane),
+            weight(out_split, lane),
+        ),
+        second,
+        first_sums,
     )
     other = core_swap(small)
     if split % 128 == 0:
@@ -1007,10 +1008,10 @@
                 pl.BlockSpec(memory_space=pltpu.SMEM),
                 pl.BlockSpec(memory_space=pltpu.VMEM),
                 pl.BlockSpec(memory_space=pltpu.VMEM),
+                pl.BlockSpec(memory_space=pl.ANY),
             ],
-            compiler_params=pltpu.CompilerParams(vmem_limit_bytes=56 * 1024 * 1024),
         name="small_grads",
-        )(core.reshape(1), small, other)
+        )(core.reshape(1), small, other, attention_out_grad)
     else:
         rows = 9 * wide // 2 // lane
         own_half, other_half = small[:rows], other[:rows]
@@ -1021,17 +1022,6 @@
         depth_grad = depth_grad.reshape(3, 3, wide)
         gains = (small[rows:] + other[rows:]).reshape(2, channels)
         input_gain_grad, attention_gain_grad = gains[0], gains[1]
-    shrink_grad, attention_in_grad, attention_out_grad = call(
-        first_kernel,
-        "shrink_and_attention_grads",
-        (
-            weight(out_split, wide // lat_size),
-            weight(in_split, lane),
-            weight(out_split, lane),
-        ),
-        first_sums,
-        megabytes=56,
-    )
     return (
         output_field.transpose(1, 0, 2),
         input_grad.transpose(1, 0, 2),

time: 193 us -> 188 us (0.974)
  Pallas kernels: 55.2 us -> 52.6 us
  local copies, waits for them, and re-layouts: 18.2 us -> 15.9 us
    unnamed x67 -> x65, local copies, waits for them, and re-layouts: 15.3 us -> 12.7 us
    pallas_call x1 -> x0, Pallas kernels: 2.44 us -> none  [sum_parts(): pl.pallas_call(sum_kernel, grid=(steps,), out_shape=jax.ShapeDtypeStruct(...]
    pallas_call x6 -> x7, Pallas kernels: 5.81 us -> 6.08 us  [call(): pl.pallas_call(kernel, out_shape=out_shape, scratch_shapes=scratch, in_sp...]
  transfers between devices with their start and end apart: 17 -> 17, of which waited for: 9 -> 8; matrix products, arithmetic and copies ran while one was open for 3% -> 3% of each run, Pallas kernels for 21% -> 20%
where the time goes in v5:
time: 188 us; the launch traced here: 187 us
  Pallas kernels  52.6 us (28%)
  blocking collectives  39.8 us (21%)
  starting transfers between devices  35.2 us (19%)
  waiting for transfers between devices  27.2 us (14%)
  local copies, waits for them, and re-layouts  15.9 us (8%)
  between operations  14.6 us (8%)
    all_to_all x2, blocking collectives, exchange(): return lax.all_to_all(values, axis, 0, 0, tiled=True)  39.8 us
    all_to_all x4, waiting for transfers between devices, exchange(): return lax.all_to_all(values, axis, 0, 0, tiled=True)  19.2 us
    pallas_call x2, Pallas kernels, backward(): pl.pallas_call(functools.partial(backward_kernel, frame, norm_factor, str...  16.5 us
    all_to_all x4, starting transfers between devices, exchange(): return lax.all_to_all(values, axis, 0, 0, tiled=True)  16.2 us
    unnamed x65, local copies, waits for them, and re-layouts  12.7 us
    pallas_call x1, Pallas kernels, attention(): pl.pallas_call(functools.partial(attention_kernel, head_width, query_bloc...  11.7 us
    ppermute x4, starting transfers between devices, from_sides(): lax.ppermute(lax.slice_in_dim(block, 0, width, axis=dim), axis, shifts(co...  10.4 us
    ppermute x4, starting transfers between devices, from_sides(): lax.ppermute(lax.slice_in_dim(block, size - width, size, axis=dim), axis,...  7.8 us
  transfers between devices with their start and end apart: 17, of which 8 were waited for; matrix products, arithmetic and copies ran while one was open for 3% of the time, Pallas kernels for 20%

profile of v5, /device:TPU:0, one launch (start us, length us, event | category | flops | bytes accessed | tf_op | source)
XLA Modules:
  0.0 187.1 jit_solution(11742950811772460326)
XLA Ops:
  8.7 4.1 %collective-permute-start.1 = (bf16[2,3,512]{2,1,0:T(4,128)(2,1)S(1)}, bf16[2,3,512]{2,1,0:T(4,128)(2,1)S(1)}, u32[]{:S(2)}, u32[]{:S(2)}) collective-permute-start(bf16[2,3,512]{2,1,0:T(4,128)(2,1)S(1)} %get-tuple-element.72), channel_id=1, source_target_pairs={{0,7},{1,0},{2,1},{3,2},{4,3},{5,4},{6,5},{7,6},{8,15},{9,8},{10,9... | collective-permute-start | bytes 18440 | tf_op jit(solution)/shard_map/ppermute | solution.py:44
  14.3 3.8 %collective-permute-start.2 = (bf16[2,96,512]{2,1,0:T(8,128)(2,1)S(1)}, bf16[2,96,512]{2,1,0:T(8,128)(2,1)S(1)}, u32[]{:S(2)}, u32[]{:S(2)}) collective-permute-start(bf16[2,96,512]{2,1,0:T(8,128)(2,1)S(1)} %pad_maximum_fusion.2.order_ref), channel_id=1, source_target_pairs={{0,8},{8,16},{16,24},{1,9},{9,17},{17,25},{2,10},{10,18},{18,26},{... | collective-permute-start | bytes 589832 | tf_op jit(solution)/shard_map/ppermute | solution.py:41
  21.7 4.5 %all-to-all-start.1 = ((bf16[8,112,128]{2,1,0:T(8,128)(2,1)}), bf16[8,112,128]{2,1,0:T(8,128)(2,1)S(1)}, u32[]{:S(2)}, u32[]{:S(2)}) async-start(bf16[8,112,128]{2,1,0:T(8,128)(2,1)} %get-tuple-element.39), calls=%async_computation.1 | async-start | bytes 458752 | tf_op jit(solution)/shard_map/all_to_all | solution.py:55
  26.2 2.5 %collective-permute-done.3 = bf16[2,96,512]{2,1,0:T(8,128)(2,1)S(1)} collective-permute-done((bf16[2,96,512]{2,1,0:T(8,128)(2,1)S(1)}, bf16[2,96,512]{2,1,0:T(8,128)(2,1)S(1)}, u32[]{:S(2)}, u32[]{:S(2)}) %collective-permute-start.3) | collective-permute-done | bytes 196640 | tf_op jit(solution)/shard_map/ppermute | solution.py:44
  29.6 7.4 %forward.1 = (bf16[8,96,384]{2,1,0:T(8,128)(2,1)}, bf16[192,512]{1,0:T(8,128)(2,1)}) custom-call(bf16[576,512]{1,0:T(8,128)(2,1)} %bitcast.31, f32[1,512]{1,0:T(1,128)} %bitcast.46, bf16[3,3,2048]{2,1,0:T(4,128)(2,1)} %kernel_ref.1, f32[1,512]{1,0:T(1,128)} %bitcast.42, bf16[512,2048]{1,0:T(8,128)(2,1)} %refs_9_.1, bf16[2048,512]{1,0:T(8,128)(2,1)} %refs_6_.1, ...), custom_call_target="tpu_custom_call" | custom-call | flops 1509949440 | bytes 5767168 | tf_op jit(solution)/shard_map/forward/pallas_call | solution.py:227
  37.0 4.3 %all-to-all-start = ((bf16[8,96,384]{2,1,0:T(8,128)(2,1)}), bf16[8,96,384]{2,1,0:T(8,128)(2,1)}, u32[]{:S(2)}, u32[]{:S(2)}) async-start(bf16[8,96,384]{2,1,0:T(8,128)(2,1)} %get-tuple-element.38), calls=%async_computation | async-start | bytes 1179648 | tf_op jit(solution)/shard_map/all_to_all | solution.py:55
  42.6 6.7 %forward_around.1 = (bf16[8,384,256]{2,1,0:T(8,128)(2,1)S(1)}, bf16[8,384,256]{2,1,0:T(8,128)(2,1)S(1)}, bf16[8,192,256]{2,1,0:T(8,128)(2,1)S(1)}, bf16[8,192,256]{2,1,0:T(8,128)(2,1)S(1)}) custom-call(bf16[576,512]{1,0:T(8,128)(2,1)S(1)} %bitcast.32, f32[1,512]{1,0:T(1,128)S(1)} %bitcast.49, bf16[512,2048]{1,0:T(8,128)(2,1)S(1)} %copy-done.1, ...), custom_call_target="tpu_custom_call" | custom-call | flops 1207959552 | bytes 13107200 | tf_op jit(solution)/shard_map/forward_around/pallas_call | solution.py:294
  52.6 5.5 %all-to-all-done = bf16[8,96,384]{2,1,0:T(8,128)(2,1)} async-done(((bf16[8,96,384]{2,1,0:T(8,128)(2,1)}), bf16[8,96,384]{2,1,0:T(8,128)(2,1)}, u32[]{:S(2)}, u32[]{:S(2)}) %all-to-all-start) | async-done | bytes 589856 | tf_op jit(solution)/shard_map/all_to_all | solution.py:55
  59.1 11.7 %attention.1 = bf16[768,512]{1,0:T(8,128)(2,1)S(1)} custom-call(bf16[768,384]{1,0:T(8,128)(2,1)} %bitcast.5.qkv_ref, bf16[8,112,128]{2,1,0:T(8,128)(2,1)S(1)} %copy-done.14, bf16[8,192,256]{2,1,0:T(8,128)(2,1)S(1)} %get-tuple-element.41.order_ref.mixed_ref), custom_call_target="tpu_custom_call" | custom-call | flops 1056964608 | bytes 1572864 | tf_op jit(solution)/shard_map/attention/pallas_call | solution.py:800
  70.8 23.5 %all_to_all.30.attended_ref = bf16[8,96,512]{2,1,0:T(8,128)(2,1)S(1)} all-to-all(bf16[8,96,512]{2,1,0:T(8,128)(2,1)S(1)} %bitcast.41), channel_id=1, replica_groups=mesh['lat'=4,'z'=4,'core'=2] {'z','core'}, dimensions={0} | all-to-all | bytes 1572864 | tf_op jit(solution)/shard_map/all_to_all | solution.py:55
  95.4 3.5 %collective-permute-start.5 = (bf16[2,1,512]{2,1,0:T(2,128)(2,1)S(1)}, bf16[2,1,512]{2,1,0:T(2,128)(2,1)S(1)}, u32[]{:S(2)}, u32[]{:S(2)}) collective-permute-start(bf16[2,1,512]{2,1,0:T(2,128)(2,1)S(1)} %get-tuple-element.69), channel_id=1, source_target_pairs={{0,7},{1,0},{2,1},{3,2},{4,3},{5,4},{6,5},{7,6},{8,15},{9,8},{10,9... | collective-permute-start | bytes 6152 | tf_op jit(solution)/shard_map/ppermute | solution.py:44
  102.1 3.4 %collective-permute-start.6 = (bf16[1,96,512]{2,1,0:T(8,128)(2,1)S(1)}, bf16[1,96,512]{2,1,0:T(8,128)(2,1)S(1)}, u32[]{:S(2)}, u32[]{:S(2)}) collective-permute-start(bf16[1,96,512]{2,1,0:T(8,128)(2,1)S(1)} %get-tuple-element.67), channel_id=1, source_target_pairs={{0,8},{8,16},{16,24},{1,9},{9,17},{17,25},{2,10},{10,18},{18,26},{... | collective-permute-start | bytes 294920 | tf_op jit(solution)/shard_map/ppermute | solution.py:41
  105.5 1.5 collective-permute-start.7
  109.8 2.8 %collective-permute-done.7.refs_2_ = bf16[1,96,512]{2,1,0:T(8,128)(2,1)S(1)} collective-permute-done((bf16[1,96,512]{2,1,0:T(8,128)(2,1)S(1)}, bf16[1,96,512]{2,1,0:T(8,128)(2,1)S(1)}, u32[]{:S(2)}, u32[]{:S(2)}) %collective-permute-start.7) | collective-permute-done | bytes 98336 | tf_op jit(solution)/shard_map/ppermute | solution.py:44
  113.2 3.9 %all-to-all-start.5 = ((bf16[4,2048,128]{2,1,0:T(8,128)(2,1)}), bf16[4,2048,128]{2,1,0:T(8,128)(2,1)S(1)}, u32[]{:S(2)}, u32[]{:S(2)}) async-start(bf16[4,2048,128]{2,1,0:T(8,128)(2,1)} %after.1.refs_4_.refs_5_), calls=%async_computation.5 | async-start | bytes 4194304 | tf_op jit(solution)/shard_map/all_to_all | solution.py:55
  117.9 8.2 %backward.2 = (bf16[4,4,256,128]{3,2,1,0:T(8,128)(2,1)}, f32[4,9,256]{2,1,0:T(8,128)}, bf16[2,90,512]{2,1,0:T(8,128)(2,1)}, f32[1,512]{1,0:T(1,128)}, f32[192,512]{1,0:T(8,128)}) custom-call(s32[1]{0:T(128)} %bitcast.1.which_ref, bf16[384,512]{1,0:T(8,128)(2,1)} %bitcast.50, bf16[192,512]{1,0:T(8,128)(2,1)} %bitcast.29, f32[1,512]{1,0:T(1,128)} %bitcast.47, ...), custom_call_target="tpu_custom_call" | custom-call | flops 805306368 | bytes 7864320 | tf_op jit(solution)/shard_map/backward/pallas_call | solution.py:655
  126.7 8.3 %backward.3 = (bf16[4,4,256,128]{3,2,1,0:T(8,128)(2,1)}, f32[4,9,256]{2,1,0:T(8,128)}, bf16[2,90,512]{2,1,0:T(8,128)(2,1)}, f32[1,512]{1,0:T(1,128)}, f32[192,512]{1,0:T(8,128)}) custom-call(s32[1]{0:T(128)} %bitcast.which_ref.core_ref, f32[192,512]{1,0:T(8,128)} %get-tuple-element.48.refs_0_, bf16[384,512]{1,0:T(8,128)(2,1)} %bitcast.51, ...), custom_call_target="tpu_custom_call" | custom-call | flops 805306368 | bytes 7864320 | tf_op jit(solution)/shard_map/backward/pallas_call | solution.py:655
  136.0 2.8 %pack.1 = bf16[4,1104,128]{2,1,0:T(8,128)(2,1)} custom-call(bf16[4,1024,128]{2,1,0:T(8,128)(2,1)} %bitcast.53, bf16[4,1024,128]{2,1,0:T(8,128)(2,1)} %bitcast.52, f32[4,9,256]{2,1,0:T(8,128)} %get-tuple-element.51.mine_ref, f32[4,9,256]{2,1,0:T(8,128)} %copy-done.28, f32[1,512]{1,0:T(1,128)} %get-tuple-element.53.first_gain_ref, f32[1,512]{1,0:T(1,128)} %copy-done.21), custom_call_target="tpu_custom_call" | custom-call | bytes 2174976 | tf_op jit(solution)/shard_map/pack/pallas_call | solution.py:77
  138.9 3.5 %all-to-all-done.5.parts_ref = bf16[4,2048,128]{2,1,0:T(8,128)(2,1)S(1)} async-done(((bf16[4,2048,128]{2,1,0:T(8,128)(2,1)}), bf16[4,2048,128]{2,1,0:T(8,128)(2,1)S(1)}, u32[]{:S(2)}, u32[]{:S(2)}) %all-to-all-start.5) | async-done | bytes 2097184 | tf_op jit(solution)/shard_map/all_to_all | solution.py:55
  142.3 3.5 %all-to-all-start.3 = ((bf16[4,1104,128]{2,1,0:T(8,128)(2,1)}), bf16[4,1104,128]{2,1,0:T(8,128)(2,1)S(1)}, u32[]{:S(2)}, u32[]{:S(2)}) async-start(bf16[4,1104,128]{2,1,0:T(8,128)(2,1)} %pack.1), calls=%async_computation.3 | async-start | bytes 2260992 | tf_op jit(solution)/shard_map/all_to_all | solution.py:55
  147.9 1.8 copy.40
  149.7 10.2 %all-to-all-done.3.parts_ref = bf16[4,1104,128]{2,1,0:T(8,128)(2,1)S(1)} async-done(((bf16[4,1104,128]{2,1,0:T(8,128)(2,1)}), bf16[4,1104,128]{2,1,0:T(8,128)(2,1)S(1)}, u32[]{:S(2)}, u32[]{:S(2)}) %all-to-all-start.3) | async-done | bytes 1130528 | tf_op jit(solution)/shard_map/all_to_all | solution.py:55
  160.1 16.3 %all_to_all.31.parts_ref = bf16[4,336,128]{2,1,0:T(8,128)(2,1)S(1)} all-to-all(bf16[4,336,128]{2,1,0:T(8,128)(2,1)S(1)} %get-tuple-element.59), channel_id=1, replica_groups=mesh['lat'=4,'z'=4,'core'=2] {'z'}, dimensions={0} | all-to-all | bytes 688128 | tf_op jit(solution)/shard_map/all_to_all | solution.py:55
  178.7 1.5 small_grads.1
  (107 shorter events, 27.2 us)
Async XLA Ops:
  7.2 13.2 %copy-start.30 = (bf16[2,90,16]{1,2,0:T(8,128)(2,1)S(1)}, bf16[2,90,16]{1,2,0:T(8,128)(2,1)}, u32[]{:S(2)}) copy-start(bf16[2,90,16]{1,2,0:T(8,128)(2,1)} %param.12) | copy-start | bytes 17284
  7.2 13.3 %copy-start.9 = (bf16[512,512]{1,0:T(8,128)(2,1)S(1)}, bf16[512,512]{1,0:T(8,128)(2,1)}, u32[]{:S(2)}) copy-start(bf16[512,512]{1,0:T(8,128)(2,1)} %out_weight_ref.3) | copy-start | bytes 1572868
  8.2 5.9 %collective-permute-start = (bf16[2,3,512]{2,1,0:T(4,128)(2,1)S(1)}, bf16[2,3,512]{2,1,0:T(4,128)(2,1)S(1)}, u32[]{:S(2)}, u32[]{:S(2)}) collective-permute-start(bf16[2,3,512]{2,1,0:T(4,128)(2,1)S(1)} %get-tuple-element.71), channel_id=1, source_target_pairs={{0,1},{1,2},{2,3},{3,4},{4,5},{5,6},{6,7},{7,0},{8,9},{9,10},{10,1... | collective-permute-start | bytes 18440 | tf_op jit(solution)/shard_map/ppermute | solution.py:41
  8.7 5.5 %collective-permute-start.1 = (bf16[2,3,512]{2,1,0:T(4,128)(2,1)S(1)}, bf16[2,3,512]{2,1,0:T(4,128)(2,1)S(1)}, u32[]{:S(2)}, u32[]{:S(2)}) collective-permute-start(bf16[2,3,512]{2,1,0:T(4,128)(2,1)S(1)} %get-tuple-element.72), channel_id=1, source_target_pairs={{0,7},{1,0},{2,1},{3,2},{4,3},{5,4},{6,5},{7,6},{8,15},{9,8},{10,9... | collective-permute-start | bytes 18440 | tf_op jit(solution)/shard_map/ppermute | solution.py:44
  14.3 15.3 %copy-start.6 = (bf16[2,96,512]{2,1,0:T(8,128)(2,1)}, bf16[2,96,512]{2,1,0:T(8,128)(2,1)S(1)}, u32[]{:S(2)}) copy-start(bf16[2,96,512]{2,1,0:T(8,128)(2,1)S(1)} %pad_maximum_fusion.2.order_ref) | copy-start | bytes 589828
  14.3 11.9 %collective-permute-start.2 = (bf16[2,96,512]{2,1,0:T(8,128)(2,1)S(1)}, bf16[2,96,512]{2,1,0:T(8,128)(2,1)S(1)}, u32[]{:S(2)}, u32[]{:S(2)}) collective-permute-start(bf16[2,96,512]{2,1,0:T(8,128)(2,1)S(1)} %pad_maximum_fusion.2.order_ref), channel_id=1, source_target_pairs={{0,8},{8,16},{16,24},{1,9},{9,17},{17,25},{2,10},{10,18},{18,26},{... | collective-permute-start | bytes 589832 | tf_op jit(solution)/shard_map/ppermute | solution.py:41
  18.1 10.5 %collective-permute-start.3 = (bf16[2,96,512]{2,1,0:T(8,128)(2,1)S(1)}, bf16[2,96,512]{2,1,0:T(8,128)(2,1)S(1)}, u32[]{:S(2)}, u32[]{:S(2)}) collective-permute-start(bf16[2,96,512]{2,1,0:T(8,128)(2,1)S(1)} %pad_maximum_fusion.2.order_ref), channel_id=1, source_target_pairs={{8,0},{16,8},{24,16},{9,1},{17,9},{25,17},{10,2},{18,10},{26,18},{... | collective-permute-start | bytes 589832 | tf_op jit(solution)/shard_map/ppermute | solution.py:44
  21.7 15.3 %all-to-all-start.1 = ((bf16[8,112,128]{2,1,0:T(8,128)(2,1)}), bf16[8,112,128]{2,1,0:T(8,128)(2,1)S(1)}, u32[]{:S(2)}, u32[]{:S(2)}) async-start(bf16[8,112,128]{2,1,0:T(8,128)(2,1)} %get-tuple-element.39), calls=%async_computation.1 | async-start | bytes 458752 | tf_op jit(solution)/shard_map/all_to_all | solution.py:55
  29.6 11.9 %copy-start.1 = (bf16[512,2048]{1,0:T(8,128)(2,1)S(1)}, bf16[512,2048]{1,0:T(8,128)(2,1)}, u32[]{:S(2)}) copy-start(bf16[512,2048]{1,0:T(8,128)(2,1)} %refs_9_.1) | copy-start | bytes 6291460
  37.0 21.1 %all-to-all-start = ((bf16[8,96,384]{2,1,0:T(8,128)(2,1)}), bf16[8,96,384]{2,1,0:T(8,128)(2,1)}, u32[]{:S(2)}, u32[]{:S(2)}) async-start(bf16[8,96,384]{2,1,0:T(8,128)(2,1)} %get-tuple-element.38), calls=%async_computation | async-start | bytes 1179648 | tf_op jit(solution)/shard_map/all_to_all | solution.py:55
  59.1 35.2 %copy-start.10 = (bf16[512,512]{1,0:T(8,128)(2,1)S(1)}, bf16[512,512]{1,0:T(8,128)(2,1)}, u32[]{:S(2)}) copy-start(bf16[512,512]{1,0:T(8,128)(2,1)} %out_weight_ref.3) | copy-start | bytes 1572868
  70.8 23.6 %copy-start.4 = (bf16[512,1536]{1,0:T(8,128)(2,1)S(1)}, bf16[512,1536]{1,0:T(8,128)(2,1)}, u32[]{:S(2)}) copy-start(bf16[512,1536]{1,0:T(8,128)(2,1)} %in_weight_ref.1) | copy-start | bytes 4718596
  70.8 23.5 %copy-start.19 = (f32[512]{0:T(512)S(1)}, f32[512]{0:T(512)}, u32[]{:S(2)}) copy-start(f32[512]{0:T(512)} %param.17) | copy-start | bytes 6148
  95.3 4.9 %collective-permute-start.4 = (bf16[2,1,512]{2,1,0:T(2,128)(2,1)S(1)}, bf16[2,1,512]{2,1,0:T(2,128)(2,1)S(1)}, u32[]{:S(2)}, u32[]{:S(2)}) collective-permute-start(bf16[2,1,512]{2,1,0:T(2,128)(2,1)S(1)} %get-tuple-element.70), channel_id=1, source_target_pairs={{0,1},{1,2},{2,3},{3,4},{4,5},{5,6},{6,7},{7,0},{8,9},{9,10},{10,1... | collective-permute-start | bytes 6152 | tf_op jit(solution)/shard_map/ppermute | solution.py:41
  95.4 4.9 %collective-permute-start.5 = (bf16[2,1,512]{2,1,0:T(2,128)(2,1)S(1)}, bf16[2,1,512]{2,1,0:T(2,128)(2,1)S(1)}, u32[]{:S(2)}, u32[]{:S(2)}) collective-permute-start(bf16[2,1,512]{2,1,0:T(2,128)(2,1)S(1)} %get-tuple-element.69), channel_id=1, source_target_pairs={{0,7},{1,0},{2,1},{3,2},{4,3},{5,4},{6,5},{7,6},{8,15},{9,8},{10,9... | collective-permute-start | bytes 6152 | tf_op jit(solution)/shard_map/ppermute | solution.py:44
  102.0 5.0 %collective-permute-start.8 = (bf16[4,2048,128]{2,1,0:T(8,128)(2,1)S(1)}, bf16[4,2048,128]{2,1,0:T(8,128)(2,1)S(1)}, u32[]{:S(2)}, u32[]{:S(2)}) collective-permute-start(bf16[4,2048,128]{2,1,0:T(8,128)(2,1)S(1)} %weight_grads.2), channel_id=1, source_target_pairs={{0,1},{1,0},{2,3},{3,2},{4,5},{5,4},{6,7},{7,6},{8,9},{9,8},{10,11... | collective-permute-start | bytes 6291464 | tf_op jit(solution)/shard_map/ppermute | solution.py:51
  102.1 7.6 %collective-permute-start.6 = (bf16[1,96,512]{2,1,0:T(8,128)(2,1)S(1)}, bf16[1,96,512]{2,1,0:T(8,128)(2,1)S(1)}, u32[]{:S(2)}, u32[]{:S(2)}) collective-permute-start(bf16[1,96,512]{2,1,0:T(8,128)(2,1)S(1)} %get-tuple-element.67), channel_id=1, source_target_pairs={{0,8},{8,16},{16,24},{1,9},{9,17},{17,25},{2,10},{10,18},{18,26},{... | collective-permute-start | bytes 294920 | tf_op jit(solution)/shard_map/ppermute | solution.py:41
  105.5 7.0 %collective-permute-start.7 = (bf16[1,96,512]{2,1,0:T(8,128)(2,1)S(1)}, bf16[1,96,512]{2,1,0:T(8,128)(2,1)S(1)}, u32[]{:S(2)}, u32[]{:S(2)}) collective-permute-start(bf16[1,96,512]{2,1,0:T(8,128)(2,1)S(1)} %get-tuple-element.68), channel_id=1, source_target_pairs={{8,0},{16,8},{24,16},{9,1},{17,9},{25,17},{10,2},{18,10},{26,18},{... | collective-permute-start | bytes 294920 | tf_op jit(solution)/shard_map/ppermute | solution.py:44
  113.2 29.1 %all-to-all-start.5 = ((bf16[4,2048,128]{2,1,0:T(8,128)(2,1)}), bf16[4,2048,128]{2,1,0:T(8,128)(2,1)S(1)}, u32[]{:S(2)}, u32[]{:S(2)}) async-start(bf16[4,2048,128]{2,1,0:T(8,128)(2,1)} %after.1.refs_4_.refs_5_), calls=%async_computation.5 | async-start | bytes 4194304 | tf_op jit(solution)/shard_map/all_to_all | solution.py:55
  126.1 8.9 %collective-permute-start.9 = (bf16[4,4,256,128]{3,2,1,0:T(8,128)(2,1)}, bf16[4,4,256,128]{3,2,1,0:T(8,128)(2,1)S(1)}, u32[]{:S(2)}, u32[]{:S(2)}) collective-permute-start(bf16[4,4,256,128]{3,2,1,0:T(8,128)(2,1)} %get-tuple-element.50), channel_id=1, source_target_pairs={{0,1},{1,0},{2,3},{3,2},{4,5},{5,4},{6,7},{7,6},{8,9},{9,8},{10,11... | collective-permute-start | bytes 3145736 | tf_op jit(solution)/shard_map/ppermute | solution.py:51
  126.2 8.8 %collective-permute-start.10 = (f32[4,9,256]{2,1,0:T(8,128)}, f32[4,9,256]{2,1,0:T(8,128)S(1)}, u32[]{:S(2)}, u32[]{:S(2)}) collective-permute-start(f32[4,9,256]{2,1,0:T(8,128)} %get-tuple-element.52), channel_id=1, source_target_pairs={{0,1},{1,0},{2,3},{3,2},{4,5},{5,4},{6,7},{7,6},{8,9},{9,8},{10,11... | collective-permute-start | bytes 110600 | tf_op jit(solution)/shard_map/ppermute | solution.py:51
  142.3 17.6 %all-to-all-start.3 = ((bf16[4,1104,128]{2,1,0:T(8,128)(2,1)}), bf16[4,1104,128]{2,1,0:T(8,128)(2,1)S(1)}, u32[]{:S(2)}, u32[]{:S(2)}) async-start(bf16[4,1104,128]{2,1,0:T(8,128)(2,1)} %pack.1), calls=%async_computation.3 | async-start | bytes 2260992 | tf_op jit(solution)/shard_map/all_to_all | solution.py:55
  145.9 30.6 %reduce-scatter.2.cloned.1.call-start = ((), (), s32[]{:S(2)}) async-start(), calls=%async_computation.7 | async-start | bytes 655360 | tf_op jit(solution)/shard_map/reduce_scatter | solution.py:925
  176.4 1.8 collective-permute-start.11
  (24 other events, 63.8 us)
Sparse Core Ops, SparseCore 0:
  149.0 23.7 reduce-scatter.1

commit v6 on v5

--- a/solution.py
+++ b/solution.py
@@ -93,7 +93,7 @@
 
 
 def early_kernel(
-    groups, cot_ref, bias_ref, out_weight_ref, order_ref, early_ref, framed_ref, bias_frame
+    groups, cot_ref, bias_ref, out_weight_ref, order_ref, early_ref, framed_ref, bias_frame, wide_frame
 ):
     row_count, lon_count, channels = cot_ref.shape
     frame = framed_ref.shape[1]
@@ -101,10 +101,11 @@
     head_count = bias_ref.shape[2]
     items = head_count // groups
     in_rows = early_ref.shape[2] == width
-    framed_ref[...] = jnp.zeros_like(framed_ref)
+    wide_frame[...] = jnp.zeros_like(wide_frame)
     bias_frame[...] = jnp.full_like(bias_frame, MASKED)
     for row in range(row_count):
-        framed_ref[row, SIDE : SIDE + lon_count, :] = cot_ref[row]
+        wide_frame[row, SIDE : SIDE + lon_count, :] = cot_ref[row].astype(F32)
+        framed_ref[row] = wide_frame[row].astype(BF16)
         bias_frame[row, SIDE : SIDE + lon_count, 0:head_count] = bias_ref[row].astype(F32)
     for row in range(row_count):
         back_heads = times_transpose(framed_ref[row], out_weight_ref[...]).astype(BF16)
@@ -144,7 +145,7 @@
         key_bias,
         attention_out,
         order,
-        scratch=[pltpu.VMEM(bias_shape, F32)],
+        scratch=[pltpu.VMEM(bias_shape, F32), pltpu.VMEM((row_count, frame, channels), F32)],
         flops=2 * row_count * frame * channels * channels,
     )
 
@@ -336,10 +337,10 @@
                 target, :, kind * width : (kind + 1) * width
             ]
     inner = inner_ref[...].astype(F32)
-    output = (inner + matmul(unpacked_ref[:, :channels], out_weight_ref[...])).astype(BF16)
+    output = inner + matmul(unpacked_ref[:, :channels], out_weight_ref[...])
     for row in range(row_count):
         start = row * frame + SIDE
-        output_ref[row] = output[start : start + lon_count]
+        output_ref[row] = output[start : start + lon_count].astype(BF16)
     back_second = times_transpose(unpacked_ref[:, channels:], in_weight_ref[...])
     inverse = inverse_rms(inner)
     gain_grad_ref[...] = norm_factor * jnp.sum(back_second * inner * inverse, axis=0, keepdims=True)
@@ -622,13 +623,12 @@
     inverse = inverse_rms(state)
     grads = back_normed[...]
     gain_grad_ref[...] = norm_factor * jnp.sum(grads * state * inverse, axis=0, keepdims=True)
-    result = (
-        back_ref[frame : frame + cells, :].astype(F32)
-        + norm_back(grads, state, inverse, gain_ref[...])
-    ).astype(BF16)
+    result = back_ref[frame : frame + cells, :].astype(F32) + norm_back(
+        grads, state, inverse, gain_ref[...]
+    )
     for row in range(row_count):
         start = row * frame + SIDE
-        input_ref[row] = result[start : start + lon_count]
+        input_ref[row] = result[start : start + lon_count].astype(BF16)
     for send in sends:
         send.wait()
 

time: 188 us -> 188 us (level)
  no operation moved by 1% of the time
where the time goes in v6:
time: 188 us; the launch traced here: 187 us
  Pallas kernels  52.6 us (28%)
  blocking collectives  39.8 us (21%)
  starting transfers between devices  35.2 us (19%)
  waiting for transfers between devices  27.2 us (14%)
  local copies, waits for them, and re-layouts  15.9 us (8%)
  between operations  14.6 us (8%)
    all_to_all x2, blocking collectives, exchange(): return lax.all_to_all(values, axis, 0, 0, tiled=True)  39.8 us
    all_to_all x4, waiting for transfers between devices, exchange(): return lax.all_to_all(values, axis, 0, 0, tiled=True)  19.2 us
    pallas_call x2, Pallas kernels, backward(): pl.pallas_call(functools.partial(backward_kernel, frame, norm_factor, str...  16.5 us
    all_to_all x4, starting transfers between devices, exchange(): return lax.all_to_all(values, axis, 0, 0, tiled=True)  16.2 us
    unnamed x65, local copies, waits for them, and re-layouts  12.7 us
    pallas_call x1, Pallas kernels, attention(): pl.pallas_call(functools.partial(attention_kernel, head_width, query_bloc...  11.7 us
    ppermute x4, starting transfers between devices, from_sides(): lax.ppermute(lax.slice_in_dim(block, 0, width, axis=dim), axis, shifts(co...  10.4 us
    ppermute x4, starting transfers between devices, from_sides(): lax.ppermute(lax.slice_in_dim(block, size - width, size, axis=dim), axis,...  7.8 us
  transfers between devices with their start and end apart: 17, of which 8 were waited for; matrix products, arithmetic and copies ran while one was open for 3% of the time, Pallas kernels for 20%

profile of v6, /device:TPU:0, one launch (start us, length us, event | category | flops | bytes accessed | tf_op | source)
XLA Modules:
  0.0 187.0 jit_solution(18346408097799314229)
XLA Ops:
  8.7 4.1 %collective-permute-start.1 = (bf16[2,3,512]{2,1,0:T(4,128)(2,1)S(1)}, bf16[2,3,512]{2,1,0:T(4,128)(2,1)S(1)}, u32[]{:S(2)}, u32[]{:S(2)}) collective-permute-start(bf16[2,3,512]{2,1,0:T(4,128)(2,1)S(1)} %get-tuple-element.72), channel_id=1, source_target_pairs={{0,7},{1,0},{2,1},{3,2},{4,3},{5,4},{6,5},{7,6},{8,15},{9,8},{10,9... | collective-permute-start | bytes 18440 | tf_op jit(solution)/shard_map/ppermute | solution.py:44
  14.3 3.8 %collective-permute-start.2 = (bf16[2,96,512]{2,1,0:T(8,128)(2,1)S(1)}, bf16[2,96,512]{2,1,0:T(8,128)(2,1)S(1)}, u32[]{:S(2)}, u32[]{:S(2)}) collective-permute-start(bf16[2,96,512]{2,1,0:T(8,128)(2,1)S(1)} %pad_maximum_fusion.2.order_ref), channel_id=1, source_target_pairs={{0,8},{8,16},{16,24},{1,9},{9,17},{17,25},{2,10},{10,18},{18,26},{... | collective-permute-start | bytes 589832 | tf_op jit(solution)/shard_map/ppermute | solution.py:41
  21.7 4.5 %all-to-all-start.1 = ((bf16[8,112,128]{2,1,0:T(8,128)(2,1)}), bf16[8,112,128]{2,1,0:T(8,128)(2,1)S(1)}, u32[]{:S(2)}, u32[]{:S(2)}) async-start(bf16[8,112,128]{2,1,0:T(8,128)(2,1)} %get-tuple-element.39), calls=%async_computation.1 | async-start | bytes 458752 | tf_op jit(solution)/shard_map/all_to_all | solution.py:55
  26.2 2.5 %collective-permute-done.3 = bf16[2,96,512]{2,1,0:T(8,128)(2,1)S(1)} collective-permute-done((bf16[2,96,512]{2,1,0:T(8,128)(2,1)S(1)}, bf16[2,96,512]{2,1,0:T(8,128)(2,1)S(1)}, u32[]{:S(2)}, u32[]{:S(2)}) %collective-permute-start.3) | collective-permute-done | bytes 196640 | tf_op jit(solution)/shard_map/ppermute | solution.py:44
  29.6 7.4 %forward.1 = (bf16[8,96,384]{2,1,0:T(8,128)(2,1)}, bf16[192,512]{1,0:T(8,128)(2,1)}) custom-call(bf16[576,512]{1,0:T(8,128)(2,1)} %bitcast.31, f32[1,512]{1,0:T(1,128)} %bitcast.46, bf16[3,3,2048]{2,1,0:T(4,128)(2,1)} %kernel_ref.1, f32[1,512]{1,0:T(1,128)} %bitcast.42, bf16[512,2048]{1,0:T(8,128)(2,1)} %refs_9_.1, bf16[2048,512]{1,0:T(8,128)(2,1)} %refs_6_.1, ...), custom_call_target="tpu_custom_call" | custom-call | flops 1509949440 | bytes 5767168 | tf_op jit(solution)/shard_map/forward/pallas_call | solution.py:228
  37.0 4.3 %all-to-all-start = ((bf16[8,96,384]{2,1,0:T(8,128)(2,1)}), bf16[8,96,384]{2,1,0:T(8,128)(2,1)}, u32[]{:S(2)}, u32[]{:S(2)}) async-start(bf16[8,96,384]{2,1,0:T(8,128)(2,1)} %get-tuple-element.38), calls=%async_computation | async-start | bytes 1179648 | tf_op jit(solution)/shard_map/all_to_all | solution.py:55
  42.6 6.7 %forward_around.1 = (bf16[8,384,256]{2,1,0:T(8,128)(2,1)S(1)}, bf16[8,384,256]{2,1,0:T(8,128)(2,1)S(1)}, bf16[8,192,256]{2,1,0:T(8,128)(2,1)S(1)}, bf16[8,192,256]{2,1,0:T(8,128)(2,1)S(1)}) custom-call(bf16[576,512]{1,0:T(8,128)(2,1)S(1)} %bitcast.32, f32[1,512]{1,0:T(1,128)S(1)} %bitcast.49, bf16[512,2048]{1,0:T(8,128)(2,1)S(1)} %copy-done.1, ...), custom_call_target="tpu_custom_call" | custom-call | flops 1207959552 | bytes 13107200 | tf_op jit(solution)/shard_map/forward_around/pallas_call | solution.py:295
  52.6 5.5 %all-to-all-done = bf16[8,96,384]{2,1,0:T(8,128)(2,1)} async-done(((bf16[8,96,384]{2,1,0:T(8,128)(2,1)}), bf16[8,96,384]{2,1,0:T(8,128)(2,1)}, u32[]{:S(2)}, u32[]{:S(2)}) %all-to-all-start) | async-done | bytes 589856 | tf_op jit(solution)/shard_map/all_to_all | solution.py:55
  59.1 11.7 %attention.1 = bf16[768,512]{1,0:T(8,128)(2,1)S(1)} custom-call(bf16[768,384]{1,0:T(8,128)(2,1)} %bitcast.5.qkv_ref, bf16[8,112,128]{2,1,0:T(8,128)(2,1)S(1)} %copy-done.14, bf16[8,192,256]{2,1,0:T(8,128)(2,1)S(1)} %get-tuple-element.41.order_ref.mixed_ref), custom_call_target="tpu_custom_call" | custom-call | flops 1056964608 | bytes 1572864 | tf_op jit(solution)/shard_map/attention/pallas_call | solution.py:800
  70.8 23.5 %all_to_all.30.attended_ref = bf16[8,96,512]{2,1,0:T(8,128)(2,1)S(1)} all-to-all(bf16[8,96,512]{2,1,0:T(8,128)(2,1)S(1)} %bitcast.41), channel_id=1, replica_groups=mesh['lat'=4,'z'=4,'core'=2] {'z','core'}, dimensions={0} | all-to-all | bytes 1572864 | tf_op jit(solution)/shard_map/all_to_all | solution.py:55
  95.4 3.5 %collective-permute-start.5 = (bf16[2,1,512]{2,1,0:T(2,128)(2,1)S(1)}, bf16[2,1,512]{2,1,0:T(2,128)(2,1)S(1)}, u32[]{:S(2)}, u32[]{:S(2)}) collective-permute-start(bf16[2,1,512]{2,1,0:T(2,128)(2,1)S(1)} %get-tuple-element.69), channel_id=1, source_target_pairs={{0,7},{1,0},{2,1},{3,2},{4,3},{5,4},{6,5},{7,6},{8,15},{9,8},{10,9... | collective-permute-start | bytes 6152 | tf_op jit(solution)/shard_map/ppermute | solution.py:44
  102.1 3.4 %collective-permute-start.6 = (bf16[1,96,512]{2,1,0:T(8,128)(2,1)S(1)}, bf16[1,96,512]{2,1,0:T(8,128)(2,1)S(1)}, u32[]{:S(2)}, u32[]{:S(2)}) collective-permute-start(bf16[1,96,512]{2,1,0:T(8,128)(2,1)S(1)} %get-tuple-element.67), channel_id=1, source_target_pairs={{0,8},{8,16},{16,24},{1,9},{9,17},{17,25},{2,10},{10,18},{18,26},{... | collective-permute-start | bytes 294920 | tf_op jit(solution)/shard_map/ppermute | solution.py:41
  105.5 1.5 collective-permute-start.7
  109.8 2.8 %collective-permute-done.7.refs_2_ = bf16[1,96,512]{2,1,0:T(8,128)(2,1)S(1)} collective-permute-done((bf16[1,96,512]{2,1,0:T(8,128)(2,1)S(1)}, bf16[1,96,512]{2,1,0:T(8,128)(2,1)S(1)}, u32[]{:S(2)}, u32[]{:S(2)}) %collective-permute-start.7) | collective-permute-done | bytes 98336 | tf_op jit(solution)/shard_map/ppermute | solution.py:44
  113.2 3.9 %all-to-all-start.5 = ((bf16[4,2048,128]{2,1,0:T(8,128)(2,1)}), bf16[4,2048,128]{2,1,0:T(8,128)(2,1)S(1)}, u32[]{:S(2)}, u32[]{:S(2)}) async-start(bf16[4,2048,128]{2,1,0:T(8,128)(2,1)} %after.1.refs_4_.refs_5_), calls=%async_computation.5 | async-start | bytes 4194304 | tf_op jit(solution)/shard_map/all_to_all | solution.py:55
  117.9 8.2 %backward.2 = (bf16[4,4,256,128]{3,2,1,0:T(8,128)(2,1)}, f32[4,9,256]{2,1,0:T(8,128)}, bf16[2,90,512]{2,1,0:T(8,128)(2,1)}, f32[1,512]{1,0:T(1,128)}, f32[192,512]{1,0:T(8,128)}) custom-call(s32[1]{0:T(128)} %bitcast.1.which_ref, bf16[384,512]{1,0:T(8,128)(2,1)} %bitcast.50, bf16[192,512]{1,0:T(8,128)(2,1)} %bitcast.29, f32[1,512]{1,0:T(1,128)} %bitcast.47, ...), custom_call_target="tpu_custom_call" | custom-call | flops 805306368 | bytes 7864320 | tf_op jit(solution)/shard_map/backward/pallas_call | solution.py:655
  126.7 8.3 %backward.3 = (bf16[4,4,256,128]{3,2,1,0:T(8,128)(2,1)}, f32[4,9,256]{2,1,0:T(8,128)}, bf16[2,90,512]{2,1,0:T(8,128)(2,1)}, f32[1,512]{1,0:T(1,128)}, f32[192,512]{1,0:T(8,128)}) custom-call(s32[1]{0:T(128)} %bitcast.which_ref.core_ref, f32[192,512]{1,0:T(8,128)} %get-tuple-element.48.refs_0_, bf16[384,512]{1,0:T(8,128)(2,1)} %bitcast.51, ...), custom_call_target="tpu_custom_call" | custom-call | flops 805306368 | bytes 7864320 | tf_op jit(solution)/shard_map/backward/pallas_call | solution.py:655
  136.1 2.8 %pack.1 = bf16[4,1104,128]{2,1,0:T(8,128)(2,1)} custom-call(bf16[4,1024,128]{2,1,0:T(8,128)(2,1)} %bitcast.53, bf16[4,1024,128]{2,1,0:T(8,128)(2,1)} %bitcast.52, f32[4,9,256]{2,1,0:T(8,128)} %get-tuple-element.51.mine_ref, f32[4,9,256]{2,1,0:T(8,128)} %copy-done.28, f32[1,512]{1,0:T(1,128)} %get-tuple-element.53.first_gain_ref, f32[1,512]{1,0:T(1,128)} %copy-done.21), custom_call_target="tpu_custom_call" | custom-call | bytes 2174976 | tf_op jit(solution)/shard_map/pack/pallas_call | solution.py:77
  138.9 3.5 %all-to-all-done.5.parts_ref = bf16[4,2048,128]{2,1,0:T(8,128)(2,1)S(1)} async-done(((bf16[4,2048,128]{2,1,0:T(8,128)(2,1)}), bf16[4,2048,128]{2,1,0:T(8,128)(2,1)S(1)}, u32[]{:S(2)}, u32[]{:S(2)}) %all-to-all-start.5) | async-done | bytes 2097184 | tf_op jit(solution)/shard_map/all_to_all | solution.py:55
  142.3 3.5 %all-to-all-start.3 = ((bf16[4,1104,128]{2,1,0:T(8,128)(2,1)}), bf16[4,1104,128]{2,1,0:T(8,128)(2,1)S(1)}, u32[]{:S(2)}, u32[]{:S(2)}) async-start(bf16[4,1104,128]{2,1,0:T(8,128)(2,1)} %pack.1), calls=%async_computation.3 | async-start | bytes 2260992 | tf_op jit(solution)/shard_map/all_to_all | solution.py:55
  147.9 1.8 copy.40
  149.7 10.2 %all-to-all-done.3.parts_ref = bf16[4,1104,128]{2,1,0:T(8,128)(2,1)S(1)} async-done(((bf16[4,1104,128]{2,1,0:T(8,128)(2,1)}), bf16[4,1104,128]{2,1,0:T(8,128)(2,1)S(1)}, u32[]{:S(2)}, u32[]{:S(2)}) %all-to-all-start.3) | async-done | bytes 1130528 | tf_op jit(solution)/shard_map/all_to_all | solution.py:55
  160.0 16.3 %all_to_all.31.parts_ref = bf16[4,336,128]{2,1,0:T(8,128)(2,1)S(1)} all-to-all(bf16[4,336,128]{2,1,0:T(8,128)(2,1)S(1)} %get-tuple-element.59), channel_id=1, replica_groups=mesh['lat'=4,'z'=4,'core'=2] {'z'}, dimensions={0} | all-to-all | bytes 688128 | tf_op jit(solution)/shard_map/all_to_all | solution.py:55
  178.7 1.5 small_grads.1
  (107 shorter events, 27.2 us)
Async XLA Ops:
  7.2 13.2 %copy-start.30 = (bf16[2,90,16]{1,2,0:T(8,128)(2,1)S(1)}, bf16[2,90,16]{1,2,0:T(8,128)(2,1)}, u32[]{:S(2)}) copy-start(bf16[2,90,16]{1,2,0:T(8,128)(2,1)} %param.12) | copy-start | bytes 17284
  7.2 13.3 %copy-start.9 = (bf16[512,512]{1,0:T(8,128)(2,1)S(1)}, bf16[512,512]{1,0:T(8,128)(2,1)}, u32[]{:S(2)}) copy-start(bf16[512,512]{1,0:T(8,128)(2,1)} %out_weight_ref.3) | copy-start | bytes 1572868
  8.2 5.9 %collective-permute-start = (bf16[2,3,512]{2,1,0:T(4,128)(2,1)S(1)}, bf16[2,3,512]{2,1,0:T(4,128)(2,1)S(1)}, u32[]{:S(2)}, u32[]{:S(2)}) collective-permute-start(bf16[2,3,512]{2,1,0:T(4,128)(2,1)S(1)} %get-tuple-element.71), channel_id=1, source_target_pairs={{0,1},{1,2},{2,3},{3,4},{4,5},{5,6},{6,7},{7,0},{8,9},{9,10},{10,1... | collective-permute-start | bytes 18440 | tf_op jit(solution)/shard_map/ppermute | solution.py:41
  8.7 5.5 %collective-permute-start.1 = (bf16[2,3,512]{2,1,0:T(4,128)(2,1)S(1)}, bf16[2,3,512]{2,1,0:T(4,128)(2,1)S(1)}, u32[]{:S(2)}, u32[]{:S(2)}) collective-permute-start(bf16[2,3,512]{2,1,0:T(4,128)(2,1)S(1)} %get-tuple-element.72), channel_id=1, source_target_pairs={{0,7},{1,0},{2,1},{3,2},{4,3},{5,4},{6,5},{7,6},{8,15},{9,8},{10,9... | collective-permute-start | bytes 18440 | tf_op jit(solution)/shard_map/ppermute | solution.py:44
  14.3 15.3 %copy-start.6 = (bf16[2,96,512]{2,1,0:T(8,128)(2,1)}, bf16[2,96,512]{2,1,0:T(8,128)(2,1)S(1)}, u32[]{:S(2)}) copy-start(bf16[2,96,512]{2,1,0:T(8,128)(2,1)S(1)} %pad_maximum_fusion.2.order_ref) | copy-start | bytes 589828
  14.3 11.9 %collective-permute-start.2 = (bf16[2,96,512]{2,1,0:T(8,128)(2,1)S(1)}, bf16[2,96,512]{2,1,0:T(8,128)(2,1)S(1)}, u32[]{:S(2)}, u32[]{:S(2)}) collective-permute-start(bf16[2,96,512]{2,1,0:T(8,128)(2,1)S(1)} %pad_maximum_fusion.2.order_ref), channel_id=1, source_target_pairs={{0,8},{8,16},{16,24},{1,9},{9,17},{17,25},{2,10},{10,18},{18,26},{... | collective-permute-start | bytes 589832 | tf_op jit(solution)/shard_map/ppermute | solution.py:41
  18.1 10.5 %collective-permute-start.3 = (bf16[2,96,512]{2,1,0:T(8,128)(2,1)S(1)}, bf16[2,96,512]{2,1,0:T(8,128)(2,1)S(1)}, u32[]{:S(2)}, u32[]{:S(2)}) collective-permute-start(bf16[2,96,512]{2,1,0:T(8,128)(2,1)S(1)} %pad_maximum_fusion.2.order_ref), channel_id=1, source_target_pairs={{8,0},{16,8},{24,16},{9,1},{17,9},{25,17},{10,2},{18,10},{26,18},{... | collective-permute-start | bytes 589832 | tf_op jit(solution)/shard_map/ppermute | solution.py:44
  21.7 15.3 %all-to-all-start.1 = ((bf16[8,112,128]{2,1,0:T(8,128)(2,1)}), bf16[8,112,128]{2,1,0:T(8,128)(2,1)S(1)}, u32[]{:S(2)}, u32[]{:S(2)}) async-start(bf16[8,112,128]{2,1,0:T(8,128)(2,1)} %get-tuple-element.39), calls=%async_computation.1 | async-start | bytes 458752 | tf_op jit(solution)/shard_map/all_to_all | solution.py:55
  29.6 11.9 %copy-start.1 = (bf16[512,2048]{1,0:T(8,128)(2,1)S(1)}, bf16[512,2048]{1,0:T(8,128)(2,1)}, u32[]{:S(2)}) copy-start(bf16[512,2048]{1,0:T(8,128)(2,1)} %refs_9_.1) | copy-start | bytes 6291460
  37.0 21.1 %all-to-all-start = ((bf16[8,96,384]{2,1,0:T(8,128)(2,1)}), bf16[8,96,384]{2,1,0:T(8,128)(2,1)}, u32[]{:S(2)}, u32[]{:S(2)}) async-start(bf16[8,96,384]{2,1,0:T(8,128)(2,1)} %get-tuple-element.38), calls=%async_computation | async-start | bytes 1179648 | tf_op jit(solution)/shard_map/all_to_all | solution.py:55
  59.1 35.2 %copy-start.10 = (bf16[512,512]{1,0:T(8,128)(2,1)S(1)}, bf16[512,512]{1,0:T(8,128)(2,1)}, u32[]{:S(2)}) copy-start(bf16[512,512]{1,0:T(8,128)(2,1)} %out_weight_ref.3) | copy-start | bytes 1572868
  70.8 23.6 %copy-start.4 = (bf16[512,1536]{1,0:T(8,128)(2,1)S(1)}, bf16[512,1536]{1,0:T(8,128)(2,1)}, u32[]{:S(2)}) copy-start(bf16[512,1536]{1,0:T(8,128)(2,1)} %in_weight_ref.1) | copy-start | bytes 4718596
  70.8 23.5 %copy-start.19 = (f32[512]{0:T(512)S(1)}, f32[512]{0:T(512)}, u32[]{:S(2)}) copy-start(f32[512]{0:T(512)} %param.17) | copy-start | bytes 6148
  95.3 4.9 %collective-permute-start.4 = (bf16[2,1,512]{2,1,0:T(2,128)(2,1)S(1)}, bf16[2,1,512]{2,1,0:T(2,128)(2,1)S(1)}, u32[]{:S(2)}, u32[]{:S(2)}) collective-permute-start(bf16[2,1,512]{2,1,0:T(2,128)(2,1)S(1)} %get-tuple-element.70), channel_id=1, source_target_pairs={{0,1},{1,2},{2,3},{3,4},{4,5},{5,6},{6,7},{7,0},{8,9},{9,10},{10,1... | collective-permute-start | bytes 6152 | tf_op jit(solution)/shard_map/ppermute | solution.py:41
  95.4 4.9 %collective-permute-start.5 = (bf16[2,1,512]{2,1,0:T(2,128)(2,1)S(1)}, bf16[2,1,512]{2,1,0:T(2,128)(2,1)S(1)}, u32[]{:S(2)}, u32[]{:S(2)}) collective-permute-start(bf16[2,1,512]{2,1,0:T(2,128)(2,1)S(1)} %get-tuple-element.69), channel_id=1, source_target_pairs={{0,7},{1,0},{2,1},{3,2},{4,3},{5,4},{6,5},{7,6},{8,15},{9,8},{10,9... | collective-permute-start | bytes 6152 | tf_op jit(solution)/shard_map/ppermute | solution.py:44
  102.0 5.0 %collective-permute-start.8 = (bf16[4,2048,128]{2,1,0:T(8,128)(2,1)S(1)}, bf16[4,2048,128]{2,1,0:T(8,128)(2,1)S(1)}, u32[]{:S(2)}, u32[]{:S(2)}) collective-permute-start(bf16[4,2048,128]{2,1,0:T(8,128)(2,1)S(1)} %weight_grads.2), channel_id=1, source_target_pairs={{0,1},{1,0},{2,3},{3,2},{4,5},{5,4},{6,7},{7,6},{8,9},{9,8},{10,11... | collective-permute-start | bytes 6291464 | tf_op jit(solution)/shard_map/ppermute | solution.py:51
  102.1 7.6 %collective-permute-start.6 = (bf16[1,96,512]{2,1,0:T(8,128)(2,1)S(1)}, bf16[1,96,512]{2,1,0:T(8,128)(2,1)S(1)}, u32[]{:S(2)}, u32[]{:S(2)}) collective-permute-start(bf16[1,96,512]{2,1,0:T(8,128)(2,1)S(1)} %get-tuple-element.67), channel_id=1, source_target_pairs={{0,8},{8,16},{16,24},{1,9},{9,17},{17,25},{2,10},{10,18},{18,26},{... | collective-permute-start | bytes 294920 | tf_op jit(solution)/shard_map/ppermute | solution.py:41
  105.5 7.0 %collective-permute-start.7 = (bf16[1,96,512]{2,1,0:T(8,128)(2,1)S(1)}, bf16[1,96,512]{2,1,0:T(8,128)(2,1)S(1)}, u32[]{:S(2)}, u32[]{:S(2)}) collective-permute-start(bf16[1,96,512]{2,1,0:T(8,128)(2,1)S(1)} %get-tuple-element.68), channel_id=1, source_target_pairs={{8,0},{16,8},{24,16},{9,1},{17,9},{25,17},{10,2},{18,10},{26,18},{... | collective-permute-start | bytes 294920 | tf_op jit(solution)/shard_map/ppermute | solution.py:44
  113.2 29.1 %all-to-all-start.5 = ((bf16[4,2048,128]{2,1,0:T(8,128)(2,1)}), bf16[4,2048,128]{2,1,0:T(8,128)(2,1)S(1)}, u32[]{:S(2)}, u32[]{:S(2)}) async-start(bf16[4,2048,128]{2,1,0:T(8,128)(2,1)} %after.1.refs_4_.refs_5_), calls=%async_computation.5 | async-start | bytes 4194304 | tf_op jit(solution)/shard_map/all_to_all | solution.py:55
  126.1 8.9 %collective-permute-start.9 = (bf16[4,4,256,128]{3,2,1,0:T(8,128)(2,1)}, bf16[4,4,256,128]{3,2,1,0:T(8,128)(2,1)S(1)}, u32[]{:S(2)}, u32[]{:S(2)}) collective-permute-start(bf16[4,4,256,128]{3,2,1,0:T(8,128)(2,1)} %get-tuple-element.50), channel_id=1, source_target_pairs={{0,1},{1,0},{2,3},{3,2},{4,5},{5,4},{6,7},{7,6},{8,9},{9,8},{10,11... | collective-permute-start | bytes 3145736 | tf_op jit(solution)/shard_map/ppermute | solution.py:51
  126.2 8.8 %collective-permute-start.10 = (f32[4,9,256]{2,1,0:T(8,128)}, f32[4,9,256]{2,1,0:T(8,128)S(1)}, u32[]{:S(2)}, u32[]{:S(2)}) collective-permute-start(f32[4,9,256]{2,1,0:T(8,128)} %get-tuple-element.52), channel_id=1, source_target_pairs={{0,1},{1,0},{2,3},{3,2},{4,5},{5,4},{6,7},{7,6},{8,9},{9,8},{10,11... | collective-permute-start | bytes 110600 | tf_op jit(solution)/shard_map/ppermute | solution.py:51
  142.3 17.6 %all-to-all-start.3 = ((bf16[4,1104,128]{2,1,0:T(8,128)(2,1)}), bf16[4,1104,128]{2,1,0:T(8,128)(2,1)S(1)}, u32[]{:S(2)}, u32[]{:S(2)}) async-start(bf16[4,1104,128]{2,1,0:T(8,128)(2,1)} %pack.1), calls=%async_computation.3 | async-start | bytes 2260992 | tf_op jit(solution)/shard_map/all_to_all | solution.py:55
  145.9 30.6 %reduce-scatter.2.cloned.1.call-start = ((), (), s32[]{:S(2)}) async-start(), calls=%async_computation.7 | async-start | bytes 655360 | tf_op jit(solution)/shard_map/reduce_scatter | solution.py:925
  176.3 1.8 collective-permute-start.11
  (24 other events, 63.8 us)
Sparse Core Ops, SparseCore 0:
  149.0 23.7 reduce-scatter.1

commit v7 on v6

--- a/solution.py
+++ b/solution.py
@@ -353,8 +353,11 @@
     norm_factor, z_size, which_ref, unpacked_ref, inner_ref, gain_ref, cot_ref, back_inner_ref,
     mixed_ref, order_ref, *refs
 ):
-    added_ref = refs[0] if len(refs) == 8 else None
-    out_ref, whole_in, whole_out, whole_back, in_t, out_t, back_t = refs[-7:]
+    added_ref = out_hbm = None
+    if len(refs) == 10:
+        added_ref, out_hbm, *refs, sent = refs
+    out_ref, whole_in, whole_out, whole_back, in_t, out_t, back_t = refs
+    sends = []
     lat_size, _, lane = out_ref.shape
     channels = inner_ref.shape[1]
     blocks, _, part = mixed_ref.shape
@@ -395,6 +398,13 @@
             for piece in range(part // lane):
                 put(lat, start, out_split, values[:, piece * lane : (piece + 1) * lane])
                 start += out_split
+        if out_hbm is not None:
+            sends.append(
+                pltpu.make_async_copy(out_ref.at[lat], out_hbm.at[lat], sent.at[lat])
+            )
+            sends[lat].start()
+    for send in sends:
+        send.wait()
 
 
 def weight_grads(
@@ -409,19 +419,27 @@
         operands += (added,)
     in_specs = [pl.BlockSpec(memory_space=pltpu.VMEM)] * len(operands)
     in_specs[6] = pl.BlockSpec(memory_space=pl.ANY)
+    out_spec, first_scratch, last_scratch = pl.BlockSpec(memory_space=pltpu.VMEM), [], []
+    if added is not None:
+        out_spec = pl.BlockSpec(memory_space=pl.ANY)
+        first_scratch = [pltpu.VMEM((lat_size, rows, lane), BF16)]
+        last_scratch = [pltpu.SemaphoreType.DMA((lat_size,))]
     tall, short = pltpu.VMEM((3 * channels, own), BF16), pltpu.VMEM((channels, own), BF16)
     return pl.pallas_call(
         functools.partial(weight_grads_kernel, norm_factor, z_size),
         out_shape=jax.ShapeDtypeStruct((lat_size, rows, lane), BF16),
         in_specs=[pl.BlockSpec(memory_space=pltpu.SMEM)] + in_specs,
-        scratch_shapes=[
+        out_specs=out_spec,
+        scratch_shapes=first_scratch
+        + [
             tall,
             short,
             short,
             pltpu.VMEM((3 * channels // 2, own), BF16),
             pltpu.VMEM((channels // 2, own), BF16),
             pltpu.VMEM((channels // 2, own), BF16),
-        ],
+        ]
+        + last_scratch,
         compiler_params=pltpu.CompilerParams(vmem_limit_bytes=20 * 1024 * 1024),
         cost_estimate=pl.CostEstimate(
             flops=own * channels * (4 * channels + wide),

time: 188 us -> 189 us (level)
  no operation moved by 1% of the time
where the time goes in v7:
time: 189 us; the launch traced here: 188 us
  Pallas kernels  53.3 us (28%)
  blocking collectives  39.3 us (21%)
  starting transfers between devices  35.2 us (19%)
  waiting for transfers between devices  27.8 us (15%)
  local copies, waits for them, and re-layouts  15.9 us (8%)
  between operations  14.6 us (8%)
    all_to_all x2, blocking collectives, exchange(): return lax.all_to_all(values, axis, 0, 0, tiled=True)  39.3 us
    all_to_all x4, waiting for transfers between devices, exchange(): return lax.all_to_all(values, axis, 0, 0, tiled=True)  20.5 us
    pallas_call x2, Pallas kernels, backward(): pl.pallas_call(functools.partial(backward_kernel, frame, norm_factor, str...  16.5 us
    all_to_all x4, starting transfers between devices, exchange(): return lax.all_to_all(values, axis, 0, 0, tiled=True)  16.2 us
    unnamed x65, local copies, waits for them, and re-layouts  12.7 us
    pallas_call x1, Pallas kernels, attention(): pl.pallas_call(functools.partial(attention_kernel, head_width, query_bloc...  11.7 us
    ppermute x4, starting transfers between devices, from_sides(): lax.ppermute(lax.slice_in_dim(block, 0, width, axis=dim), axis, shifts(co...  10.4 us
    ppermute x4, starting transfers between devices, from_sides(): lax.ppermute(lax.slice_in_dim(block, size - width, size, axis=dim), axis,...  7.8 us
  transfers between devices with their start and end apart: 17, of which 8 were waited for; matrix products, arithmetic and copies ran while one was open for 3% of the time, Pallas kernels for 20%

profile of v7, /device:TPU:0, one launch (start us, length us, event | category | flops | bytes accessed | tf_op | source)
XLA Modules:
  0.0 187.8 jit_solution(16766892129622599312)
XLA Ops:
  8.7 4.1 %collective-permute-start.1 = (bf16[2,3,512]{2,1,0:T(4,128)(2,1)S(1)}, bf16[2,3,512]{2,1,0:T(4,128)(2,1)S(1)}, u32[]{:S(2)}, u32[]{:S(2)}) collective-permute-start(bf16[2,3,512]{2,1,0:T(4,128)(2,1)S(1)} %get-tuple-element.72), channel_id=1, source_target_pairs={{0,7},{1,0},{2,1},{3,2},{4,3},{5,4},{6,5},{7,6},{8,15},{9,8},{10,9... | collective-permute-start | bytes 18440 | tf_op jit(solution)/shard_map/ppermute | solution.py:44
  14.3 3.8 %collective-permute-start.2 = (bf16[2,96,512]{2,1,0:T(8,128)(2,1)S(1)}, bf16[2,96,512]{2,1,0:T(8,128)(2,1)S(1)}, u32[]{:S(2)}, u32[]{:S(2)}) collective-permute-start(bf16[2,96,512]{2,1,0:T(8,128)(2,1)S(1)} %pad_maximum_fusion.2.order_ref), channel_id=1, source_target_pairs={{0,8},{8,16},{16,24},{1,9},{9,17},{17,25},{2,10},{10,18},{18,26},{... | collective-permute-start | bytes 589832 | tf_op jit(solution)/shard_map/ppermute | solution.py:41
  21.7 4.5 %all-to-all-start.1 = ((bf16[8,112,128]{2,1,0:T(8,128)(2,1)}), bf16[8,112,128]{2,1,0:T(8,128)(2,1)S(1)}, u32[]{:S(2)}, u32[]{:S(2)}) async-start(bf16[8,112,128]{2,1,0:T(8,128)(2,1)} %get-tuple-element.39), calls=%async_computation.1 | async-start | bytes 458752 | tf_op jit(solution)/shard_map/all_to_all | solution.py:55
  26.2 2.5 %collective-permute-done.3 = bf16[2,96,512]{2,1,0:T(8,128)(2,1)S(1)} collective-permute-done((bf16[2,96,512]{2,1,0:T(8,128)(2,1)S(1)}, bf16[2,96,512]{2,1,0:T(8,128)(2,1)S(1)}, u32[]{:S(2)}, u32[]{:S(2)}) %collective-permute-start.3) | collective-permute-done | bytes 196640 | tf_op jit(solution)/shard_map/ppermute | solution.py:44
  29.6 7.4 %forward.1 = (bf16[8,96,384]{2,1,0:T(8,128)(2,1)}, bf16[192,512]{1,0:T(8,128)(2,1)}) custom-call(bf16[576,512]{1,0:T(8,128)(2,1)} %bitcast.31, f32[1,512]{1,0:T(1,128)} %bitcast.46, bf16[3,3,2048]{2,1,0:T(4,128)(2,1)} %kernel_ref.1, f32[1,512]{1,0:T(1,128)} %bitcast.42, bf16[512,2048]{1,0:T(8,128)(2,1)} %refs_9_.1, bf16[2048,512]{1,0:T(8,128)(2,1)} %refs_6_.1, ...), custom_call_target="tpu_custom_call" | custom-call | flops 1509949440 | bytes 5767168 | tf_op jit(solution)/shard_map/forward/pallas_call | solution.py:228
  37.0 4.3 %all-to-all-start = ((bf16[8,96,384]{2,1,0:T(8,128)(2,1)}), bf16[8,96,384]{2,1,0:T(8,128)(2,1)}, u32[]{:S(2)}, u32[]{:S(2)}) async-start(bf16[8,96,384]{2,1,0:T(8,128)(2,1)} %get-tuple-element.38), calls=%async_computation | async-start | bytes 1179648 | tf_op jit(solution)/shard_map/all_to_all | solution.py:55
  42.6 6.7 %forward_around.1 = (bf16[8,384,256]{2,1,0:T(8,128)(2,1)S(1)}, bf16[8,384,256]{2,1,0:T(8,128)(2,1)S(1)}, bf16[8,192,256]{2,1,0:T(8,128)(2,1)S(1)}, bf16[8,192,256]{2,1,0:T(8,128)(2,1)S(1)}) custom-call(bf16[576,512]{1,0:T(8,128)(2,1)S(1)} %bitcast.32, f32[1,512]{1,0:T(1,128)S(1)} %bitcast.49, bf16[512,2048]{1,0:T(8,128)(2,1)S(1)} %copy-done.1, ...), custom_call_target="tpu_custom_call" | custom-call | flops 1207959552 | bytes 13107200 | tf_op jit(solution)/shard_map/forward_around/pallas_call | solution.py:295
  52.6 5.5 %all-to-all-done = bf16[8,96,384]{2,1,0:T(8,128)(2,1)} async-done(((bf16[8,96,384]{2,1,0:T(8,128)(2,1)}), bf16[8,96,384]{2,1,0:T(8,128)(2,1)}, u32[]{:S(2)}, u32[]{:S(2)}) %all-to-all-start) | async-done | bytes 589856 | tf_op jit(solution)/shard_map/all_to_all | solution.py:55
  59.1 11.7 %attention.1 = bf16[768,512]{1,0:T(8,128)(2,1)S(1)} custom-call(bf16[768,384]{1,0:T(8,128)(2,1)} %bitcast.5.qkv_ref, bf16[8,112,128]{2,1,0:T(8,128)(2,1)S(1)} %copy-done.14, bf16[8,192,256]{2,1,0:T(8,128)(2,1)S(1)} %get-tuple-element.41.order_ref.mixed_ref), custom_call_target="tpu_custom_call" | custom-call | flops 1056964608 | bytes 1572864 | tf_op jit(solution)/shard_map/attention/pallas_call | solution.py:818
  70.8 23.5 %all_to_all.30.attended_ref = bf16[8,96,512]{2,1,0:T(8,128)(2,1)S(1)} all-to-all(bf16[8,96,512]{2,1,0:T(8,128)(2,1)S(1)} %bitcast.41), channel_id=1, replica_groups=mesh['lat'=4,'z'=4,'core'=2] {'z','core'}, dimensions={0} | all-to-all | bytes 1572864 | tf_op jit(solution)/shard_map/all_to_all | solution.py:55
  95.4 3.5 %collective-permute-start.5 = (bf16[2,1,512]{2,1,0:T(2,128)(2,1)S(1)}, bf16[2,1,512]{2,1,0:T(2,128)(2,1)S(1)}, u32[]{:S(2)}, u32[]{:S(2)}) collective-permute-start(bf16[2,1,512]{2,1,0:T(2,128)(2,1)S(1)} %get-tuple-element.69), channel_id=1, source_target_pairs={{0,7},{1,0},{2,1},{3,2},{4,3},{5,4},{6,5},{7,6},{8,15},{9,8},{10,9... | collective-permute-start | bytes 6152 | tf_op jit(solution)/shard_map/ppermute | solution.py:44
  102.1 3.4 %collective-permute-start.6 = (bf16[1,96,512]{2,1,0:T(8,128)(2,1)S(1)}, bf16[1,96,512]{2,1,0:T(8,128)(2,1)S(1)}, u32[]{:S(2)}, u32[]{:S(2)}) collective-permute-start(bf16[1,96,512]{2,1,0:T(8,128)(2,1)S(1)} %get-tuple-element.67), channel_id=1, source_target_pairs={{0,8},{8,16},{16,24},{1,9},{9,17},{17,25},{2,10},{10,18},{18,26},{... | collective-permute-start | bytes 294920 | tf_op jit(solution)/shard_map/ppermute | solution.py:41
  107.0 2.0 %weight_grads.3.refs_0_ = bf16[4,2048,128]{2,1,0:T(8,128)(2,1)S(1)} custom-call(s32[1]{0:T(128)} %bitcast.which_ref.core_ref, bf16[192,2048]{1,0:T(8,128)(2,1)S(1)} %get-tuple-element.44.unpacked_ref, bf16[192,512]{1,0:T(8,128)(2,1)S(1)} %copy-done.11, f32[1,512]{1,0:T(1,128)S(1)} %bitcast.45, bf16[192,512]{1,0:T(8,128)(2,1)S(1)} %bitcast.37, ...), custom_call_target="tpu_custom_call" | custom-call | flops 402653184 | bytes 8388608 | tf_op jit(solution)/shard_map/weight_grads/pallas_call | solution.py:428
  110.4 2.1 %collective-permute-done.7.refs_2_ = bf16[1,96,512]{2,1,0:T(8,128)(2,1)S(1)} collective-permute-done((bf16[1,96,512]{2,1,0:T(8,128)(2,1)S(1)}, bf16[1,96,512]{2,1,0:T(8,128)(2,1)S(1)}, u32[]{:S(2)}, u32[]{:S(2)}) %collective-permute-start.7) | collective-permute-done | bytes 98336 | tf_op jit(solution)/shard_map/ppermute | solution.py:44
  113.2 3.9 %all-to-all-start.5 = ((bf16[4,2048,128]{2,1,0:T(8,128)(2,1)}), bf16[4,2048,128]{2,1,0:T(8,128)(2,1)S(1)}, u32[]{:S(2)}, u32[]{:S(2)}) async-start(bf16[4,2048,128]{2,1,0:T(8,128)(2,1)} %after.1.refs_4_.refs_5_), calls=%async_computation.5 | async-start | bytes 4194304 | tf_op jit(solution)/shard_map/all_to_all | solution.py:55
  117.9 8.2 %backward.2 = (bf16[4,4,256,128]{3,2,1,0:T(8,128)(2,1)}, f32[4,9,256]{2,1,0:T(8,128)}, bf16[2,90,512]{2,1,0:T(8,128)(2,1)}, f32[1,512]{1,0:T(1,128)}, f32[192,512]{1,0:T(8,128)}) custom-call(s32[1]{0:T(128)} %bitcast.1.which_ref, bf16[384,512]{1,0:T(8,128)(2,1)} %bitcast.50, bf16[192,512]{1,0:T(8,128)(2,1)} %bitcast.29, f32[1,512]{1,0:T(1,128)} %bitcast.47, ...), custom_call_target="tpu_custom_call" | custom-call | flops 805306368 | bytes 7864320 | tf_op jit(solution)/shard_map/backward/pallas_call | solution.py:673
  126.7 8.3 %backward.3 = (bf16[4,4,256,128]{3,2,1,0:T(8,128)(2,1)}, f32[4,9,256]{2,1,0:T(8,128)}, bf16[2,90,512]{2,1,0:T(8,128)(2,1)}, f32[1,512]{1,0:T(1,128)}, f32[192,512]{1,0:T(8,128)}) custom-call(s32[1]{0:T(128)} %bitcast.which_ref.core_ref, f32[192,512]{1,0:T(8,128)} %get-tuple-element.48.refs_0_, bf16[384,512]{1,0:T(8,128)(2,1)} %bitcast.51, ...), custom_call_target="tpu_custom_call" | custom-call | flops 805306368 | bytes 7864320 | tf_op jit(solution)/shard_map/backward/pallas_call | solution.py:673
  136.1 2.8 %pack.1 = bf16[4,1104,128]{2,1,0:T(8,128)(2,1)} custom-call(bf16[4,1024,128]{2,1,0:T(8,128)(2,1)} %bitcast.53, bf16[4,1024,128]{2,1,0:T(8,128)(2,1)} %bitcast.52, f32[4,9,256]{2,1,0:T(8,128)} %get-tuple-element.51.mine_ref, f32[4,9,256]{2,1,0:T(8,128)} %copy-done.28, f32[1,512]{1,0:T(1,128)} %get-tuple-element.53.first_gain_ref, f32[1,512]{1,0:T(1,128)} %copy-done.21), custom_call_target="tpu_custom_call" | custom-call | bytes 2174976 | tf_op jit(solution)/shard_map/pack/pallas_call | solution.py:77
  138.9 3.9 %all-to-all-done.5.parts_ref = bf16[4,2048,128]{2,1,0:T(8,128)(2,1)S(1)} async-done(((bf16[4,2048,128]{2,1,0:T(8,128)(2,1)}), bf16[4,2048,128]{2,1,0:T(8,128)(2,1)S(1)}, u32[]{:S(2)}, u32[]{:S(2)}) %all-to-all-start.5) | async-done | bytes 2097184 | tf_op jit(solution)/shard_map/all_to_all | solution.py:55
  142.8 3.5 %all-to-all-start.3 = ((bf16[4,1104,128]{2,1,0:T(8,128)(2,1)}), bf16[4,1104,128]{2,1,0:T(8,128)(2,1)S(1)}, u32[]{:S(2)}, u32[]{:S(2)}) async-start(bf16[4,1104,128]{2,1,0:T(8,128)(2,1)} %pack.1), calls=%async_computation.3 | async-start | bytes 2260992 | tf_op jit(solution)/shard_map/all_to_all | solution.py:55
  148.3 1.8 copy.40
  150.1 11.1 %all-to-all-done.3.parts_ref = bf16[4,1104,128]{2,1,0:T(8,128)(2,1)S(1)} async-done(((bf16[4,1104,128]{2,1,0:T(8,128)(2,1)}), bf16[4,1104,128]{2,1,0:T(8,128)(2,1)S(1)}, u32[]{:S(2)}, u32[]{:S(2)}) %all-to-all-start.3) | async-done | bytes 1130528 | tf_op jit(solution)/shard_map/all_to_all | solution.py:55
  161.3 15.8 %all_to_all.31.parts_ref = bf16[4,336,128]{2,1,0:T(8,128)(2,1)S(1)} all-to-all(bf16[4,336,128]{2,1,0:T(8,128)(2,1)S(1)} %get-tuple-element.59), channel_id=1, replica_groups=mesh['lat'=4,'z'=4,'core'=2] {'z'}, dimensions={0} | all-to-all | bytes 688128 | tf_op jit(solution)/shard_map/all_to_all | solution.py:55
  179.5 1.5 small_grads.1
  (107 shorter events, 27.3 us)
Async XLA Ops:
  7.2 13.2 %copy-start.30 = (bf16[2,90,16]{1,2,0:T(8,128)(2,1)S(1)}, bf16[2,90,16]{1,2,0:T(8,128)(2,1)}, u32[]{:S(2)}) copy-start(bf16[2,90,16]{1,2,0:T(8,128)(2,1)} %param.12) | copy-start | bytes 17284
  7.2 13.3 %copy-start.9 = (bf16[512,512]{1,0:T(8,128)(2,1)S(1)}, bf16[512,512]{1,0:T(8,128)(2,1)}, u32[]{:S(2)}) copy-start(bf16[512,512]{1,0:T(8,128)(2,1)} %out_weight_ref.3) | copy-start | bytes 1572868
  8.2 5.9 %collective-permute-start = (bf16[2,3,512]{2,1,0:T(4,128)(2,1)S(1)}, bf16[2,3,512]{2,1,0:T(4,128)(2,1)S(1)}, u32[]{:S(2)}, u32[]{:S(2)}) collective-permute-start(bf16[2,3,512]{2,1,0:T(4,128)(2,1)S(1)} %get-tuple-element.71), channel_id=1, source_target_pairs={{0,1},{1,2},{2,3},{3,4},{4,5},{5,6},{6,7},{7,0},{8,9},{9,10},{10,1... | collective-permute-start | bytes 18440 | tf_op jit(solution)/shard_map/ppermute | solution.py:41
  8.7 5.5 %collective-permute-start.1 = (bf16[2,3,512]{2,1,0:T(4,128)(2,1)S(1)}, bf16[2,3,512]{2,1,0:T(4,128)(2,1)S(1)}, u32[]{:S(2)}, u32[]{:S(2)}) collective-permute-start(bf16[2,3,512]{2,1,0:T(4,128)(2,1)S(1)} %get-tuple-element.72), channel_id=1, source_target_pairs={{0,7},{1,0},{2,1},{3,2},{4,3},{5,4},{6,5},{7,6},{8,15},{9,8},{10,9... | collective-permute-start | bytes 18440 | tf_op jit(solution)/shard_map/ppermute | solution.py:44
  14.3 15.3 %copy-start.6 = (bf16[2,96,512]{2,1,0:T(8,128)(2,1)}, bf16[2,96,512]{2,1,0:T(8,128)(2,1)S(1)}, u32[]{:S(2)}) copy-start(bf16[2,96,512]{2,1,0:T(8,128)(2,1)S(1)} %pad_maximum_fusion.2.order_ref) | copy-start | bytes 589828
  14.3 11.9 %collective-permute-start.2 = (bf16[2,96,512]{2,1,0:T(8,128)(2,1)S(1)}, bf16[2,96,512]{2,1,0:T(8,128)(2,1)S(1)}, u32[]{:S(2)}, u32[]{:S(2)}) collective-permute-start(bf16[2,96,512]{2,1,0:T(8,128)(2,1)S(1)} %pad_maximum_fusion.2.order_ref), channel_id=1, source_target_pairs={{0,8},{8,16},{16,24},{1,9},{9,17},{17,25},{2,10},{10,18},{18,26},{... | collective-permute-start | bytes 589832 | tf_op jit(solution)/shard_map/ppermute | solution.py:41
  18.1 10.5 %collective-permute-start.3 = (bf16[2,96,512]{2,1,0:T(8,128)(2,1)S(1)}, bf16[2,96,512]{2,1,0:T(8,128)(2,1)S(1)}, u32[]{:S(2)}, u32[]{:S(2)}) collective-permute-start(bf16[2,96,512]{2,1,0:T(8,128)(2,1)S(1)} %pad_maximum_fusion.2.order_ref), channel_id=1, source_target_pairs={{8,0},{16,8},{24,16},{9,1},{17,9},{25,17},{10,2},{18,10},{26,18},{... | collective-permute-start | bytes 589832 | tf_op jit(solution)/shard_map/ppermute | solution.py:44
  21.7 15.3 %all-to-all-start.1 = ((bf16[8,112,128]{2,1,0:T(8,128)(2,1)}), bf16[8,112,128]{2,1,0:T(8,128)(2,1)S(1)}, u32[]{:S(2)}, u32[]{:S(2)}) async-start(bf16[8,112,128]{2,1,0:T(8,128)(2,1)} %get-tuple-element.39), calls=%async_computation.1 | async-start | bytes 458752 | tf_op jit(solution)/shard_map/all_to_all | solution.py:55
  29.6 11.9 %copy-start.1 = (bf16[512,2048]{1,0:T(8,128)(2,1)S(1)}, bf16[512,2048]{1,0:T(8,128)(2,1)}, u32[]{:S(2)}) copy-start(bf16[512,2048]{1,0:T(8,128)(2,1)} %refs_9_.1) | copy-start | bytes 6291460
  37.0 21.1 %all-to-all-start = ((bf16[8,96,384]{2,1,0:T(8,128)(2,1)}), bf16[8,96,384]{2,1,0:T(8,128)(2,1)}, u32[]{:S(2)}, u32[]{:S(2)}) async-start(bf16[8,96,384]{2,1,0:T(8,128)(2,1)} %get-tuple-element.38), calls=%async_computation | async-start | bytes 1179648 | tf_op jit(solution)/shard_map/all_to_all | solution.py:55
  59.1 35.2 %copy-start.10 = (bf16[512,512]{1,0:T(8,128)(2,1)S(1)}, bf16[512,512]{1,0:T(8,128)(2,1)}, u32[]{:S(2)}) copy-start(bf16[512,512]{1,0:T(8,128)(2,1)} %out_weight_ref.3) | copy-start | bytes 1572868
  70.8 23.6 %copy-start.4 = (bf16[512,1536]{1,0:T(8,128)(2,1)S(1)}, bf16[512,1536]{1,0:T(8,128)(2,1)}, u32[]{:S(2)}) copy-start(bf16[512,1536]{1,0:T(8,128)(2,1)} %in_weight_ref.1) | copy-start | bytes 4718596
  70.8 23.5 %copy-start.19 = (f32[512]{0:T(512)S(1)}, f32[512]{0:T(512)}, u32[]{:S(2)}) copy-start(f32[512]{0:T(512)} %param.17) | copy-start | bytes 6148
  95.3 4.9 %collective-permute-start.4 = (bf16[2,1,512]{2,1,0:T(2,128)(2,1)S(1)}, bf16[2,1,512]{2,1,0:T(2,128)(2,1)S(1)}, u32[]{:S(2)}, u32[]{:S(2)}) collective-permute-start(bf16[2,1,512]{2,1,0:T(2,128)(2,1)S(1)} %get-tuple-element.70), channel_id=1, source_target_pairs={{0,1},{1,2},{2,3},{3,4},{4,5},{5,6},{6,7},{7,0},{8,9},{9,10},{10,1... | collective-permute-start | bytes 6152 | tf_op jit(solution)/shard_map/ppermute | solution.py:41
  95.4 4.9 %collective-permute-start.5 = (bf16[2,1,512]{2,1,0:T(2,128)(2,1)S(1)}, bf16[2,1,512]{2,1,0:T(2,128)(2,1)S(1)}, u32[]{:S(2)}, u32[]{:S(2)}) collective-permute-start(bf16[2,1,512]{2,1,0:T(2,128)(2,1)S(1)} %get-tuple-element.69), channel_id=1, source_target_pairs={{0,7},{1,0},{2,1},{3,2},{4,3},{5,4},{6,5},{7,6},{8,15},{9,8},{10,9... | collective-permute-start | bytes 6152 | tf_op jit(solution)/shard_map/ppermute | solution.py:44
  102.0 5.0 %collective-permute-start.8 = (bf16[4,2048,128]{2,1,0:T(8,128)(2,1)S(1)}, bf16[4,2048,128]{2,1,0:T(8,128)(2,1)S(1)}, u32[]{:S(2)}, u32[]{:S(2)}) collective-permute-start(bf16[4,2048,128]{2,1,0:T(8,128)(2,1)S(1)} %weight_grads.2), channel_id=1, source_target_pairs={{0,1},{1,0},{2,3},{3,2},{4,5},{5,4},{6,7},{7,6},{8,9},{9,8},{10,11... | collective-permute-start | bytes 6291464 | tf_op jit(solution)/shard_map/ppermute | solution.py:51
  102.1 8.3 %collective-permute-start.6 = (bf16[1,96,512]{2,1,0:T(8,128)(2,1)S(1)}, bf16[1,96,512]{2,1,0:T(8,128)(2,1)S(1)}, u32[]{:S(2)}, u32[]{:S(2)}) collective-permute-start(bf16[1,96,512]{2,1,0:T(8,128)(2,1)S(1)} %get-tuple-element.67), channel_id=1, source_target_pairs={{0,8},{8,16},{16,24},{1,9},{9,17},{17,25},{2,10},{10,18},{18,26},{... | collective-permute-start | bytes 294920 | tf_op jit(solution)/shard_map/ppermute | solution.py:41
  105.5 7.0 %collective-permute-start.7 = (bf16[1,96,512]{2,1,0:T(8,128)(2,1)S(1)}, bf16[1,96,512]{2,1,0:T(8,128)(2,1)S(1)}, u32[]{:S(2)}, u32[]{:S(2)}) collective-permute-start(bf16[1,96,512]{2,1,0:T(8,128)(2,1)S(1)} %get-tuple-element.68), channel_id=1, source_target_pairs={{8,0},{16,8},{24,16},{9,1},{17,9},{25,17},{10,2},{18,10},{26,18},{... | collective-permute-start | bytes 294920 | tf_op jit(solution)/shard_map/ppermute | solution.py:44
  113.2 29.6 %all-to-all-start.5 = ((bf16[4,2048,128]{2,1,0:T(8,128)(2,1)}), bf16[4,2048,128]{2,1,0:T(8,128)(2,1)S(1)}, u32[]{:S(2)}, u32[]{:S(2)}) async-start(bf16[4,2048,128]{2,1,0:T(8,128)(2,1)} %after.1.refs_4_.refs_5_), calls=%async_computation.5 | async-start | bytes 4194304 | tf_op jit(solution)/shard_map/all_to_all | solution.py:55
  126.1 8.9 %collective-permute-start.9 = (bf16[4,4,256,128]{3,2,1,0:T(8,128)(2,1)}, bf16[4,4,256,128]{3,2,1,0:T(8,128)(2,1)S(1)}, u32[]{:S(2)}, u32[]{:S(2)}) collective-permute-start(bf16[4,4,256,128]{3,2,1,0:T(8,128)(2,1)} %get-tuple-element.50), channel_id=1, source_target_pairs={{0,1},{1,0},{2,3},{3,2},{4,5},{5,4},{6,7},{7,6},{8,9},{9,8},{10,11... | collective-permute-start | bytes 3145736 | tf_op jit(solution)/shard_map/ppermute | solution.py:51
  126.2 8.8 %collective-permute-start.10 = (f32[4,9,256]{2,1,0:T(8,128)}, f32[4,9,256]{2,1,0:T(8,128)S(1)}, u32[]{:S(2)}, u32[]{:S(2)}) collective-permute-start(f32[4,9,256]{2,1,0:T(8,128)} %get-tuple-element.52), channel_id=1, source_target_pairs={{0,1},{1,0},{2,3},{3,2},{4,5},{5,4},{6,7},{7,6},{8,9},{9,8},{10,11... | collective-permute-start | bytes 110600 | tf_op jit(solution)/shard_map/ppermute | solution.py:51
  142.8 18.4 %all-to-all-start.3 = ((bf16[4,1104,128]{2,1,0:T(8,128)(2,1)}), bf16[4,1104,128]{2,1,0:T(8,128)(2,1)S(1)}, u32[]{:S(2)}, u32[]{:S(2)}) async-start(bf16[4,1104,128]{2,1,0:T(8,128)(2,1)} %pack.1), calls=%async_computation.3 | async-start | bytes 2260992 | tf_op jit(solution)/shard_map/all_to_all | solution.py:55
  146.3 30.9 %reduce-scatter.2.cloned.1.call-start = ((), (), s32[]{:S(2)}) async-start(), calls=%async_computation.7 | async-start | bytes 655360 | tf_op jit(solution)/shard_map/reduce_scatter | solution.py:943
  177.1 1.8 collective-permute-start.11
  (24 other events, 63.2 us)
Sparse Core Ops, SparseCore 0:
  149.4 23.9 reduce-scatter.1
